TPU v7x, 256 devices: a whole 4x4x8 slice. The times are simulated.
256 devices in a mesh: seq: 64 (over z, x, core), head: 4 (over y).
Axes of the slice: x: 4, y: 4, z: 8, core: 2. Of those that a mesh axis runs over, the one named last changes fastest.
Arguments:
- query: bfloat16 [8192, 4096], P('seq', 'head'), may hold values from -4.5 to 4.5
- keys: bfloat16 [8192, 4096], P('seq', 'head'), may hold values from -4.5 to 4.5
- values: bfloat16 [8192, 4096], P('seq', 'head'), may hold values from -60 to 60
- gain: float32 [4096], P('head'), may hold values from 0.5 to 1.5
- out_grad: bfloat16 [8192, 4096], P('seq', 'head'), may hold values from -8 to 8
Outputs:
- out: bfloat16 [8192, 4096], P('seq', 'head')
- query_grad: bfloat16 [8192, 4096], P('seq', 'head')
- key_grad: bfloat16 [8192, 4096], P('seq', 'head')
- value_grad: bfloat16 [8192, 4096], P('seq', 'head')
All inputs are finite; a program needn't handle non-finite values.
Results may differ from a plain program's by a relative error of at most 0.04.
Values may be sent and summed in bfloat16 or wider, within the bound.
No kernel may reach another device: no remote copies, remote signals or barrier semaphores. Data moves between devices by JAX's collectives and lax.ppermute only.
A program may use at most 64 MiB of HBM per device.

v0:
```python
from functools import reduce
import math

import jax
import jax.numpy as jnp
from jax import lax
from jax.sharding import PartitionSpec as P

HEADS = 32
DH = 128
BLOCK = 128
LEVELS = 4


eps = 1e-06
floor_score = -1e30


def swapped(shard, axis, distance):
    return lax.ppermute(shard, axis, [(i, i ^ 1 << distance) for i in range(lax.axis_size(axis))])


def from_behind(shard, axis, by):
    count = lax.axis_size(axis)
    pairs = [(i, i + by) for i in range(count) if 0 <= i + by < count]
    return lax.ppermute(shard, axis, pairs)


def padded_2(block, sides, width):
    for axis, dim in sides:
        count = lax.axis_size(axis)
        forward = [(i, i + 1) for i in range(count - 1)]
        backward = [(target, source) for source, target in forward]
        low = lax.ppermute(
            lax.slice_in_dim(block, block.shape[dim] - width, None, axis=dim), axis, forward
        )
        high = lax.ppermute(lax.slice_in_dim(block, 0, width, axis=dim), axis, backward)
        block = jnp.concatenate([low, block, high], axis=dim)
    return block


def pooled(x, level):
    return (
        x.astype(jnp.float32)
        .reshape(x.shape[0] >> level, 2**level, x.shape[1])
        .mean(axis=1)
        .astype(jnp.bfloat16)
    )


def pool_sum(x, level):
    return x.reshape((x.shape[0] >> level, 2**level) + x.shape[1:]).sum(axis=1)


def expand(x, level):
    if level == 0:
        return x
    return jnp.broadcast_to(x[:, None], (x.shape[0], 2**level) + x.shape[1:]).reshape(
        (x.shape[0] << level,) + x.shape[1:]
    )


def per_row(x):
    return x.transpose(0, 2, 1).reshape(x.shape[0] * x.shape[2], x.shape[1])


def attend(query_blocks, pair_blocks, valid):
    scores = jnp.einsum(
        "nqhd,nkhd->nhqk", query_blocks, pair_blocks[0], preferred_element_type=jnp.float32
    ) * (1.0 / math.sqrt(DH))
    if valid is not None:
        scores = jnp.where(valid[:, None, None, :], scores, floor_score)
    top = jnp.max(scores, axis=3)
    weights = jnp.exp(scores - top[..., None])
    if valid is not None:
        weights = jnp.where(valid[:, None, None, :], weights, 0.0)
    summed = jnp.einsum(
        "nhqk,nkhd->nqhd",
        weights.astype(jnp.bfloat16),
        pair_blocks[1],
        preferred_element_type=jnp.float32,
    )
    return (
        weights,
        per_row(top),
        per_row(jnp.sum(weights, axis=3)),
        summed.reshape(-1, summed.shape[2], summed.shape[3]),
    )


def attend_back(pair_blocks, weights, grad_blocks, offset_blocks):
    rounded_w = weights.astype(jnp.bfloat16)
    pressure = jnp.einsum(
        "nqhd,nkhd->nhqk", grad_blocks, pair_blocks[1], preferred_element_type=jnp.float32
    )
    slope = (weights * (pressure - offset_blocks[..., None])).astype(jnp.bfloat16)
    query_part = jnp.einsum(
        "nhqk,nkhd->nqhd", slope, pair_blocks[0], preferred_element_type=jnp.float32
    ) * (1.0 / math.sqrt(DH))
    return (rounded_w, slope, query_part)


def key_part(slope, rounded_w, query_blocks, grad_blocks):
    key_term = jnp.einsum(
        "nhqk,nqhd->nkhd", slope, query_blocks, preferred_element_type=jnp.float32
    ) * (1.0 / math.sqrt(DH))
    value_term = jnp.einsum(
        "nhqk,nqhd->nkhd", rounded_w, grad_blocks, preferred_element_type=jnp.float32
    )
    return jnp.stack([key_term, value_term])


def collect(pair, count, place):
    span = BLOCK // count
    bit = span.bit_length() - 1
    mine = swapped(pair, "seq", bit)
    position = place % span
    pieces = [mine]
    for step in range(1, span):
        below = from_behind(mine, "seq", step)
        above = from_behind(mine, "seq", step - span)
        pieces.append(jnp.where(position >= step, below, above))
    ordered = jnp.concatenate(pieces[::-1], axis=1)
    doubled = jnp.concatenate([ordered, ordered], axis=1)
    result = lax.dynamic_slice_in_dim(doubled, (span - 1 - position) * count, BLOCK, 1)
    return result


def dispatch(partial_value, count, place):
    span = BLOCK // count
    bit = span.bit_length() - 1
    position = place % span
    summed = lax.dynamic_slice_in_dim(partial_value, position * count, count, 1)
    for step in range(1, span):
        piece = lax.dynamic_slice_in_dim(partial_value, (position - step) % span * count, count, 1)
        from_above = from_behind(piece.astype(jnp.bfloat16), "seq", -step).astype(piece.dtype)
        from_below = from_behind(piece.astype(jnp.bfloat16), "seq", span - step).astype(piece.dtype)
        summed = summed + jnp.where(position + step < span, from_above, from_below)
    return swapped(summed.astype(jnp.bfloat16), "seq", bit).astype(summed.dtype)


def local(query, keys, values, gain, out_grad):
    rows, width = query.shape
    heads = width // DH
    place = lax.axis_index("seq")
    blocks_here = rows // BLOCK
    pair = jnp.stack([keys, values])
    padded = padded_2(pair, (("seq", 1),), BLOCK)
    near = jnp.concatenate(
        [
            padded[:, side * BLOCK : side * BLOCK + rows].reshape(2, blocks_here, BLOCK, heads, DH)
            for side in range(3)
        ],
        axis=2,
    )
    number = place * blocks_here + jnp.arange(blocks_here)
    final_block = blocks_here * lax.axis_size("seq") - 1
    edge_left = jnp.broadcast_to((number > 0)[:, None], (blocks_here, BLOCK))
    edge_right = jnp.broadcast_to((number < final_block)[:, None], (blocks_here, BLOCK))
    valid = jnp.concatenate(
        [edge_left, jnp.ones((blocks_here, BLOCK), jnp.bool_), edge_right], axis=1
    )
    saved = []
    for level in range(LEVELS):
        if level == 0:
            query_blocks = query.reshape(blocks_here, BLOCK, heads, DH)
            pairs = near
            mask = valid
        else:
            count = rows >> level
            pooled_query = pooled(query, level)
            pooled_pair = jnp.stack([pooled(keys, level), pooled(values, level)])
            query_blocks = pooled_query.reshape(1, count, heads, DH)
            pairs = collect(pooled_pair, count, place).reshape(2, 1, BLOCK, heads, DH)
            mask = None
        weights, top, total_level, summed = attend(query_blocks, pairs, mask)
        saved.append((query_blocks, pairs, weights, top, total_level, summed))
    tops = [expand(saved[level][3], level) for level in range(LEVELS)]
    best = reduce(jnp.maximum, tops)
    factors = [2.0**level * jnp.exp(tops[level] - best) for level in range(LEVELS)]
    total = reduce(
        jnp.add, [factors[level] * expand(saved[level][4], level) for level in range(LEVELS)]
    )
    numer = reduce(
        jnp.add,
        [factors[level][..., None] * expand(saved[level][5], level) for level in range(LEVELS)],
    )
    attn = (numer / total[..., None]).reshape(rows, width).astype(jnp.bfloat16)
    flat = attn.astype(jnp.float32)
    squares = lax.psum(jnp.sum(flat * flat, axis=1), "head")
    inv = lax.rsqrt(squares / (HEADS * DH) + eps)
    out = (flat * inv[:, None] * gain).astype(jnp.bfloat16)
    scaled = out_grad.astype(jnp.float32) * gain
    inner = lax.psum(jnp.sum(scaled * flat, axis=1), "head")
    attn_grad = (
        inv[:, None] * scaled - flat * (inv * inv * inv * inner / (HEADS * DH))[:, None]
    ).astype(jnp.bfloat16)
    grad_f = attn_grad.reshape(rows, heads, DH).astype(jnp.float32)
    dot = jnp.sum(grad_f * flat.reshape(rows, heads, DH), axis=2)
    query_grad = jnp.zeros((rows, heads, DH), jnp.float32)
    key_grad = jnp.zeros((rows, heads, DH), jnp.float32)
    value_grad = jnp.zeros((rows, heads, DH), jnp.float32)
    for level in range(LEVELS):
        query_blocks, pairs, weights = (saved[level][0], saved[level][1], saved[level][2])
        groups, depth = (query_blocks.shape[0], query_blocks.shape[1])
        share = factors[level] / total
        grad_rows = pool_sum(share[..., None] * grad_f, level).astype(jnp.bfloat16)
        offset = pool_sum(share * dot, level)
        grad_blocks = grad_rows.reshape(groups, depth, heads, DH)
        offset_blocks = offset.reshape(groups, depth, heads).transpose(0, 2, 1)
        rounded_w, slope, query_part = attend_back(pairs, weights, grad_blocks, offset_blocks)
        query_grad = query_grad + expand(query_part.reshape(-1, heads, DH), level) / 2.0**level
        if level == 0:
            centre = key_part(
                slope[..., BLOCK : 2 * BLOCK],
                rounded_w[..., BLOCK : 2 * BLOCK],
                query_blocks,
                grad_blocks,
            )
            left_part = key_part(
                slope[..., :BLOCK], rounded_w[..., :BLOCK], query_blocks, grad_blocks
            )
            right_part = key_part(
                slope[..., 2 * BLOCK :], rounded_w[..., 2 * BLOCK :], query_blocks, grad_blocks
            )
            inner_left = left_part[:, 1:]
            inner_right = right_part[:, :-1]
            from_right = from_behind(left_part[:, 0].astype(jnp.bfloat16), "seq", -1).astype(
                jnp.float32
            )
            from_left = from_behind(right_part[:, -1].astype(jnp.bfloat16), "seq", 1).astype(
                jnp.float32
            )
            zero = jnp.zeros((2, 1, BLOCK, heads, DH), jnp.float32)
            own = (
                centre
                + jnp.concatenate([inner_left, zero], axis=1)
                + jnp.concatenate([zero, inner_right], axis=1)
            )
            own = own.reshape(2, rows, heads, DH)
            own = own.at[:, :BLOCK].add(from_left).at[:, rows - BLOCK :].add(from_right)
        else:
            count = rows >> level
            part = key_part(slope, rounded_w, query_blocks, grad_blocks)
            own = dispatch(part.reshape(2, BLOCK, width), count, place).reshape(2, count, heads, DH)
        key_grad = key_grad + expand(own[0], level) / 2.0**level
        value_grad = value_grad + expand(own[1], level) / 2.0**level
    return (
        out,
        query_grad.reshape(rows, width).astype(jnp.bfloat16),
        key_grad.reshape(rows, width).astype(jnp.bfloat16),
        value_grad.reshape(rows, width).astype(jnp.bfloat16),
    )


def solution(mesh):
    in_specs = (P("seq", "head"), P("seq", "head"), P("seq", "head"), P("head"), P("seq", "head"))
    out_specs = (P("seq", "head"), P("seq", "head"), P("seq", "head"), P("seq", "head"))
    return jax.shard_map(local, mesh=mesh, in_specs=in_specs, out_specs=out_specs, check_vma=False)
```

profile of v0, /device:TPU:96, one launch (start us, length us, event | category | flops | bytes accessed | tf_op | source)
XLA Modules:
  0.0 609.9 jit_solution(5180234049975911151)
XLA Ops:
  3.8 3.6 collective-permute-start.1
  20.1 7.8 %collective-permute-done.12 = bf16[2,16,1024]{1,2,0:T(8,128)(2,1)} collective-permute-done((bf16[2,16,1024]{1,2,0:T(8,128)(2,1)S(1)}, bf16[2,16,1024]{1,2,0:T(8,128)(2,1)}, u32[]{:S(2)}, u32[]{:S(2)}) %collective-permute-start.12) | collective-permute-done | bytes 65568 | tf_op jit(solution)/shard_map/ppermute | solution.py:20
  32.9 13.3 %collective-permute-done.26 = bf16[2,16,1024]{1,2,0:T(8,128)(2,1)S(1)} collective-permute-done((bf16[2,16,1024]{1,2,0:T(8,128)(2,1)}, bf16[2,16,1024]{1,2,0:T(8,128)(2,1)S(1)}, u32[]{:S(2)}, u32[]{:S(2)}) %collective-permute-start.26) | collective-permute-done | bytes 65568 | tf_op jit(solution)/shard_map/ppermute | solution.py:26
  50.1 23.7 %collective-permute-done.24 = bf16[2,16,1024]{1,2,0:T(8,128)(2,1)S(1)} collective-permute-done((bf16[2,16,1024]{1,2,0:T(8,128)(2,1)}, bf16[2,16,1024]{1,2,0:T(8,128)(2,1)S(1)}, u32[]{:S(2)}, u32[]{:S(2)}) %collective-permute-start.24) | collective-permute-done | bytes 65568 | tf_op jit(solution)/shard_map/ppermute | solution.py:26
  75.8 10.1 %collective-permute-start.21 = (bf16[2,16,1024]{1,2,0:T(8,128)(2,1)}, bf16[2,16,1024]{1,2,0:T(8,128)(2,1)S(1)}, u32[]{:S(2)}, u32[]{:S(2)}) collective-permute-start(bf16[2,16,1024]{1,2,0:T(8,128)(2,1)} %collective-permute-done.12), channel_id=1, source_target_pairs={{0,12},{4,16},{8,20},{12,24},{16,28},{20,32},{24,36},{28,40},{32,4... | collective-permute-start | bytes 196616 | tf_op jit(solution)/shard_map/ppermute | solution.py:26
  86.0 17.9 %collective-permute-done.22 = bf16[2,16,1024]{1,2,0:T(8,128)(2,1)S(1)} collective-permute-done((bf16[2,16,1024]{1,2,0:T(8,128)(2,1)}, bf16[2,16,1024]{1,2,0:T(8,128)(2,1)S(1)}, u32[]{:S(2)}, u32[]{:S(2)}) %collective-permute-start.22) | collective-permute-done | bytes 65568 | tf_op jit(solution)/shard_map/ppermute | solution.py:26
  105.8 5.4 collective-permute-start.19
  111.3 17.8 %collective-permute-done.20 = bf16[2,16,1024]{1,2,0:T(8,128)(2,1)S(1)} collective-permute-done((bf16[2,16,1024]{1,2,0:T(8,128)(2,1)}, bf16[2,16,1024]{1,2,0:T(8,128)(2,1)S(1)}, u32[]{:S(2)}, u32[]{:S(2)}) %collective-permute-start.20) | collective-permute-done | bytes 65568 | tf_op jit(solution)/shard_map/ppermute | solution.py:26
  133.0 16.7 %collective-permute-done.18 = bf16[2,16,1024]{1,2,0:T(8,128)(2,1)S(1)} collective-permute-done((bf16[2,16,1024]{1,2,0:T(8,128)(2,1)}, bf16[2,16,1024]{1,2,0:T(8,128)(2,1)S(1)}, u32[]{:S(2)}, u32[]{:S(2)}) %collective-permute-start.18) | collective-permute-done | bytes 65568 | tf_op jit(solution)/shard_map/ppermute | solution.py:26
  151.6 3.4 collective-permute-start.15
  155.1 19.8 %collective-permute-done.16 = bf16[2,16,1024]{1,2,0:T(8,128)(2,1)S(1)} collective-permute-done((bf16[2,16,1024]{1,2,0:T(8,128)(2,1)}, bf16[2,16,1024]{1,2,0:T(8,128)(2,1)S(1)}, u32[]{:S(2)}, u32[]{:S(2)}) %collective-permute-start.16) | collective-permute-done | bytes 65568 | tf_op jit(solution)/shard_map/ppermute | solution.py:26
  176.8 4.2 collective-permute-start.13
  181.1 2.8 collective-permute-done.14
  183.8 5.6 collective-permute-start.5
  192.1 10.1 %concatenate.33 = bf16[2,256,1024]{1,2,0:T(8,128)(2,1)} concatenate(bf16[2,16,1024]{1,2,0:T(8,128)(2,1)} %broadcast_select_fusion.6, bf16[2,16,1024]{1,2,0:T(8,128)(2,1)S(1)} %broadcast_select_fusion.5, bf16[2,16,1024]{1,2,0:T(8,128)(2,1)S(1)} %broadcast_select_fusion.4, bf16[2,16,1024]{1,2,0:T(8,128)(2,1)S(1)} %broadcast_select_fusion.3, ...), dimensions={1} | concatenate | bytes 2097152 | tf_op jit(solution)/shard_map/concatenate | solution.py:124
  212.7 6.0 collective-permute-start.11
  221.5 11.0 %collective-permute-done.11 = bf16[2,32,1024]{1,2,0:T(8,128)(2,1)S(1)} collective-permute-done((bf16[2,32,1024]{1,2,0:T(8,128)(2,1)}, bf16[2,32,1024]{1,2,0:T(8,128)(2,1)S(1)}, u32[]{:S(2)}, u32[]{:S(2)}) %collective-permute-start.11) | collective-permute-done | bytes 131104 | tf_op jit(solution)/shard_map/ppermute | solution.py:26
  232.5 3.1 collective-permute-start.9
  236.9 5.7 collective-permute-start.8
  242.7 5.1 collective-permute-done.9
  247.8 6.3 %collective-permute-start.7 = (bf16[2,32,1024]{1,2,0:T(8,128)(2,1)}, bf16[2,32,1024]{1,2,0:T(8,128)(2,1)S(1)}, u32[]{:S(2)}, u32[]{:S(2)}) collective-permute-start(bf16[2,32,1024]{1,2,0:T(8,128)(2,1)} %collective-permute-done.5), channel_id=1, source_target_pairs={{4,0},{8,4},{12,8},{16,12},{20,16},{24,20},{28,24},{32,28},{36,32}... | collective-permute-start | bytes 393224 | tf_op jit(solution)/shard_map/ppermute | solution.py:26
  255.1 3.8 collective-permute-start.6
  259.0 3.6 collective-permute-done.7
  262.5 10.0 %collective-permute-done.6 = bf16[2,32,1024]{1,2,0:T(8,128)(2,1)S(1)} collective-permute-done((bf16[2,32,1024]{1,2,0:T(8,128)(2,1)}, bf16[2,32,1024]{1,2,0:T(8,128)(2,1)S(1)}, u32[]{:S(2)}, u32[]{:S(2)}) %collective-permute-start.6) | collective-permute-done | bytes 131104 | tf_op jit(solution)/shard_map/ppermute | solution.py:26
  272.6 6.1 concatenate.32
  286.6 3.9 collective-permute-start.4
  321.0 3.8 fusion.62
  337.1 2.9 fusion.66
  340.1 11.0 %all-reduce = (f32[128]{0:T(128)S(1)}, f32[128]{0:T(128)S(1)}) all-reduce(f32[128]{0:T(128)} %get-tuple-element.76, f32[128]{0:T(128)} %get-tuple-element.74), channel_id=1, replica_groups=mesh['seq'=64,'head'=4] {'head'}, use_global_device_ids=true, to_apply=%region_18.19 | all-reduce | flops 256 | bytes 2048 | tf_op jit(solution)/shard_map/psum | solution.py:190
  376.6 5.0 collective-permute-start.51
  384.2 5.0 collective-permute-start.40
  394.5 3.6 collective-permute-start.42
  402.9 3.7 collective-permute-start.44
  406.6 8.0 %collective-permute-start.43 = (bf16[2,16,1024]{1,2,0:T(8,128)(2,1)S(1)}, bf16[2,16,1024]{1,2,0:T(8,128)(2,1)S(1)}, u32[]{:S(2)}, u32[]{:S(2)}) collective-permute-start(bf16[2,16,1024]{1,2,0:T(8,128)(2,1)S(1)} %copy-done.41), channel_id=1, source_target_pairs={{12,0},{16,4},{20,8},{24,12},{28,16},{32,20},{36,24},{40,28},{44,3... | collective-permute-start | bytes 196616 | tf_op jit(solution)/shard_map/ppermute | solution.py:26
  414.7 14.4 %collective-permute-start.46 = (bf16[2,16,1024]{1,2,0:T(8,128)(2,1)S(1)}, bf16[2,16,1024]{1,2,0:T(8,128)(2,1)S(1)}, u32[]{:S(2)}, u32[]{:S(2)}) collective-permute-start(bf16[2,16,1024]{1,2,0:T(8,128)(2,1)S(1)} %copy-done.40), channel_id=1, source_target_pairs={{0,16},{4,20},{8,24},{12,28},{16,32},{20,36},{24,40},{28,44},{32,4... | collective-permute-start | bytes 196616 | tf_op jit(solution)/shard_map/ppermute | solution.py:26
  430.0 6.9 %collective-permute-done.42 = bf16[2,16,1024]{1,2,0:T(8,128)(2,1)S(1)} collective-permute-done((bf16[2,16,1024]{1,2,0:T(8,128)(2,1)}, bf16[2,16,1024]{1,2,0:T(8,128)(2,1)S(1)}, u32[]{:S(2)}, u32[]{:S(2)}) %collective-permute-start.42) | collective-permute-done | bytes 65568 | tf_op jit(solution)/shard_map/ppermute | solution.py:26
  441.4 10.2 %collective-permute-start.47 = (bf16[2,16,1024]{1,2,0:T(8,128)(2,1)S(1)}, bf16[2,16,1024]{1,2,0:T(8,128)(2,1)S(1)}, u32[]{:S(2)}, u32[]{:S(2)}) collective-permute-start(bf16[2,16,1024]{1,2,0:T(8,128)(2,1)S(1)} %copy-done.39), channel_id=1, source_target_pairs={{20,0},{24,4},{28,8},{32,12},{36,16},{40,20},{44,24},{48,28},{52,3... | collective-permute-start | bytes 196616 | tf_op jit(solution)/shard_map/ppermute | solution.py:26
  451.6 13.4 %collective-permute-start.50 = (bf16[2,16,1024]{1,2,0:T(8,128)(2,1)S(1)}, bf16[2,16,1024]{1,2,0:T(8,128)(2,1)S(1)}, u32[]{:S(2)}, u32[]{:S(2)}) collective-permute-start(bf16[2,16,1024]{1,2,0:T(8,128)(2,1)S(1)} %copy-done.38), channel_id=1, source_target_pairs={{0,8},{4,12},{8,16},{12,20},{16,24},{20,28},{24,32},{28,36},{32,40... | collective-permute-start | bytes 196616 | tf_op jit(solution)/shard_map/ppermute | solution.py:26
  465.0 15.3 %collective-permute-start.49 = (bf16[2,16,1024]{1,2,0:T(8,128)(2,1)S(1)}, bf16[2,16,1024]{1,2,0:T(8,128)(2,1)S(1)}, u32[]{:S(2)}, u32[]{:S(2)}) collective-permute-start(bf16[2,16,1024]{1,2,0:T(8,128)(2,1)S(1)} %copy-done.38), channel_id=1, source_target_pairs={{24,0},{28,4},{32,8},{36,12},{40,16},{44,20},{48,24},{52,28},{56,3... | collective-permute-start | bytes 196616 | tf_op jit(solution)/shard_map/ppermute | solution.py:26
  483.2 8.1 %collective-permute-start.32 = (bf16[2,32,1024]{1,2,0:T(8,128)(2,1)}, bf16[2,32,1024]{1,2,0:T(8,128)(2,1)}, u32[]{:S(2)}, u32[]{:S(2)}) collective-permute-start(bf16[2,32,1024]{1,2,0:T(8,128)(2,1)} %get-tuple-element.88), channel_id=1, source_target_pairs={{4,0},{8,4},{12,8},{16,12},{20,16},{24,20},{28,24},{32,28},{36,32}... | collective-permute-start | bytes 393224 | tf_op jit(solution)/shard_map/ppermute | solution.py:26
  491.2 10.5 %collective-permute-done.47 = bf16[2,16,1024]{1,2,0:T(8,128)(2,1)S(1)} collective-permute-done((bf16[2,16,1024]{1,2,0:T(8,128)(2,1)S(1)}, bf16[2,16,1024]{1,2,0:T(8,128)(2,1)S(1)}, u32[]{:S(2)}, u32[]{:S(2)}) %collective-permute-start.47) | collective-permute-done | bytes 65568 | tf_op jit(solution)/shard_map/ppermute | solution.py:26
  503.6 6.0 collective-permute-start.34
  509.7 20.6 %collective-permute-done.49 = bf16[2,16,1024]{1,2,0:T(8,128)(2,1)S(1)} collective-permute-done((bf16[2,16,1024]{1,2,0:T(8,128)(2,1)S(1)}, bf16[2,16,1024]{1,2,0:T(8,128)(2,1)S(1)}, u32[]{:S(2)}, u32[]{:S(2)}) %collective-permute-start.49) | collective-permute-done | bytes 65568 | tf_op jit(solution)/shard_map/ppermute | solution.py:26
  534.2 8.2 %collective-permute-done.53 = bf16[2,16,1024]{1,2,0:T(8,128)(2,1)S(1)} collective-permute-done((bf16[2,16,1024]{1,2,0:T(8,128)(2,1)S(1)}, bf16[2,16,1024]{1,2,0:T(8,128)(2,1)S(1)}, u32[]{:S(2)}, u32[]{:S(2)}) %collective-permute-start.53) | collective-permute-done | bytes 65568 | tf_op jit(solution)/shard_map/ppermute | solution.py:20
  550.6 5.8 collective-permute-start.29
  559.9 4.2 collective-permute-start.28
  568.3 16.1 %collective-permute-done.38 = bf16[2,32,1024]{1,2,0:T(8,128)(2,1)S(1)} collective-permute-done((bf16[2,32,1024]{1,2,0:T(8,128)(2,1)S(1)}, bf16[2,32,1024]{1,2,0:T(8,128)(2,1)S(1)}, u32[]{:S(2)}, u32[]{:S(2)}) %collective-permute-start.38) | collective-permute-done | bytes 131104 | tf_op jit(solution)/shard_map/ppermute | solution.py:20
  585.6 13.6 %collective-permute-done.31 = bf16[2,64,1024]{1,2,0:T(8,128)(2,1)S(1)} collective-permute-done((bf16[2,64,1024]{1,2,0:T(8,128)(2,1)}, bf16[2,64,1024]{1,2,0:T(8,128)(2,1)S(1)}, u32[]{:S(2)}, u32[]{:S(2)}) %collective-permute-start.31) | collective-permute-done | bytes 262176 | tf_op jit(solution)/shard_map/ppermute | solution.py:20
  (457 shorter events, 183.5 us)
Async XLA Ops:
  3.8 288.6 %collective-permute-start.1 = (bf16[2,128,1024]{1,2,0:T(8,128)(2,1)}, bf16[2,128,1024]{1,2,0:T(8,128)(2,1)}, u32[]{:S(2)}, u32[]{:S(2)}) collective-permute-start(bf16[2,128,1024]{1,2,0:T(8,128)(2,1)} %pad_maximum_fusion.1), channel_id=1, source_target_pairs={{4,0},{8,4},{12,8},{16,12},{20,16},{24,20},{28,24},{32,28},{36,32}... | collective-permute-start | bytes 1572872 | tf_op jit(solution)/shard_map/ppermute | solution.py:37
  7.5 286.3 %collective-permute-start = (bf16[2,128,1024]{1,2,0:T(8,128)(2,1)}, bf16[2,128,1024]{1,2,0:T(8,128)(2,1)}, u32[]{:S(2)}, u32[]{:S(2)}) collective-permute-start(bf16[2,128,1024]{1,2,0:T(8,128)(2,1)} %pad_maximum_fusion.1), channel_id=1, source_target_pairs={{0,4},{4,8},{8,12},{12,16},{16,20},{20,24},{24,28},{28,32},{32,36}... | collective-permute-start | bytes 1572872 | tf_op jit(solution)/shard_map/ppermute | solution.py:34
  12.1 274.5 %collective-permute-start.2 = (bf16[2,64,1024]{2,1,0:T(8,128)(2,1)}, bf16[2,64,1024]{2,1,0:T(8,128)(2,1)}, u32[]{:S(2)}, u32[]{:S(2)}) collective-permute-start(bf16[2,64,1024]{2,1,0:T(8,128)(2,1)} %pad_maximum_fusion.2), channel_id=1, source_target_pairs={{0,8},{4,12},{8,0},{12,4},{16,24},{20,28},{24,16},{28,20},{32,40},... | collective-permute-start | bytes 786440 | tf_op jit(solution)/shard_map/ppermute | solution.py:20
  27.9 18.3 %collective-permute-start.26 = (bf16[2,16,1024]{1,2,0:T(8,128)(2,1)}, bf16[2,16,1024]{1,2,0:T(8,128)(2,1)S(1)}, u32[]{:S(2)}, u32[]{:S(2)}) collective-permute-start(bf16[2,16,1024]{1,2,0:T(8,128)(2,1)} %collective-permute-done.12), channel_id=1, source_target_pairs={{28,0},{32,4},{36,8},{40,12},{44,16},{48,20},{52,24},{56,28},{60,3... | collective-permute-start | bytes 196616 | tf_op jit(solution)/shard_map/ppermute | solution.py:26
  29.8 18.3 %collective-permute-start.25 = (bf16[2,16,1024]{1,2,0:T(8,128)(2,1)}, bf16[2,16,1024]{1,2,0:T(8,128)(2,1)S(1)}, u32[]{:S(2)}, u32[]{:S(2)}) collective-permute-start(bf16[2,16,1024]{1,2,0:T(8,128)(2,1)} %collective-permute-done.12), channel_id=1, source_target_pairs={{0,4},{4,8},{8,12},{12,16},{16,20},{20,24},{24,28},{28,32},{32,36}... | collective-permute-start | bytes 196616 | tf_op jit(solution)/shard_map/ppermute | solution.py:26
  46.2 27.7 %collective-permute-start.24 = (bf16[2,16,1024]{1,2,0:T(8,128)(2,1)}, bf16[2,16,1024]{1,2,0:T(8,128)(2,1)S(1)}, u32[]{:S(2)}, u32[]{:S(2)}) collective-permute-start(bf16[2,16,1024]{1,2,0:T(8,128)(2,1)} %collective-permute-done.12), channel_id=1, source_target_pairs={{24,0},{28,4},{32,8},{36,12},{40,16},{44,20},{48,24},{52,28},{56,3... | collective-permute-start | bytes 196616 | tf_op jit(solution)/shard_map/ppermute | solution.py:26
  48.1 27.7 %collective-permute-start.23 = (bf16[2,16,1024]{1,2,0:T(8,128)(2,1)}, bf16[2,16,1024]{1,2,0:T(8,128)(2,1)S(1)}, u32[]{:S(2)}, u32[]{:S(2)}) collective-permute-start(bf16[2,16,1024]{1,2,0:T(8,128)(2,1)} %collective-permute-done.12), channel_id=1, source_target_pairs={{0,8},{4,12},{8,16},{12,20},{16,24},{20,28},{24,32},{28,36},{32,40... | collective-permute-start | bytes 196616 | tf_op jit(solution)/shard_map/ppermute | solution.py:26
  73.9 30.0 %collective-permute-start.22 = (bf16[2,16,1024]{1,2,0:T(8,128)(2,1)}, bf16[2,16,1024]{1,2,0:T(8,128)(2,1)S(1)}, u32[]{:S(2)}, u32[]{:S(2)}) collective-permute-start(bf16[2,16,1024]{1,2,0:T(8,128)(2,1)} %collective-permute-done.12), channel_id=1, source_target_pairs={{20,0},{24,4},{28,8},{32,12},{36,16},{40,20},{44,24},{48,28},{52,3... | collective-permute-start | bytes 196616 | tf_op jit(solution)/shard_map/ppermute | solution.py:26
  75.8 30.0 %collective-permute-start.21 = (bf16[2,16,1024]{1,2,0:T(8,128)(2,1)}, bf16[2,16,1024]{1,2,0:T(8,128)(2,1)S(1)}, u32[]{:S(2)}, u32[]{:S(2)}) collective-permute-start(bf16[2,16,1024]{1,2,0:T(8,128)(2,1)} %collective-permute-done.12), channel_id=1, source_target_pairs={{0,12},{4,16},{8,20},{12,24},{16,28},{20,32},{24,36},{28,40},{32,4... | collective-permute-start | bytes 196616 | tf_op jit(solution)/shard_map/ppermute | solution.py:26
  103.9 25.2 %collective-permute-start.20 = (bf16[2,16,1024]{1,2,0:T(8,128)(2,1)}, bf16[2,16,1024]{1,2,0:T(8,128)(2,1)S(1)}, u32[]{:S(2)}, u32[]{:S(2)}) collective-permute-start(bf16[2,16,1024]{1,2,0:T(8,128)(2,1)} %collective-permute-done.12), channel_id=1, source_target_pairs={{16,0},{20,4},{24,8},{28,12},{32,16},{36,20},{40,24},{44,28},{48,3... | collective-permute-start | bytes 196616 | tf_op jit(solution)/shard_map/ppermute | solution.py:26
  105.8 25.2 %collective-permute-start.19 = (bf16[2,16,1024]{1,2,0:T(8,128)(2,1)}, bf16[2,16,1024]{1,2,0:T(8,128)(2,1)S(1)}, u32[]{:S(2)}, u32[]{:S(2)}) collective-permute-start(bf16[2,16,1024]{1,2,0:T(8,128)(2,1)} %collective-permute-done.12), channel_id=1, source_target_pairs={{0,16},{4,20},{8,24},{12,28},{16,32},{20,36},{24,40},{28,44},{32,4... | collective-permute-start | bytes 196616 | tf_op jit(solution)/shard_map/ppermute | solution.py:26
  129.1 20.6 %collective-permute-start.18 = (bf16[2,16,1024]{1,2,0:T(8,128)(2,1)}, bf16[2,16,1024]{1,2,0:T(8,128)(2,1)S(1)}, u32[]{:S(2)}, u32[]{:S(2)}) collective-permute-start(bf16[2,16,1024]{1,2,0:T(8,128)(2,1)} %collective-permute-done.12), channel_id=1, source_target_pairs={{12,0},{16,4},{20,8},{24,12},{28,16},{32,20},{36,24},{40,28},{44,3... | collective-permute-start | bytes 196616 | tf_op jit(solution)/shard_map/ppermute | solution.py:26
  131.0 20.6 %collective-permute-start.17 = (bf16[2,16,1024]{1,2,0:T(8,128)(2,1)}, bf16[2,16,1024]{1,2,0:T(8,128)(2,1)S(1)}, u32[]{:S(2)}, u32[]{:S(2)}) collective-permute-start(bf16[2,16,1024]{1,2,0:T(8,128)(2,1)} %collective-permute-done.12), channel_id=1, source_target_pairs={{0,20},{4,24},{8,28},{12,32},{16,36},{20,40},{24,44},{28,48},{32,5... | collective-permute-start | bytes 196616 | tf_op jit(solution)/shard_map/ppermute | solution.py:26
  149.7 25.2 %collective-permute-start.16 = (bf16[2,16,1024]{1,2,0:T(8,128)(2,1)}, bf16[2,16,1024]{1,2,0:T(8,128)(2,1)S(1)}, u32[]{:S(2)}, u32[]{:S(2)}) collective-permute-start(bf16[2,16,1024]{1,2,0:T(8,128)(2,1)} %collective-permute-done.12), channel_id=1, source_target_pairs={{8,0},{12,4},{16,8},{20,12},{24,16},{28,20},{32,24},{36,28},{40,32... | collective-permute-start | bytes 196616 | tf_op jit(solution)/shard_map/ppermute | solution.py:26
  151.6 25.2 %collective-permute-start.15 = (bf16[2,16,1024]{1,2,0:T(8,128)(2,1)}, bf16[2,16,1024]{1,2,0:T(8,128)(2,1)S(1)}, u32[]{:S(2)}, u32[]{:S(2)}) collective-permute-start(bf16[2,16,1024]{1,2,0:T(8,128)(2,1)} %collective-permute-done.12), channel_id=1, source_target_pairs={{0,24},{4,28},{8,32},{12,36},{16,40},{20,44},{24,48},{28,52},{32,5... | collective-permute-start | bytes 196616 | tf_op jit(solution)/shard_map/ppermute | solution.py:26
  183.8 28.9 %collective-permute-start.5 = (bf16[2,32,1024]{1,2,0:T(8,128)(2,1)}, bf16[2,32,1024]{1,2,0:T(8,128)(2,1)}, u32[]{:S(2)}, u32[]{:S(2)}) collective-permute-start(bf16[2,32,1024]{1,2,0:T(8,128)(2,1)} %copy.403), channel_id=1, source_target_pairs={{0,16},{4,20},{8,24},{12,28},{16,0},{20,4},{24,8},{28,12},{32,48},... | collective-permute-start | bytes 393224 | tf_op jit(solution)/shard_map/ppermute | solution.py:20
  212.7 19.8 %collective-permute-start.11 = (bf16[2,32,1024]{1,2,0:T(8,128)(2,1)}, bf16[2,32,1024]{1,2,0:T(8,128)(2,1)S(1)}, u32[]{:S(2)}, u32[]{:S(2)}) collective-permute-start(bf16[2,32,1024]{1,2,0:T(8,128)(2,1)} %collective-permute-done.5), channel_id=1, source_target_pairs={{12,0},{16,4},{20,8},{24,12},{28,16},{32,20},{36,24},{40,28},{44,3... | collective-permute-start | bytes 393224 | tf_op jit(solution)/shard_map/ppermute | solution.py:26
  218.7 18.1 %collective-permute-start.10 = (bf16[2,32,1024]{1,2,0:T(8,128)(2,1)}, bf16[2,32,1024]{1,2,0:T(8,128)(2,1)S(1)}, u32[]{:S(2)}, u32[]{:S(2)}) collective-permute-start(bf16[2,32,1024]{1,2,0:T(8,128)(2,1)} %collective-permute-done.5), channel_id=1, source_target_pairs={{0,4},{4,8},{8,12},{12,16},{16,20},{20,24},{24,28},{28,32},{32,36}... | collective-permute-start | bytes 393224 | tf_op jit(solution)/shard_map/ppermute | solution.py:26
  232.5 15.2 %collective-permute-start.9 = (bf16[2,32,1024]{1,2,0:T(8,128)(2,1)}, bf16[2,32,1024]{1,2,0:T(8,128)(2,1)S(1)}, u32[]{:S(2)}, u32[]{:S(2)}) collective-permute-start(bf16[2,32,1024]{1,2,0:T(8,128)(2,1)} %collective-permute-done.5), channel_id=1, source_target_pairs={{8,0},{12,4},{16,8},{20,12},{24,16},{28,20},{32,24},{36,28},{40,32... | collective-permute-start | bytes 393224 | tf_op jit(solution)/shard_map/ppermute | solution.py:26
  236.9 18.2 %collective-permute-start.8 = (bf16[2,32,1024]{1,2,0:T(8,128)(2,1)}, bf16[2,32,1024]{1,2,0:T(8,128)(2,1)S(1)}, u32[]{:S(2)}, u32[]{:S(2)}) collective-permute-start(bf16[2,32,1024]{1,2,0:T(8,128)(2,1)} %collective-permute-done.5), channel_id=1, source_target_pairs={{0,8},{4,12},{8,16},{12,20},{16,24},{20,28},{24,32},{28,36},{32,40... | collective-permute-start | bytes 393224 | tf_op jit(solution)/shard_map/ppermute | solution.py:26
  255.1 17.5 %collective-permute-start.6 = (bf16[2,32,1024]{1,2,0:T(8,128)(2,1)}, bf16[2,32,1024]{1,2,0:T(8,128)(2,1)S(1)}, u32[]{:S(2)}, u32[]{:S(2)}) collective-permute-start(bf16[2,32,1024]{1,2,0:T(8,128)(2,1)} %collective-permute-done.5), channel_id=1, source_target_pairs={{0,12},{4,16},{8,20},{12,24},{16,28},{20,32},{24,36},{28,40},{32,4... | collective-permute-start | bytes 393224 | tf_op jit(solution)/shard_map/ppermute | solution.py:26
  286.6 16.8 %collective-permute-start.4 = (bf16[2,64,1024]{2,1,0:T(8,128)(2,1)}, bf16[2,64,1024]{2,1,0:T(8,128)(2,1)}, u32[]{:S(2)}, u32[]{:S(2)}) collective-permute-start(bf16[2,64,1024]{2,1,0:T(8,128)(2,1)} %collective-permute-done.2), channel_id=1, source_target_pairs={{4,0},{8,4},{12,8},{16,12},{20,16},{24,20},{28,24},{32,28},{36,32}... | collective-permute-start | bytes 786440 | tf_op jit(solution)/shard_map/ppermute | solution.py:26
  374.6 26.3 %collective-permute-start.52 = (bf16[2,16,1024]{1,2,0:T(8,128)(2,1)}, bf16[2,16,1024]{1,2,0:T(8,128)(2,1)}, u32[]{:S(2)}, u32[]{:S(2)}) collective-permute-start(bf16[2,16,1024]{1,2,0:T(8,128)(2,1)} %fusion.35), channel_id=1, source_target_pairs={{0,4},{4,8},{8,12},{12,16},{16,20},{20,24},{24,28},{28,32},{32,36}... | collective-permute-start | bytes 196616 | tf_op jit(solution)/shard_map/ppermute | solution.py:26
  376.6 26.3 %collective-permute-start.51 = (bf16[2,16,1024]{1,2,0:T(8,128)(2,1)}, bf16[2,16,1024]{1,2,0:T(8,128)(2,1)}, u32[]{:S(2)}, u32[]{:S(2)}) collective-permute-start(bf16[2,16,1024]{1,2,0:T(8,128)(2,1)} %fusion.35), channel_id=1, source_target_pairs={{28,0},{32,4},{36,8},{40,12},{44,16},{48,20},{52,24},{56,28},{60,3... | collective-permute-start | bytes 196616 | tf_op jit(solution)/shard_map/ppermute | solution.py:26
  384.2 22.4 %collective-permute-start.40 = (bf16[2,16,1024]{1,2,0:T(8,128)(2,1)}, bf16[2,16,1024]{1,2,0:T(8,128)(2,1)}, u32[]{:S(2)}, u32[]{:S(2)}) collective-permute-start(bf16[2,16,1024]{1,2,0:T(8,128)(2,1)} %get-tuple-element.91), channel_id=1, source_target_pairs={{0,28},{4,32},{8,36},{12,40},{16,44},{20,48},{24,52},{28,56},{32,6... | collective-permute-start | bytes 196616 | tf_op jit(solution)/shard_map/ppermute | solution.py:26
  389.3 25.4 %collective-permute-start.39 = (bf16[2,16,1024]{1,2,0:T(8,128)(2,1)}, bf16[2,16,1024]{1,2,0:T(8,128)(2,1)}, u32[]{:S(2)}, u32[]{:S(2)}) collective-permute-start(bf16[2,16,1024]{1,2,0:T(8,128)(2,1)} %get-tuple-element.91), channel_id=1, source_target_pairs={{4,0},{8,4},{12,8},{16,12},{20,16},{24,20},{28,24},{32,28},{36,32}... | collective-permute-start | bytes 196616 | tf_op jit(solution)/shard_map/ppermute | solution.py:26
  394.5 42.4 %collective-permute-start.42 = (bf16[2,16,1024]{1,2,0:T(8,128)(2,1)}, bf16[2,16,1024]{1,2,0:T(8,128)(2,1)S(1)}, u32[]{:S(2)}, u32[]{:S(2)}) collective-permute-start(bf16[2,16,1024]{1,2,0:T(8,128)(2,1)} %get-tuple-element.92), channel_id=1, source_target_pairs={{0,24},{4,28},{8,32},{12,36},{16,40},{20,44},{24,48},{28,52},{32,5... | collective-permute-start | bytes 196616 | tf_op jit(solution)/shard_map/ppermute | solution.py:26
  400.8 38.3 %collective-permute-start.41 = (bf16[2,16,1024]{1,2,0:T(8,128)(2,1)S(1)}, bf16[2,16,1024]{1,2,0:T(8,128)(2,1)S(1)}, u32[]{:S(2)}, u32[]{:S(2)}) collective-permute-start(bf16[2,16,1024]{1,2,0:T(8,128)(2,1)S(1)} %copy-done.42), channel_id=1, source_target_pairs={{8,0},{12,4},{16,8},{20,12},{24,16},{28,20},{32,24},{36,28},{40,32... | collective-permute-start | bytes 196616 | tf_op jit(solution)/shard_map/ppermute | solution.py:26
  402.9 38.4 %collective-permute-start.44 = (bf16[2,16,1024]{1,2,0:T(8,128)(2,1)S(1)}, bf16[2,16,1024]{1,2,0:T(8,128)(2,1)S(1)}, u32[]{:S(2)}, u32[]{:S(2)}) collective-permute-start(bf16[2,16,1024]{1,2,0:T(8,128)(2,1)S(1)} %copy-done.41), channel_id=1, source_target_pairs={{0,20},{4,24},{8,28},{12,32},{16,36},{20,40},{24,44},{28,48},{32,5... | collective-permute-start | bytes 196616 | tf_op jit(solution)/shard_map/ppermute | solution.py:26
  406.6 44.9 %collective-permute-start.43 = (bf16[2,16,1024]{1,2,0:T(8,128)(2,1)S(1)}, bf16[2,16,1024]{1,2,0:T(8,128)(2,1)S(1)}, u32[]{:S(2)}, u32[]{:S(2)}) collective-permute-start(bf16[2,16,1024]{1,2,0:T(8,128)(2,1)S(1)} %copy-done.41), channel_id=1, source_target_pairs={{12,0},{16,4},{20,8},{24,12},{28,16},{32,20},{36,24},{40,28},{44,3... | collective-permute-start | bytes 196616 | tf_op jit(solution)/shard_map/ppermute | solution.py:26
  414.7 50.3 %collective-permute-start.46 = (bf16[2,16,1024]{1,2,0:T(8,128)(2,1)S(1)}, bf16[2,16,1024]{1,2,0:T(8,128)(2,1)S(1)}, u32[]{:S(2)}, u32[]{:S(2)}) collective-permute-start(bf16[2,16,1024]{1,2,0:T(8,128)(2,1)S(1)} %copy-done.40), channel_id=1, source_target_pairs={{0,16},{4,20},{8,24},{12,28},{16,32},{20,36},{24,40},{28,44},{32,4... | collective-permute-start | bytes 196616 | tf_op jit(solution)/shard_map/ppermute | solution.py:26
  436.9 44.4 %collective-permute-start.45 = (bf16[2,16,1024]{1,2,0:T(8,128)(2,1)S(1)}, bf16[2,16,1024]{1,2,0:T(8,128)(2,1)S(1)}, u32[]{:S(2)}, u32[]{:S(2)}) collective-permute-start(bf16[2,16,1024]{1,2,0:T(8,128)(2,1)S(1)} %copy-done.40), channel_id=1, source_target_pairs={{16,0},{20,4},{24,8},{28,12},{32,16},{36,20},{40,24},{44,28},{48,3... | collective-permute-start | bytes 196616 | tf_op jit(solution)/shard_map/ppermute | solution.py:26
  439.1 44.1 %collective-permute-start.48 = (bf16[2,16,1024]{1,2,0:T(8,128)(2,1)S(1)}, bf16[2,16,1024]{1,2,0:T(8,128)(2,1)S(1)}, u32[]{:S(2)}, u32[]{:S(2)}) collective-permute-start(bf16[2,16,1024]{1,2,0:T(8,128)(2,1)S(1)} %copy-done.39), channel_id=1, source_target_pairs={{0,12},{4,16},{8,20},{12,24},{16,28},{20,32},{24,36},{28,40},{32,4... | collective-permute-start | bytes 196616 | tf_op jit(solution)/shard_map/ppermute | solution.py:26
  441.4 60.3 %collective-permute-start.47 = (bf16[2,16,1024]{1,2,0:T(8,128)(2,1)S(1)}, bf16[2,16,1024]{1,2,0:T(8,128)(2,1)S(1)}, u32[]{:S(2)}, u32[]{:S(2)}) collective-permute-start(bf16[2,16,1024]{1,2,0:T(8,128)(2,1)S(1)} %copy-done.39), channel_id=1, source_target_pairs={{20,0},{24,4},{28,8},{32,12},{36,16},{40,20},{44,24},{48,28},{52,3... | collective-permute-start | bytes 196616 | tf_op jit(solution)/shard_map/ppermute | solution.py:26
  451.6 52.1 %collective-permute-start.50 = (bf16[2,16,1024]{1,2,0:T(8,128)(2,1)S(1)}, bf16[2,16,1024]{1,2,0:T(8,128)(2,1)S(1)}, u32[]{:S(2)}, u32[]{:S(2)}) collective-permute-start(bf16[2,16,1024]{1,2,0:T(8,128)(2,1)S(1)} %copy-done.38), channel_id=1, source_target_pairs={{0,8},{4,12},{8,16},{12,20},{16,24},{20,28},{24,32},{28,36},{32,40... | collective-permute-start | bytes 196616 | tf_op jit(solution)/shard_map/ppermute | solution.py:26
  465.0 65.3 %collective-permute-start.49 = (bf16[2,16,1024]{1,2,0:T(8,128)(2,1)S(1)}, bf16[2,16,1024]{1,2,0:T(8,128)(2,1)S(1)}, u32[]{:S(2)}, u32[]{:S(2)}) collective-permute-start(bf16[2,16,1024]{1,2,0:T(8,128)(2,1)S(1)} %copy-done.38), channel_id=1, source_target_pairs={{24,0},{28,4},{32,8},{36,12},{40,16},{44,20},{48,24},{52,28},{56,3... | collective-permute-start | bytes 196616 | tf_op jit(solution)/shard_map/ppermute | solution.py:26
  481.2 63.9 %collective-permute-start.33 = (bf16[2,32,1024]{1,2,0:T(8,128)(2,1)}, bf16[2,32,1024]{1,2,0:T(8,128)(2,1)}, u32[]{:S(2)}, u32[]{:S(2)}) collective-permute-start(bf16[2,32,1024]{1,2,0:T(8,128)(2,1)} %get-tuple-element.88), channel_id=1, source_target_pairs={{0,12},{4,16},{8,20},{12,24},{16,28},{20,32},{24,36},{28,40},{32,4... | collective-permute-start | bytes 393224 | tf_op jit(solution)/shard_map/ppermute | solution.py:26
  483.2 65.5 %collective-permute-start.32 = (bf16[2,32,1024]{1,2,0:T(8,128)(2,1)}, bf16[2,32,1024]{1,2,0:T(8,128)(2,1)}, u32[]{:S(2)}, u32[]{:S(2)}) collective-permute-start(bf16[2,32,1024]{1,2,0:T(8,128)(2,1)} %get-tuple-element.88), channel_id=1, source_target_pairs={{4,0},{8,4},{12,8},{16,12},{20,16},{24,20},{28,24},{32,28},{36,32}... | collective-permute-start | bytes 393224 | tf_op jit(solution)/shard_map/ppermute | solution.py:26
  501.7 48.9 %collective-permute-start.35 = (bf16[2,32,1024]{1,2,0:T(8,128)(2,1)}, bf16[2,32,1024]{1,2,0:T(8,128)(2,1)}, u32[]{:S(2)}, u32[]{:S(2)}) collective-permute-start(bf16[2,32,1024]{1,2,0:T(8,128)(2,1)} %get-tuple-element.89), channel_id=1, source_target_pairs={{0,8},{4,12},{8,16},{12,20},{16,24},{20,28},{24,32},{28,36},{32,40... | collective-permute-start | bytes 393224 | tf_op jit(solution)/shard_map/ppermute | solution.py:26
  503.6 52.7 %collective-permute-start.34 = (bf16[2,32,1024]{1,2,0:T(8,128)(2,1)}, bf16[2,32,1024]{1,2,0:T(8,128)(2,1)}, u32[]{:S(2)}, u32[]{:S(2)}) collective-permute-start(bf16[2,32,1024]{1,2,0:T(8,128)(2,1)} %get-tuple-element.89), channel_id=1, source_target_pairs={{8,0},{12,4},{16,8},{20,12},{24,16},{28,20},{32,24},{36,28},{40,32... | collective-permute-start | bytes 393224 | tf_op jit(solution)/shard_map/ppermute | solution.py:26
  542.3 17.5 %collective-permute-start.37 = (bf16[2,32,1024]{1,2,0:T(8,128)(2,1)}, bf16[2,32,1024]{1,2,0:T(8,128)(2,1)}, u32[]{:S(2)}, u32[]{:S(2)}) collective-permute-start(bf16[2,32,1024]{1,2,0:T(8,128)(2,1)} %get-tuple-element.90), channel_id=1, source_target_pairs={{0,4},{4,8},{8,12},{12,16},{16,20},{20,24},{24,28},{28,32},{32,36}... | collective-permute-start | bytes 393224 | tf_op jit(solution)/shard_map/ppermute | solution.py:26
  545.1 18.9 %collective-permute-start.36 = (bf16[2,32,1024]{1,2,0:T(8,128)(2,1)}, bf16[2,32,1024]{1,2,0:T(8,128)(2,1)}, u32[]{:S(2)}, u32[]{:S(2)}) collective-permute-start(bf16[2,32,1024]{1,2,0:T(8,128)(2,1)} %get-tuple-element.90), channel_id=1, source_target_pairs={{12,0},{16,4},{20,8},{24,12},{28,16},{32,20},{36,24},{40,28},{44,3... | collective-permute-start | bytes 393224 | tf_op jit(solution)/shard_map/ppermute | solution.py:26
  548.7 17.9 %collective-permute-start.30 = (bf16[2,64,1024]{1,2,0:T(8,128)(2,1)}, bf16[2,64,1024]{1,2,0:T(8,128)(2,1)S(1)}, u32[]{:S(2)}, u32[]{:S(2)}) collective-permute-start(bf16[2,64,1024]{1,2,0:T(8,128)(2,1)} %fusion.19), channel_id=1, source_target_pairs={{0,4},{4,8},{8,12},{12,16},{16,20},{20,24},{24,28},{28,32},{32,36}... | collective-permute-start | bytes 786440 | tf_op jit(solution)/shard_map/ppermute | solution.py:26
  550.6 15.9 %collective-permute-start.29 = (bf16[2,64,1024]{1,2,0:T(8,128)(2,1)}, bf16[2,64,1024]{1,2,0:T(8,128)(2,1)S(1)}, u32[]{:S(2)}, u32[]{:S(2)}) collective-permute-start(bf16[2,64,1024]{1,2,0:T(8,128)(2,1)} %fusion.19), channel_id=1, source_target_pairs={{4,0},{8,4},{12,8},{16,12},{20,16},{24,20},{28,24},{32,28},{36,32}... | collective-permute-start | bytes 786440 | tf_op jit(solution)/shard_map/ppermute | solution.py:26
  556.3 45.7 %collective-permute-start.27 = (bf16[2,128,8,128]{3,1,2,0:T(8,128)(2,1)}, bf16[2,128,8,128]{3,1,2,0:T(8,128)(2,1)}, u32[]{:S(2)}, u32[]{:S(2)}) collective-permute-start(bf16[2,128,8,128]{3,1,2,0:T(8,128)(2,1)} %maximum_bitcast_fusion.1), channel_id=1, source_target_pairs={{0,4},{4,8},{8,12},{12,16},{16,20},{20,24},{24,28},{28,32},{32,36}... | collective-permute-start | bytes 1572872 | tf_op jit(solution)/shard_map/ppermute | solution.py:26
  559.9 42.2 %collective-permute-start.28 = (bf16[2,128,8,128]{3,1,2,0:T(8,128)(2,1)}, bf16[2,128,8,128]{3,1,2,0:T(8,128)(2,1)}, u32[]{:S(2)}, u32[]{:S(2)}) collective-permute-start(bf16[2,128,8,128]{3,1,2,0:T(8,128)(2,1)} %maximum_bitcast_fusion.2), channel_id=1, source_target_pairs={{4,0},{8,4},{12,8},{16,12},{20,16},{24,20},{28,24},{32,28},{36,32}... | collective-permute-start | bytes 1572872 | tf_op jit(solution)/shard_map/ppermute | solution.py:26
  566.4 17.9 %collective-permute-start.38 = (bf16[2,32,1024]{1,2,0:T(8,128)(2,1)S(1)}, bf16[2,32,1024]{1,2,0:T(8,128)(2,1)S(1)}, u32[]{:S(2)}, u32[]{:S(2)}) collective-permute-start(bf16[2,32,1024]{1,2,0:T(8,128)(2,1)S(1)} %fusion.29), channel_id=1, source_target_pairs={{0,16},{4,20},{8,24},{12,28},{16,0},{20,4},{24,8},{28,12},{32,48},... | collective-permute-start | bytes 393224 | tf_op jit(solution)/shard_map/ppermute | solution.py:20
  567.7 31.5 %collective-permute-start.31 = (bf16[2,64,1024]{1,2,0:T(8,128)(2,1)}, bf16[2,64,1024]{1,2,0:T(8,128)(2,1)S(1)}, u32[]{:S(2)}, u32[]{:S(2)}) collective-permute-start(bf16[2,64,1024]{1,2,0:T(8,128)(2,1)} %fusion.22), channel_id=1, source_target_pairs={{0,8},{4,12},{8,0},{12,4},{16,24},{20,28},{24,16},{28,20},{32,40},... | collective-permute-start | bytes 786440 | tf_op jit(solution)/shard_map/ppermute | solution.py:20
  (82 other events, 930.7 us)
where the time goes:
time: 622 us; the launch traced here: 610 us
  waiting for transfers between devices  231 us (37%)
  starting transfers between devices  213 us (34%)
  local copies, waits for them, and re-layouts  83.2 us (13%)
  other arithmetic  44.5 us (7%)
  matrix products  23.8 us (4%)
  blocking collectives  11 us (2%)
    ppermute x46, starting transfers between devices, from_behind(): return lax.ppermute(shard, axis, pairs)  201 us
    ppermute x46, waiting for transfers between devices, from_behind(): return lax.ppermute(shard, axis, pairs)  185 us
    ppermute x6, waiting for transfers between devices, swapped(): lax.ppermute(shard, axis, [(i, i ^ 1 << distance) for i in range(lax.axis...  45.7 us
    concatenate x2, local copies, waits for them, and re-layouts, collect(): doubled = jnp.concatenate([ordered, ordered], axis=1)  16.2 us
    reshape x21, local copies, waits for them, and re-layouts, expand(): jnp.broadcast_to(x[:, None], (x.shape[0], 2 ** level) + x.shape[1:])  12.9 us
  transfers between devices with their start and end apart: 54, of which 23 were waited for; matrix products, arithmetic and copies ran while one was open for 13% of the time, Pallas kernels for 0%

commit v1 on v0

v1 whole, which is shorter than its diff:
```python
import math

import jax
import jax.numpy as jnp
from jax import lax
from jax.experimental import pallas as pl
from jax.experimental.pallas import tpu as pltpu
from jax.sharding import PartitionSpec as P

DH = 128
BLOCK = 128
GROUP = 8
TOKENS = GROUP * BLOCK
COARSE = TOKENS // 2 + TOKENS // 4 + TOKENS // 8
START = {1: 0, 2: TOKENS // 2, 3: TOKENS // 2 + TOKENS // 4}
EPS = 1e-06
FLOOR = -1e30
SCALE = 1.0 / math.sqrt(DH)
VMEM = pl.BlockSpec(memory_space=pltpu.VMEM)
F32 = jnp.float32
BF16 = jnp.bfloat16


def call(kernel, outs, n_in, scratch=(), flops=0, nbytes=0):
    return pl.pallas_call(
        kernel,
        out_shape=[jax.ShapeDtypeStruct(s, d) for s, d in outs],
        in_specs=[VMEM] * n_in,
        out_specs=[VMEM] * len(outs),
        scratch_shapes=[pltpu.VMEM(s, d) for s, d in scratch],
        compiler_params=pltpu.CompilerParams(vmem_limit_bytes=48 * 1024 * 1024),
        cost_estimate=pl.CostEstimate(flops=flops, bytes_accessed=nbytes, transcendentals=0),
    )


def rows(b, n=1):
    return pl.ds(b * BLOCK, n * BLOCK)


def nt(a, b):
    return lax.dot_general(a, b, (((1,), (1,)), ((), ())), preferred_element_type=F32)


def nn(a, b):
    return lax.dot_general(a, b, (((1,), (0,)), ((), ())), preferred_element_type=F32)


def tn(a, b):
    return lax.dot_general(a, b, (((0,), (0,)), ((), ())), preferred_element_type=F32)


def member():
    return lax.rem(lax.axis_index("seq"), GROUP)


def group():
    return lax.div(lax.axis_index("seq"), GROUP)


def pack_kernel(q, k, v, d, *messages):
    me = member()
    for step, message in enumerate(messages):
        cols = pl.ds(pl.multiple_of((me ^ step) * DH, DH), DH)
        for i, x in enumerate((q, k, v, d)):
            message[i] = x[:, cols]


def assemble_kernel(*refs):
    parts, (q, k, v, d, qp, kp, vp, pair, other, f32) = refs[:GROUP], refs[GROUP:]
    me = member()
    odd = lax.rem(group(), 2)
    for step, part in enumerate(parts):
        at = pl.ds(pl.multiple_of((me ^ step) * BLOCK, BLOCK), BLOCK)
        for i, x in enumerate((q, k, v, d)):
            x[at, :] = part[i]
    for x, p in ((q, qp), (k, kp), (v, vp)):
        f32[...] = x[...].astype(F32)
        n = TOKENS
        for level in (1, 2, 3):
            n //= 2
            pooled = f32[pl.ds(0, n, 2), :] + f32[pl.ds(1, n, 2), :]
            p[pl.ds(START[level], n), :] = (pooled * 0.5**level).astype(BF16)
            f32[pl.ds(0, n), :] = pooled
    last = (GROUP - 1) * BLOCK
    near = pl.ds(pl.multiple_of((1 - odd) * last, BLOCK), BLOCK)
    far = pl.ds(pl.multiple_of(odd * last, BLOCK), BLOCK)
    pair[0] = k[near, :]
    pair[1] = v[near, :]
    pair[2] = kp[pl.ds(START[3], BLOCK), :]
    pair[3] = vp[pl.ds(START[3], BLOCK), :]
    other[0] = k[far, :]
    other[1] = v[far, :]


def extend(ext, x, pair, other, i):
    odd = lax.rem(group(), 2) == 1
    ext[rows(1, GROUP), :] = x[...]
    ext[rows(0), :] = jnp.where(odd, pair[i], other[i])
    ext[rows(GROUP + 1), :] = jnp.where(odd, other[i], pair[i])


def spread(scratch, x, n, times=2):
    for j in range(times):
        scratch[pl.ds(j, n, times), :] = x
    return scratch[pl.ds(0, n * times), :]


def row_sum(x):
    ones = jnp.ones((8, DH), BF16)
    high = x.astype(BF16)
    low = (x - high.astype(F32)).astype(BF16)
    return (nt(ones, high) + nt(ones, low))[:1]


def forward_kernel(
    q, k, v, d, qp, kp, vp, pair, other, gain,
    attn, stats, w0, wc, share, share1, share2,
    ext_k, ext_v, tops, totals, sums, up_m, up_t, up_s,
):
    z = group()
    extend(ext_k, k, pair, other, 0)
    extend(ext_v, v, pair, other, 1)

    def block(queries, keys, values, at, invalid=None):
        scores = nt(queries, keys) * SCALE
        if invalid is not None:
            side, bad = invalid
            lane = lax.broadcasted_iota(jnp.int32, scores.shape, 1) // BLOCK
            scores = jnp.where((lane == side) & bad, FLOOR, scores)
        top = jnp.max(scores, axis=1, keepdims=True)
        weights = jnp.exp(scores - top)
        rounded = weights.astype(BF16)
        tops[at, :] = jnp.broadcast_to(top, (BLOCK, DH))
        totals[at, :] = jnp.broadcast_to(jnp.sum(weights, axis=1, keepdims=True), (BLOCK, DH))
        sums[at, :] = nn(rounded, values)
        return rounded

    base = TOKENS // BLOCK
    for b in range(GROUP):
        invalid = (0, z == 0) if b == 0 else None
        if b == GROUP - 1:
            invalid = (2, z == lax.axis_size("seq") // GROUP - 1)
        w0[rows(b), :] = block(q[rows(b), :], ext_k[rows(b, 3), :], ext_v[rows(b, 3), :], rows(b), invalid)
    for c in range(6):
        w = block(qp[rows(c), :], kp[rows(c ^ 1), :], vp[rows(c ^ 1), :], rows(base + c))
        wc[rows(c), :] = w
    wc[rows(6), :] = block(qp[rows(6), :], pair[2], pair[3], rows(base + 6))

    at = rows(base + 6)
    m, t, s = tops[at, :], totals[at, :] * 8.0, sums[at, :] * 8.0
    n = TOKENS // 8
    for level, out in ((2, share2), (1, share1), (0, share)):
        em, et, es = spread(up_m, m, n), spread(up_t, t, n), spread(up_s, s, n)
        n *= 2
        at = pl.ds(TOKENS + START[level], n) if level else pl.ds(0, n)
        own = tops[at, :]
        m = jnp.maximum(own, em)
        here = 2.0**level * jnp.exp(own - m)
        up = jnp.exp(em - m)
        t = here * totals[at, :] + up * et
        s = here * sums[at, :] + up * es
        if level == 0:
            inverse = 1.0 / t
            here, up = here * inverse, up * inverse
            s = s * inverse
        out[0] = here
        out[1] = up
    rounded = s.astype(BF16)
    attn[...] = rounded
    flat = rounded.astype(F32)
    scaled = d[...].astype(F32) * gain[...]
    square = flat * flat
    inner = scaled * flat
    for b in range(GROUP):
        one = slice(b * BLOCK, (b + 1) * BLOCK)
        stats[0, pl.ds(b, 1), :] = row_sum(square[one])
        stats[1, pl.ds(b, 1), :] = row_sum(inner[one])


def backward_kernel(
    features,
    s0, s1, s2, s3, q, k, v, d, qp, kp, vp, pair, other, gain,
    attn, w0, wc, share, share1, share2,
    out, q_grad, k_grad, v_grad, pair_out, other_out,
    ext_k, ext_v, g0, gc, off0, offc, sl0, slc, buf, buf2, grads,
):
    odd = lax.rem(group(), 2) == 1
    extend(ext_k, k, pair, other, 0)
    extend(ext_v, v, pair, other, 1)
    sums = s0[...] + s1[...] + s2[...] + s3[...]
    inv_row = lax.rsqrt(sums[0] * (1.0 / features) + EPS)
    drop_row = inv_row * inv_row * inv_row * sums[1] * (1.0 / features)
    for b in range(GROUP):
        inv = jnp.broadcast_to(inv_row[b : b + 1], (BLOCK, DH)).T
        drop = jnp.broadcast_to(drop_row[b : b + 1], (BLOCK, DH)).T
        flat = attn[rows(b), :].astype(F32)
        scale_inv = inv * gain[...]
        out[rows(b), :] = (flat * scale_inv).astype(BF16)
        scaled = d[rows(b), :].astype(F32) * gain[...]
        grad = (inv * scaled - flat * drop).astype(BF16).astype(F32)
        dot = jnp.broadcast_to(jnp.sum(grad * flat, axis=1, keepdims=True), (BLOCK, DH))
        here, up = share[0, rows(b), :], share[1, rows(b), :]
        g0[rows(b), :] = (here * grad).astype(BF16)
        off0[rows(b), :] = here * dot
        buf[rows(b), :] = up * grad
        buf2[rows(b), :] = up * dot
    n = TOKENS
    for level, sh in ((1, share1), (2, share2), (3, None)):
        n //= 2
        g = buf[pl.ds(0, n, 2), :] + buf[pl.ds(1, n, 2), :]
        o = buf2[pl.ds(0, n, 2), :] + buf2[pl.ds(1, n, 2), :]
        at = pl.ds(START[level], n)
        if sh is None:
            gc[at, :] = (g * 8.0).astype(BF16)
            offc[at, :] = o * 8.0
        else:
            here, up = sh[0], sh[1]
            gc[at, :] = (g * here).astype(BF16)
            offc[at, :] = o * here
            buf[pl.ds(0, n), :] = g * up
            buf2[pl.ds(0, n), :] = o * up

    def block(grad, values, weights, offset, keys):
        pressure = nt(grad, values)
        wide = jnp.concatenate([offset] * (values.shape[0] // BLOCK), axis=1)
        slope = (weights.astype(F32) * (pressure - wide)).astype(BF16)
        return slope, nn(slope, keys) * SCALE

    for c in range(7):
        values = pair[3] if c == 6 else vp[rows(c ^ 1), :]
        keys = pair[2] if c == 6 else kp[rows(c ^ 1), :]
        slope, part = block(gc[rows(c), :], values, wc[rows(c), :], offc[rows(c), :], keys)
        slc[rows(c), :] = slope
        grads[rows(c), :] = part
    pair_out[2] = (tn(slc[rows(6), :], qp[rows(6), :]) * SCALE).astype(BF16)
    pair_out[3] = tn(wc[rows(6), :], gc[rows(6), :]).astype(BF16)
    e = grads[rows(6), :] * 0.125
    e = grads[rows(4, 2), :] * 0.25 + spread(buf, e, 128)
    e = grads[rows(0, 4), :] * 0.5 + spread(buf, e, 256)
    spread(buf, e, 512)
    for b in range(GROUP):
        slope, part = block(
            g0[rows(b), :], ext_v[rows(b, 3), :], w0[rows(b), :], off0[rows(b), :], ext_k[rows(b, 3), :]
        )
        sl0[rows(b), :] = slope
        q_grad[rows(b), :] = (part + buf[rows(b), :]).astype(BF16)

    def key_value(weight, factor, left, left_c, right, right_c, res):
        for c in range(6):
            grads[rows(c ^ 1), :] = tn(left_c[rows(c), :], right_c[rows(c), :])
        e = grads[rows(4, 2), :] * (0.25 * factor)
        e = grads[rows(0, 4), :] * (0.5 * factor) + spread(buf, e, 256)
        spread(buf, e, 512)
        edges = []
        for j in range(-1, GROUP + 1):
            total = None
            for side in range(3):
                b = j + 1 - side
                if 0 <= b < GROUP:
                    part = tn(left[rows(b), pl.ds(side * BLOCK, BLOCK)], right[rows(b), :])
                    total = part if total is None else total + part
            if 0 <= j < GROUP:
                res[rows(j), :] = total * factor + buf[rows(j), :]
            else:
                edges.append((total * factor).astype(BF16))
        pair_out[weight] = jnp.where(odd, edges[0], edges[1])
        other_out[weight] = jnp.where(odd, edges[1], edges[0])

    key_value(0, SCALE, sl0, slc, q, qp, k_grad)
    key_value(1, 1.0, w0, wc, g0, gc, v_grad)


def collect_kernel(out, q_grad, k_grad, v_grad, pair, other, *refs):
    messages, buf = refs[:-1], refs[-1]
    odd = lax.rem(group(), 2) == 1
    me = member()
    finished = []
    for i, x in enumerate((k_grad, v_grad)):
        spread(buf, pair[2 + i].astype(F32) * 0.125, 128, 8)
        buf[...] += x[...]
        buf[rows(0), :] += jnp.where(odd, pair[i], other[i]).astype(F32)
        buf[rows(GROUP - 1), :] += jnp.where(odd, other[i], pair[i]).astype(F32)
        for step, message in enumerate(messages):
            at = pl.ds(pl.multiple_of((me ^ step) * BLOCK, BLOCK), BLOCK)
            message[2 + i] = buf[at, :].astype(BF16)
    for step, message in enumerate(messages):
        at = pl.ds(pl.multiple_of((me ^ step) * BLOCK, BLOCK), BLOCK)
        message[0] = out[at, :]
        message[1] = q_grad[at, :]


def unpack_kernel(*refs):
    parts, results = refs[:GROUP], refs[GROUP:]
    me = member()
    for step, part in enumerate(parts):
        cols = pl.ds(pl.multiple_of((me ^ step) * DH, DH), DH)
        for i, x in enumerate(results):
            x[:, cols] = part[i]


def seq_permute(x, pairs):
    return lax.ppermute(x, "seq", pairs)


def swap(x, bits):
    return seq_permute(x, [(i, i ^ bits) for i in range(lax.axis_size("seq"))])


def swap_all(messages):
    result = [messages[0]] + [None] * (GROUP - 1)
    for step in (4, 5, 6, 7, 2, 3, 1):
        result[step] = swap(messages[step], step)
    return result


def swap_other(x):
    groups = lax.axis_size("seq") // GROUP
    up = [(g * GROUP + r, (g + 1) * GROUP + r) for g in range(1, groups - 1, 2) for r in range(GROUP)]
    return seq_permute(x, up + [(target, source) for source, target in up])


def local(query, keys, values, gain, out_grad):
    token = (BLOCK, query.shape[1])
    message = ((4, BLOCK, DH), BF16)
    edge = ((2, BLOCK, DH), BF16)
    whole = ((TOKENS, DH), BF16)
    whole_f = ((TOKENS, DH), F32)
    coarse = ((COARSE, DH), BF16)
    coarse_f = ((COARSE, DH), F32)
    extended = ((TOKENS + 2 * BLOCK, DH), BF16)
    wide = ((TOKENS, 3 * BLOCK), BF16)
    shares = [((2, TOKENS >> level, DH), F32) for level in range(3)]
    every = ((TOKENS + COARSE, DH), F32)
    features = query.shape[1] * lax.axis_size("head")

    my_gain = lax.dynamic_slice_in_dim(gain, (lax.axis_index("seq") % GROUP) * DH, DH).reshape(1, DH)
    packed = call(pack_kernel, [message] * GROUP, 4)(query, keys, values, out_grad)
    parts = swap_all(packed)
    q, k, v, d, qp, kp, vp, pair, other = call(
        assemble_kernel, [whole] * 4 + [coarse] * 3 + [message, edge], GROUP, [whole_f]
    )(*parts)
    pair, other = swap(pair, GROUP), swap_other(other)
    attn, stats, w0, wc, *share = call(
        forward_kernel,
        [whole, ((2, GROUP, DH), F32), wide, coarse] + shares,
        10,
        [extended] * 2 + [every] * 3 + [whole_f] * 3,
    )(q, k, v, d, qp, kp, vp, pair, other, my_gain)
    stats = stats + swap(stats, 1)
    stats = stats + swap(stats, 4) + swap(stats, 6) + swap(stats, 2)
    heads = lax.axis_size("head")
    stats = [stats] + [
        lax.ppermute(stats, "head", [(i, i ^ step) for i in range(heads)]) for step in (2, 3, 1)
    ]

    def backward(*refs):
        backward_kernel(features, *refs)

    out, q_grad, k_grad, v_grad, pair_back, other_back = call(
        backward,
        [whole, whole, whole_f, whole_f, message, edge],
        20,
        [extended] * 2 + [whole, coarse, whole_f, coarse_f, wide, coarse, whole_f, whole_f, coarse_f],
    )(*stats, q, k, v, d, qp, kp, vp, pair, other, my_gain, attn, w0, wc, *share)
    pair_back, other_back = swap(pair_back, GROUP), swap_other(other_back)
    messages = call(collect_kernel, [message] * GROUP, 6, [whole_f])(
        out, q_grad, k_grad, v_grad, pair_back, other_back
    )
    parts = swap_all(messages)
    return call(unpack_kernel, [(token, BF16)] * 4, GROUP)(*parts)


def solution(mesh):
    spec = P("seq", "head")
    in_specs = (spec, spec, spec, P("head"), spec)
    return jax.shard_map(
        local, mesh=mesh, in_specs=in_specs, out_specs=(spec,) * 4, check_vma=False
    )
```

time: 622 us -> 92.8 us (0.15)
  the two profiles are of different devices: /device:TPU:96 before, /device:TPU:33 now
where the time goes in v1:
time: 92.8 us; the launch traced here: 92.4 us
  starting transfers between devices  41 us (44%)
  waiting for transfers between devices  33.6 us (36%)
  Pallas kernels  12.1 us (13%)
  local copies, waits for them, and re-layouts  4.88 us (5%)
    ppermute x22, starting transfers between devices, seq_permute(): return lax.ppermute(x, 'seq', pairs)  37.1 us
    ppermute x22, waiting for transfers between devices, seq_permute(): return lax.ppermute(x, 'seq', pairs)  30.3 us
    pallas_call x1, Pallas kernels, local(): call(forward_kernel, [whole, ((2, GROUP, DH), F32), wide, coarse] + share...  4.95 us
    unnamed x12, local copies, waits for them, and re-layouts  4.81 us
    pallas_call x1, Pallas kernels, local(): call(backward, [whole, whole, whole_f, whole_f, message, edge], 20, [exte...  4.8 us
    ppermute x3, starting transfers between devices, local(): lax.ppermute(stats, 'head', [(i, i ^ step) for i in range(heads)])  3.91 us
    ppermute x3, waiting for transfers between devices, local(): lax.ppermute(stats, 'head', [(i, i ^ step) for i in range(heads)])  3.34 us
  transfers between devices with their start and end apart: 25, of which 16 were waited for; matrix products, arithmetic and copies ran while one was open for 0% of the time, Pallas kernels for 0%

profile of v1, /device:TPU:33, one launch (start us, length us, event | category | flops | bytes accessed | tf_op | source)
XLA Modules:
  0.0 92.4 jit_solution(12274294817935842152)
XLA Ops:
  0.7 0.9 %copy-done.2 = bf16[128,1024]{1,0:T(8,128)(2,1)S(1)} copy-done((bf16[128,1024]{1,0:T(8,128)(2,1)S(1)}, bf16[128,1024]{1,0:T(8,128)(2,1)}, u32[]{:S(2)}) %copy-start.2) | copy-done | bytes 262168
  1.6 0.9 %copy-done.3 = bf16[128,1024]{1,0:T(8,128)(2,1)S(1)} copy-done((bf16[128,1024]{1,0:T(8,128)(2,1)S(1)}, bf16[128,1024]{1,0:T(8,128)(2,1)}, u32[]{:S(2)}) %copy-start.3) | copy-done | bytes 262168
  2.6 0.9 %copy-done.4 = bf16[128,1024]{1,0:T(8,128)(2,1)S(1)} copy-done((bf16[128,1024]{1,0:T(8,128)(2,1)S(1)}, bf16[128,1024]{1,0:T(8,128)(2,1)}, u32[]{:S(2)}) %copy-start.4) | copy-done | bytes 262168
  3.5 0.9 %copy-done.5 = bf16[128,1024]{1,0:T(8,128)(2,1)S(1)} copy-done((bf16[128,1024]{1,0:T(8,128)(2,1)S(1)}, bf16[128,1024]{1,0:T(8,128)(2,1)}, u32[]{:S(2)}) %copy-start.5) | copy-done | bytes 262168
  4.7 0.8 collective-permute-start
  5.5 1.2 %collective-permute-start.1 = (bf16[4,128,128]{2,1,0:T(8,128)(2,1)S(1)}, bf16[4,128,128]{2,1,0:T(8,128)(2,1)S(1)}, u32[]{:S(2)}, u32[]{:S(2)}) collective-permute-start(bf16[4,128,128]{2,1,0:T(8,128)(2,1)S(1)} %get-tuple-element.44), channel_id=1, source_target_pairs={{0,8},{4,12},{8,0},{12,4},{16,24},{20,28},{24,16},{28,20},{32,40},... | collective-permute-start | bytes 393224 | tf_op jit(solution)/shard_map/ppermute | solution.py:302
  6.7 0.5 collective-permute-start.2
  7.2 2.7 %collective-permute-start.3 = (bf16[4,128,128]{2,1,0:T(8,128)(2,1)S(1)}, bf16[4,128,128]{2,1,0:T(8,128)(2,1)S(1)}, u32[]{:S(2)}, u32[]{:S(2)}) collective-permute-start(bf16[4,128,128]{2,1,0:T(8,128)(2,1)S(1)} %get-tuple-element.46), channel_id=1, source_target_pairs={{0,16},{4,20},{8,24},{12,28},{16,0},{20,4},{24,8},{28,12},{32,48},... | collective-permute-start | bytes 393224 | tf_op jit(solution)/shard_map/ppermute | solution.py:302
  10.0 0.6 collective-permute-start.4
  10.5 2.5 %collective-permute-start.5 = (bf16[4,128,128]{2,1,0:T(8,128)(2,1)S(1)}, bf16[4,128,128]{2,1,0:T(8,128)(2,1)S(1)}, u32[]{:S(2)}, u32[]{:S(2)}) collective-permute-start(bf16[4,128,128]{2,1,0:T(8,128)(2,1)S(1)} %get-tuple-element.48), channel_id=1, source_target_pairs={{0,24},{4,28},{8,16},{12,20},{16,8},{20,12},{24,0},{28,4},{32,56},... | collective-permute-start | bytes 393224 | tf_op jit(solution)/shard_map/ppermute | solution.py:302
  13.0 1.3 %collective-permute-start.6 = (bf16[4,128,128]{2,1,0:T(8,128)(2,1)S(1)}, bf16[4,128,128]{2,1,0:T(8,128)(2,1)S(1)}, u32[]{:S(2)}, u32[]{:S(2)}) collective-permute-start(bf16[4,128,128]{2,1,0:T(8,128)(2,1)S(1)} %get-tuple-element.49), channel_id=1, source_target_pairs={{0,28},{4,24},{8,20},{12,16},{16,12},{20,8},{24,4},{28,0},{32,60},... | collective-permute-start | bytes 393224 | tf_op jit(solution)/shard_map/ppermute | solution.py:302
  14.3 4.1 %collective-permute-done.3.refs_4_ = bf16[4,128,128]{2,1,0:T(8,128)(2,1)S(1)} collective-permute-done((bf16[4,128,128]{2,1,0:T(8,128)(2,1)S(1)}, bf16[4,128,128]{2,1,0:T(8,128)(2,1)S(1)}, u32[]{:S(2)}, u32[]{:S(2)}) %collective-permute-start.3) | collective-permute-done | bytes 131104 | tf_op jit(solution)/shard_map/ppermute | solution.py:302
  18.4 3.1 %collective-permute-done.4.refs_5_ = bf16[4,128,128]{2,1,0:T(8,128)(2,1)S(1)} collective-permute-done((bf16[4,128,128]{2,1,0:T(8,128)(2,1)S(1)}, bf16[4,128,128]{2,1,0:T(8,128)(2,1)S(1)}, u32[]{:S(2)}, u32[]{:S(2)}) %collective-permute-start.4) | collective-permute-done | bytes 131104 | tf_op jit(solution)/shard_map/ppermute | solution.py:302
  21.5 0.9 %collective-permute-done.5.refs_6_ = bf16[4,128,128]{2,1,0:T(8,128)(2,1)S(1)} collective-permute-done((bf16[4,128,128]{2,1,0:T(8,128)(2,1)S(1)}, bf16[4,128,128]{2,1,0:T(8,128)(2,1)S(1)}, u32[]{:S(2)}, u32[]{:S(2)}) %collective-permute-start.5) | collective-permute-done | bytes 131104 | tf_op jit(solution)/shard_map/ppermute | solution.py:302
  22.4 3.0 %collective-permute-done.6.refs_7_ = bf16[4,128,128]{2,1,0:T(8,128)(2,1)S(1)} collective-permute-done((bf16[4,128,128]{2,1,0:T(8,128)(2,1)S(1)}, bf16[4,128,128]{2,1,0:T(8,128)(2,1)S(1)}, u32[]{:S(2)}, u32[]{:S(2)}) %collective-permute-start.6) | collective-permute-done | bytes 131104 | tf_op jit(solution)/shard_map/ppermute | solution.py:302
  25.4 0.4 shard_map.85
  25.8 1.4 %collective-permute-start.7 = (bf16[4,128,128]{2,1,0:T(8,128)(2,1)S(1)}, bf16[4,128,128]{2,1,0:T(8,128)(2,1)S(1)}, u32[]{:S(2)}, u32[]{:S(2)}) collective-permute-start(bf16[4,128,128]{2,1,0:T(8,128)(2,1)S(1)} %get-tuple-element.57), channel_id=1, source_target_pairs={{0,32},{4,36},{8,40},{12,44},{16,48},{20,52},{24,56},{28,60},{32,0... | collective-permute-start | bytes 393224 | tf_op jit(solution)/shard_map/ppermute | solution.py:302
  27.1 3.9 %collective-permute-start.8 = (bf16[2,128,128]{2,1,0:T(8,128)(2,1)S(1)}, bf16[2,128,128]{2,1,0:T(8,128)(2,1)S(1)}, u32[]{:S(2)}, u32[]{:S(2)}) collective-permute-start(bf16[2,128,128]{2,1,0:T(8,128)(2,1)S(1)} %get-tuple-element.58), channel_id=1, source_target_pairs={{32,64},{36,68},{40,72},{44,76},{48,80},{52,84},{56,88},{60,92},{9... | collective-permute-start | bytes 196616 | tf_op jit(solution)/shard_map/ppermute | solution.py:302
  31.1 1.9 %collective-permute-done.8.other.refs_12_ = bf16[2,128,128]{2,1,0:T(8,128)(2,1)S(1)} collective-permute-done((bf16[2,128,128]{2,1,0:T(8,128)(2,1)S(1)}, bf16[2,128,128]{2,1,0:T(8,128)(2,1)S(1)}, u32[]{:S(2)}, u32[]{:S(2)}) %collective-permute-start.8) | collective-permute-done | bytes 65568 | tf_op jit(solution)/shard_map/ppermute | solution.py:302
  33.0 5.0 %shard_map.86 = (bf16[1024,128]{1,0:T(8,128)(2,1)S(1)}, f32[2,8,128]{2,1,0:T(8,128)S(1)}, bf16[1024,384]{1,0:T(8,128)(2,1)S(1)}, bf16[896,128]{1,0:T(8,128)(2,1)...) custom-call(bf16[1024,128]{1,0:T(8,128)(2,1)S(1)} %get-tuple-element.50.q.refs_4_, ...), custom_call_target="tpu_custom_call" | custom-call | tf_op jit(solution)/shard_map/pallas_call | solution.py:343
  38.0 1.0 %copy-done.1 = f32[2,1024,128]{2,1,0:T(8,128)} copy-done((f32[2,1024,128]{2,1,0:T(8,128)}, f32[2,1024,128]{2,1,0:T(8,128)S(1)}, u32[]{:S(2)}) %copy-start.1) | copy-done | bytes 1048600
  39.0 1.0 %collective-permute-start.9 = (f32[2,8,128]{2,1,0:T(8,128)S(1)}, f32[2,8,128]{2,1,0:T(8,128)S(1)}, u32[]{:S(2)}, u32[]{:S(2)}) collective-permute-start(f32[2,8,128]{2,1,0:T(8,128)S(1)} %get-tuple-element.59), channel_id=1, source_target_pairs={{0,4},{4,0},{8,12},{12,8},{16,20},{20,16},{24,28},{28,24},{32,36},... | collective-permute-start | bytes 24584 | tf_op jit(solution)/shard_map/ppermute | solution.py:302
  40.0 0.8 collective-permute-done.9
  40.9 2.2 %collective-permute-start.11 = (f32[2,8,128]{2,1,0:T(8,128)S(1)}, f32[2,8,128]{2,1,0:T(8,128)S(1)}, u32[]{:S(2)}, u32[]{:S(2)}) collective-permute-start(f32[2,8,128]{2,1,0:T(8,128)S(1)} %add.21), channel_id=1, source_target_pairs={{0,24},{4,28},{8,16},{12,20},{16,8},{20,12},{24,0},{28,4},{32,56},... | collective-permute-start | bytes 24584 | tf_op jit(solution)/shard_map/ppermute | solution.py:302
  43.1 1.2 %collective-permute-start.10 = (f32[2,8,128]{2,1,0:T(8,128)S(1)}, f32[2,8,128]{2,1,0:T(8,128)S(1)}, u32[]{:S(2)}, u32[]{:S(2)}) collective-permute-start(f32[2,8,128]{2,1,0:T(8,128)S(1)} %add.21), channel_id=1, source_target_pairs={{0,16},{4,20},{8,24},{12,28},{16,0},{20,4},{24,8},{28,12},{32,48},... | collective-permute-start | bytes 24584 | tf_op jit(solution)/shard_map/ppermute | solution.py:302
  44.6 2.5 %collective-permute-done.10 = f32[2,8,128]{2,1,0:T(8,128)S(1)} collective-permute-done((f32[2,8,128]{2,1,0:T(8,128)S(1)}, f32[2,8,128]{2,1,0:T(8,128)S(1)}, u32[]{:S(2)}, u32[]{:S(2)}) %collective-permute-start.10) | collective-permute-done | bytes 8224 | tf_op jit(solution)/shard_map/ppermute | solution.py:302
  47.1 1.3 %collective-permute-start.15 = (f32[2,8,128]{2,1,0:T(8,128)S(1)}, f32[2,8,128]{2,1,0:T(8,128)S(1)}, u32[]{:S(2)}, u32[]{:S(2)}) collective-permute-start(f32[2,8,128]{2,1,0:T(8,128)S(1)} %add_add_fusion.refs_0_), channel_id=1, source_target_pairs={{0,1},{1,0},{2,3},{3,2},{4,5},{5,4},{6,7},{7,6},{8,9},{9,8},{10,11... | collective-permute-start | bytes 24584 | tf_op jit(solution)/shard_map/ppermute | solution.py:353
  48.4 1.9 %collective-permute-start.14 = (f32[2,8,128]{2,1,0:T(8,128)S(1)}, f32[2,8,128]{2,1,0:T(8,128)S(1)}, u32[]{:S(2)}, u32[]{:S(2)}) collective-permute-start(f32[2,8,128]{2,1,0:T(8,128)S(1)} %add_add_fusion.refs_0_), channel_id=1, source_target_pairs={{0,3},{1,2},{2,1},{3,0},{4,7},{5,6},{6,5},{7,4},{8,11},{9,10},{10,... | collective-permute-start | bytes 24584 | tf_op jit(solution)/shard_map/ppermute | solution.py:353
  50.3 0.7 collective-permute-start.13
  51.0 1.1 %collective-permute-done.14.refs_2_ = f32[2,8,128]{2,1,0:T(8,128)S(1)} collective-permute-done((f32[2,8,128]{2,1,0:T(8,128)S(1)}, f32[2,8,128]{2,1,0:T(8,128)S(1)}, u32[]{:S(2)}, u32[]{:S(2)}) %collective-permute-start.14) | collective-permute-done | bytes 8224 | tf_op jit(solution)/shard_map/ppermute | solution.py:353
  52.1 2.3 %collective-permute-done.13.refs_1_ = f32[2,8,128]{2,1,0:T(8,128)S(1)} collective-permute-done((f32[2,8,128]{2,1,0:T(8,128)S(1)}, f32[2,8,128]{2,1,0:T(8,128)S(1)}, u32[]{:S(2)}, u32[]{:S(2)}) %collective-permute-start.13) | collective-permute-done | bytes 8224 | tf_op jit(solution)/shard_map/ppermute | solution.py:353
  54.3 4.8 %shard_map.87 = (bf16[1024,128]{1,0:T(8,128)(2,1)S(1)}, bf16[1024,128]{1,0:T(8,128)(2,1)S(1)}, f32[1024,128]{1,0:T(8,128)S(1)}, f32[1024,128]{1,0:T(8,128)S(1)},...) custom-call(f32[2,8,128]{2,1,0:T(8,128)S(1)} %add_add_fusion.refs_0_, ...), custom_call_target="tpu_custom_call" | custom-call | tf_op jit(solution)/shard_map/pallas_call | solution.py:359
  59.2 5.5 %collective-permute-start.17 = (bf16[2,128,128]{2,1,0:T(8,128)(2,1)S(1)}, bf16[2,128,128]{2,1,0:T(8,128)(2,1)S(1)}, u32[]{:S(2)}, u32[]{:S(2)}) collective-permute-start(bf16[2,128,128]{2,1,0:T(8,128)(2,1)S(1)} %get-tuple-element.71), channel_id=1, source_target_pairs={{32,64},{36,68},{40,72},{44,76},{48,80},{52,84},{56,88},{60,92},{9... | collective-permute-start | bytes 196616 | tf_op jit(solution)/shard_map/ppermute | solution.py:302
  64.7 1.9 %collective-permute-done.17.other = bf16[2,128,128]{2,1,0:T(8,128)(2,1)S(1)} collective-permute-done((bf16[2,128,128]{2,1,0:T(8,128)(2,1)S(1)}, bf16[2,128,128]{2,1,0:T(8,128)(2,1)S(1)}, u32[]{:S(2)}, u32[]{:S(2)}) %collective-permute-start.17) | collective-permute-done | bytes 65568 | tf_op jit(solution)/shard_map/ppermute | solution.py:302
  66.7 0.4 shard_map.88
  67.1 4.4 %collective-permute-start.18 = (bf16[4,128,128]{2,1,0:T(8,128)(2,1)S(1)}, bf16[4,128,128]{2,1,0:T(8,128)(2,1)S(1)}, u32[]{:S(2)}, u32[]{:S(2)}) collective-permute-start(bf16[4,128,128]{2,1,0:T(8,128)(2,1)S(1)} %get-tuple-element.73), channel_id=1, source_target_pairs={{0,4},{4,0},{8,12},{12,8},{16,20},{20,16},{24,28},{28,24},{32,36},... | collective-permute-start | bytes 393224 | tf_op jit(solution)/shard_map/ppermute | solution.py:302
  71.5 1.1 %collective-permute-start.19 = (bf16[4,128,128]{2,1,0:T(8,128)(2,1)S(1)}, bf16[4,128,128]{2,1,0:T(8,128)(2,1)S(1)}, u32[]{:S(2)}, u32[]{:S(2)}) collective-permute-start(bf16[4,128,128]{2,1,0:T(8,128)(2,1)S(1)} %get-tuple-element.74), channel_id=1, source_target_pairs={{0,8},{4,12},{8,0},{12,4},{16,24},{20,28},{24,16},{28,20},{32,40},... | collective-permute-start | bytes 393224 | tf_op jit(solution)/shard_map/ppermute | solution.py:302
  72.6 0.6 collective-permute-start.20
  73.2 1.3 %collective-permute-start.21 = (bf16[4,128,128]{2,1,0:T(8,128)(2,1)S(1)}, bf16[4,128,128]{2,1,0:T(8,128)(2,1)S(1)}, u32[]{:S(2)}, u32[]{:S(2)}) collective-permute-start(bf16[4,128,128]{2,1,0:T(8,128)(2,1)S(1)} %get-tuple-element.76), channel_id=1, source_target_pairs={{0,16},{4,20},{8,24},{12,28},{16,0},{20,4},{24,8},{28,12},{32,48},... | collective-permute-start | bytes 393224 | tf_op jit(solution)/shard_map/ppermute | solution.py:302
  74.5 2.0 %collective-permute-start.22 = (bf16[4,128,128]{2,1,0:T(8,128)(2,1)S(1)}, bf16[4,128,128]{2,1,0:T(8,128)(2,1)S(1)}, u32[]{:S(2)}, u32[]{:S(2)}) collective-permute-start(bf16[4,128,128]{2,1,0:T(8,128)(2,1)S(1)} %get-tuple-element.77), channel_id=1, source_target_pairs={{0,20},{4,16},{8,28},{12,24},{16,4},{20,0},{24,12},{28,8},{32,52},... | collective-permute-start | bytes 393224 | tf_op jit(solution)/shard_map/ppermute | solution.py:302
  76.5 0.7 collective-permute-start.23
  77.3 2.2 %collective-permute-start.24 = (bf16[4,128,128]{2,1,0:T(8,128)(2,1)S(1)}, bf16[4,128,128]{2,1,0:T(8,128)(2,1)S(1)}, u32[]{:S(2)}, u32[]{:S(2)}) collective-permute-start(bf16[4,128,128]{2,1,0:T(8,128)(2,1)S(1)} %get-tuple-element.79), channel_id=1, source_target_pairs={{0,28},{4,24},{8,20},{12,16},{16,12},{20,8},{24,4},{28,0},{32,60},... | collective-permute-start | bytes 393224 | tf_op jit(solution)/shard_map/ppermute | solution.py:302
  79.5 0.6 collective-permute-done.20.refs_3_
  80.0 2.6 %collective-permute-done.21.refs_4_ = bf16[4,128,128]{2,1,0:T(8,128)(2,1)S(1)} collective-permute-done((bf16[4,128,128]{2,1,0:T(8,128)(2,1)S(1)}, bf16[4,128,128]{2,1,0:T(8,128)(2,1)S(1)}, u32[]{:S(2)}, u32[]{:S(2)}) %collective-permute-start.21) | collective-permute-done | bytes 131104 | tf_op jit(solution)/shard_map/ppermute | solution.py:302
  82.7 3.1 %collective-permute-done.22.refs_5_ = bf16[4,128,128]{2,1,0:T(8,128)(2,1)S(1)} collective-permute-done((bf16[4,128,128]{2,1,0:T(8,128)(2,1)S(1)}, bf16[4,128,128]{2,1,0:T(8,128)(2,1)S(1)}, u32[]{:S(2)}, u32[]{:S(2)}) %collective-permute-start.22) | collective-permute-done | bytes 131104 | tf_op jit(solution)/shard_map/ppermute | solution.py:302
  85.7 2.6 %collective-permute-done.23.refs_6_ = bf16[4,128,128]{2,1,0:T(8,128)(2,1)S(1)} collective-permute-done((bf16[4,128,128]{2,1,0:T(8,128)(2,1)S(1)}, bf16[4,128,128]{2,1,0:T(8,128)(2,1)S(1)}, u32[]{:S(2)}, u32[]{:S(2)}) %collective-permute-start.23) | collective-permute-done | bytes 131104 | tf_op jit(solution)/shard_map/ppermute | solution.py:302
  88.3 2.8 %collective-permute-done.24.refs_7_ = bf16[4,128,128]{2,1,0:T(8,128)(2,1)S(1)} collective-permute-done((bf16[4,128,128]{2,1,0:T(8,128)(2,1)S(1)}, bf16[4,128,128]{2,1,0:T(8,128)(2,1)S(1)}, u32[]{:S(2)}, u32[]{:S(2)}) %collective-permute-start.24) | collective-permute-done | bytes 131104 | tf_op jit(solution)/shard_map/ppermute | solution.py:302
  91.1 1.3 %shard_map.89 = (bf16[128,1024]{1,0:T(8,128)(2,1)}, bf16[128,1024]{1,0:T(8,128)(2,1)}, bf16[128,1024]{1,0:T(8,128)(2,1)}, bf16[128,1024]{1,0:T(8,128)(2,1)}) custom-call(bf16[4,128,128]{2,1,0:T(8,128)(2,1)S(1)} %get-tuple-element.72.refs_0_, bf16[4,128,128]{2,1,0:T(8,128)(2,1)S(1)} %collective-permute-done.18.refs_1_, ...), custom_call_target="tpu_custom_call" | custom-call | tf_op jit(solution)/shard_map/pallas_call | solution.py:370
  (23 shorter events, 0.8 us)
Async XLA Ops:
  0.6 30.4 %copy-start = (f32[1024]{0:T(1024)S(1)}, f32[1024]{0:T(1024)}, u32[]{:S(2)}) copy-start(f32[1024]{0:T(1024)} %param.8) | copy-start | bytes 12292
  0.6 1.0 %copy-start.2 = (bf16[128,1024]{1,0:T(8,128)(2,1)S(1)}, bf16[128,1024]{1,0:T(8,128)(2,1)}, u32[]{:S(2)}) copy-start(bf16[128,1024]{1,0:T(8,128)(2,1)} %q.1) | copy-start | bytes 786436
  1.6 0.9 %copy-start.3 = (bf16[128,1024]{1,0:T(8,128)(2,1)S(1)}, bf16[128,1024]{1,0:T(8,128)(2,1)}, u32[]{:S(2)}) copy-start(bf16[128,1024]{1,0:T(8,128)(2,1)} %k.1) | copy-start | bytes 786436
  2.6 0.9 %copy-start.4 = (bf16[128,1024]{1,0:T(8,128)(2,1)S(1)}, bf16[128,1024]{1,0:T(8,128)(2,1)}, u32[]{:S(2)}) copy-start(bf16[128,1024]{1,0:T(8,128)(2,1)} %v.1) | copy-start | bytes 786436
  3.5 0.9 %copy-start.5 = (bf16[128,1024]{1,0:T(8,128)(2,1)S(1)}, bf16[128,1024]{1,0:T(8,128)(2,1)}, u32[]{:S(2)}) copy-start(bf16[128,1024]{1,0:T(8,128)(2,1)} %d.1) | copy-start | bytes 786436
  4.7 5.8 %collective-permute-start = (bf16[4,128,128]{2,1,0:T(8,128)(2,1)S(1)}, bf16[4,128,128]{2,1,0:T(8,128)(2,1)S(1)}, u32[]{:S(2)}, u32[]{:S(2)}) collective-permute-start(bf16[4,128,128]{2,1,0:T(8,128)(2,1)S(1)} %get-tuple-element.43), channel_id=1, source_target_pairs={{0,4},{4,0},{8,12},{12,8},{16,20},{20,16},{24,28},{28,24},{32,36},... | collective-permute-start | bytes 393224 | tf_op jit(solution)/shard_map/ppermute | solution.py:302
  5.5 7.5 %collective-permute-start.1 = (bf16[4,128,128]{2,1,0:T(8,128)(2,1)S(1)}, bf16[4,128,128]{2,1,0:T(8,128)(2,1)S(1)}, u32[]{:S(2)}, u32[]{:S(2)}) collective-permute-start(bf16[4,128,128]{2,1,0:T(8,128)(2,1)S(1)} %get-tuple-element.44), channel_id=1, source_target_pairs={{0,8},{4,12},{8,0},{12,4},{16,24},{20,28},{24,16},{28,20},{32,40},... | collective-permute-start | bytes 393224 | tf_op jit(solution)/shard_map/ppermute | solution.py:302
  6.7 7.5 %collective-permute-start.2 = (bf16[4,128,128]{2,1,0:T(8,128)(2,1)S(1)}, bf16[4,128,128]{2,1,0:T(8,128)(2,1)S(1)}, u32[]{:S(2)}, u32[]{:S(2)}) collective-permute-start(bf16[4,128,128]{2,1,0:T(8,128)(2,1)S(1)} %get-tuple-element.45), channel_id=1, source_target_pairs={{0,12},{4,8},{8,4},{12,0},{16,28},{20,24},{24,20},{28,16},{32,44},... | collective-permute-start | bytes 393224 | tf_op jit(solution)/shard_map/ppermute | solution.py:302
  7.2 11.2 %collective-permute-start.3 = (bf16[4,128,128]{2,1,0:T(8,128)(2,1)S(1)}, bf16[4,128,128]{2,1,0:T(8,128)(2,1)S(1)}, u32[]{:S(2)}, u32[]{:S(2)}) collective-permute-start(bf16[4,128,128]{2,1,0:T(8,128)(2,1)S(1)} %get-tuple-element.46), channel_id=1, source_target_pairs={{0,16},{4,20},{8,24},{12,28},{16,0},{20,4},{24,8},{28,12},{32,48},... | collective-permute-start | bytes 393224 | tf_op jit(solution)/shard_map/ppermute | solution.py:302
  10.0 11.5 %collective-permute-start.4 = (bf16[4,128,128]{2,1,0:T(8,128)(2,1)S(1)}, bf16[4,128,128]{2,1,0:T(8,128)(2,1)S(1)}, u32[]{:S(2)}, u32[]{:S(2)}) collective-permute-start(bf16[4,128,128]{2,1,0:T(8,128)(2,1)S(1)} %get-tuple-element.47), channel_id=1, source_target_pairs={{0,20},{4,16},{8,28},{12,24},{16,4},{20,0},{24,12},{28,8},{32,52},... | collective-permute-start | bytes 393224 | tf_op jit(solution)/shard_map/ppermute | solution.py:302
  10.5 11.9 %collective-permute-start.5 = (bf16[4,128,128]{2,1,0:T(8,128)(2,1)S(1)}, bf16[4,128,128]{2,1,0:T(8,128)(2,1)S(1)}, u32[]{:S(2)}, u32[]{:S(2)}) collective-permute-start(bf16[4,128,128]{2,1,0:T(8,128)(2,1)S(1)} %get-tuple-element.48), channel_id=1, source_target_pairs={{0,24},{4,28},{8,16},{12,20},{16,8},{20,12},{24,0},{28,4},{32,56},... | collective-permute-start | bytes 393224 | tf_op jit(solution)/shard_map/ppermute | solution.py:302
  13.0 12.4 %collective-permute-start.6 = (bf16[4,128,128]{2,1,0:T(8,128)(2,1)S(1)}, bf16[4,128,128]{2,1,0:T(8,128)(2,1)S(1)}, u32[]{:S(2)}, u32[]{:S(2)}) collective-permute-start(bf16[4,128,128]{2,1,0:T(8,128)(2,1)S(1)} %get-tuple-element.49), channel_id=1, source_target_pairs={{0,28},{4,24},{8,20},{12,16},{16,12},{20,8},{24,4},{28,0},{32,60},... | collective-permute-start | bytes 393224 | tf_op jit(solution)/shard_map/ppermute | solution.py:302
  25.8 7.3 %collective-permute-start.7 = (bf16[4,128,128]{2,1,0:T(8,128)(2,1)S(1)}, bf16[4,128,128]{2,1,0:T(8,128)(2,1)S(1)}, u32[]{:S(2)}, u32[]{:S(2)}) collective-permute-start(bf16[4,128,128]{2,1,0:T(8,128)(2,1)S(1)} %get-tuple-element.57), channel_id=1, source_target_pairs={{0,32},{4,36},{8,40},{12,44},{16,48},{20,52},{24,56},{28,60},{32,0... | collective-permute-start | bytes 393224 | tf_op jit(solution)/shard_map/ppermute | solution.py:302
  27.1 5.9 %collective-permute-start.8 = (bf16[2,128,128]{2,1,0:T(8,128)(2,1)S(1)}, bf16[2,128,128]{2,1,0:T(8,128)(2,1)S(1)}, u32[]{:S(2)}, u32[]{:S(2)}) collective-permute-start(bf16[2,128,128]{2,1,0:T(8,128)(2,1)S(1)} %get-tuple-element.58), channel_id=1, source_target_pairs={{32,64},{36,68},{40,72},{44,76},{48,80},{52,84},{56,88},{60,92},{9... | collective-permute-start | bytes 196616 | tf_op jit(solution)/shard_map/ppermute | solution.py:302
  38.0 1.0 %copy-start.1 = (f32[2,1024,128]{2,1,0:T(8,128)}, f32[2,1024,128]{2,1,0:T(8,128)S(1)}, u32[]{:S(2)}) copy-start(f32[2,1024,128]{2,1,0:T(8,128)S(1)} %get-tuple-element.63.refs_17_) | copy-start | bytes 3145732
  39.0 1.9 %collective-permute-start.9 = (f32[2,8,128]{2,1,0:T(8,128)S(1)}, f32[2,8,128]{2,1,0:T(8,128)S(1)}, u32[]{:S(2)}, u32[]{:S(2)}) collective-permute-start(f32[2,8,128]{2,1,0:T(8,128)S(1)} %get-tuple-element.59), channel_id=1, source_target_pairs={{0,4},{4,0},{8,12},{12,8},{16,20},{20,16},{24,28},{28,24},{32,36},... | collective-permute-start | bytes 24584 | tf_op jit(solution)/shard_map/ppermute | solution.py:302
  40.9 3.4 %collective-permute-start.12 = (f32[2,8,128]{2,1,0:T(8,128)S(1)}, f32[2,8,128]{2,1,0:T(8,128)S(1)}, u32[]{:S(2)}, u32[]{:S(2)}) collective-permute-start(f32[2,8,128]{2,1,0:T(8,128)S(1)} %add.21), channel_id=1, source_target_pairs={{0,8},{4,12},{8,0},{12,4},{16,24},{20,28},{24,16},{28,20},{32,40},... | collective-permute-start | bytes 24584 | tf_op jit(solution)/shard_map/ppermute | solution.py:302
  40.9 3.7 %collective-permute-start.11 = (f32[2,8,128]{2,1,0:T(8,128)S(1)}, f32[2,8,128]{2,1,0:T(8,128)S(1)}, u32[]{:S(2)}, u32[]{:S(2)}) collective-permute-start(f32[2,8,128]{2,1,0:T(8,128)S(1)} %add.21), channel_id=1, source_target_pairs={{0,24},{4,28},{8,16},{12,20},{16,8},{20,12},{24,0},{28,4},{32,56},... | collective-permute-start | bytes 24584 | tf_op jit(solution)/shard_map/ppermute | solution.py:302
  43.1 4.0 %collective-permute-start.10 = (f32[2,8,128]{2,1,0:T(8,128)S(1)}, f32[2,8,128]{2,1,0:T(8,128)S(1)}, u32[]{:S(2)}, u32[]{:S(2)}) collective-permute-start(f32[2,8,128]{2,1,0:T(8,128)S(1)} %add.21), channel_id=1, source_target_pairs={{0,16},{4,20},{8,24},{12,28},{16,0},{20,4},{24,8},{28,12},{32,48},... | collective-permute-start | bytes 24584 | tf_op jit(solution)/shard_map/ppermute | solution.py:302
  47.1 3.9 %collective-permute-start.15 = (f32[2,8,128]{2,1,0:T(8,128)S(1)}, f32[2,8,128]{2,1,0:T(8,128)S(1)}, u32[]{:S(2)}, u32[]{:S(2)}) collective-permute-start(f32[2,8,128]{2,1,0:T(8,128)S(1)} %add_add_fusion.refs_0_), channel_id=1, source_target_pairs={{0,1},{1,0},{2,3},{3,2},{4,5},{5,4},{6,7},{7,6},{8,9},{9,8},{10,11... | collective-permute-start | bytes 24584 | tf_op jit(solution)/shard_map/ppermute | solution.py:353
  48.4 3.7 %collective-permute-start.14 = (f32[2,8,128]{2,1,0:T(8,128)S(1)}, f32[2,8,128]{2,1,0:T(8,128)S(1)}, u32[]{:S(2)}, u32[]{:S(2)}) collective-permute-start(f32[2,8,128]{2,1,0:T(8,128)S(1)} %add_add_fusion.refs_0_), channel_id=1, source_target_pairs={{0,3},{1,2},{2,1},{3,0},{4,7},{5,6},{6,5},{7,4},{8,11},{9,10},{10,... | collective-permute-start | bytes 24584 | tf_op jit(solution)/shard_map/ppermute | solution.py:353
  50.3 4.1 %collective-permute-start.13 = (f32[2,8,128]{2,1,0:T(8,128)S(1)}, f32[2,8,128]{2,1,0:T(8,128)S(1)}, u32[]{:S(2)}, u32[]{:S(2)}) collective-permute-start(f32[2,8,128]{2,1,0:T(8,128)S(1)} %add_add_fusion.refs_0_), channel_id=1, source_target_pairs={{0,2},{1,3},{2,0},{3,1},{4,6},{5,7},{6,4},{7,5},{8,10},{9,11},{10,... | collective-permute-start | bytes 24584 | tf_op jit(solution)/shard_map/ppermute | solution.py:353
  59.1 7.5 %collective-permute-start.16 = (bf16[4,128,128]{2,1,0:T(8,128)(2,1)S(1)}, bf16[4,128,128]{2,1,0:T(8,128)(2,1)S(1)}, u32[]{:S(2)}, u32[]{:S(2)}) collective-permute-start(bf16[4,128,128]{2,1,0:T(8,128)(2,1)S(1)} %get-tuple-element.70), channel_id=1, source_target_pairs={{0,32},{4,36},{8,40},{12,44},{16,48},{20,52},{24,56},{28,60},{32,0... | collective-permute-start | bytes 393224 | tf_op jit(solution)/shard_map/ppermute | solution.py:302
  59.2 7.4 %collective-permute-start.17 = (bf16[2,128,128]{2,1,0:T(8,128)(2,1)S(1)}, bf16[2,128,128]{2,1,0:T(8,128)(2,1)S(1)}, u32[]{:S(2)}, u32[]{:S(2)}) collective-permute-start(bf16[2,128,128]{2,1,0:T(8,128)(2,1)S(1)} %get-tuple-element.71), channel_id=1, source_target_pairs={{32,64},{36,68},{40,72},{44,76},{48,80},{52,84},{56,88},{60,92},{9... | collective-permute-start | bytes 196616 | tf_op jit(solution)/shard_map/ppermute | solution.py:302
  67.1 9.4 %collective-permute-start.18 = (bf16[4,128,128]{2,1,0:T(8,128)(2,1)S(1)}, bf16[4,128,128]{2,1,0:T(8,128)(2,1)S(1)}, u32[]{:S(2)}, u32[]{:S(2)}) collective-permute-start(bf16[4,128,128]{2,1,0:T(8,128)(2,1)S(1)} %get-tuple-element.73), channel_id=1, source_target_pairs={{0,4},{4,0},{8,12},{12,8},{16,20},{20,16},{24,28},{28,24},{32,36},... | collective-permute-start | bytes 393224 | tf_op jit(solution)/shard_map/ppermute | solution.py:302
  71.5 5.8 %collective-permute-start.19 = (bf16[4,128,128]{2,1,0:T(8,128)(2,1)S(1)}, bf16[4,128,128]{2,1,0:T(8,128)(2,1)S(1)}, u32[]{:S(2)}, u32[]{:S(2)}) collective-permute-start(bf16[4,128,128]{2,1,0:T(8,128)(2,1)S(1)} %get-tuple-element.74), channel_id=1, source_target_pairs={{0,8},{4,12},{8,0},{12,4},{16,24},{20,28},{24,16},{28,20},{32,40},... | collective-permute-start | bytes 393224 | tf_op jit(solution)/shard_map/ppermute | solution.py:302
  72.6 7.4 %collective-permute-start.20 = (bf16[4,128,128]{2,1,0:T(8,128)(2,1)S(1)}, bf16[4,128,128]{2,1,0:T(8,128)(2,1)S(1)}, u32[]{:S(2)}, u32[]{:S(2)}) collective-permute-start(bf16[4,128,128]{2,1,0:T(8,128)(2,1)S(1)} %get-tuple-element.75), channel_id=1, source_target_pairs={{0,12},{4,8},{8,4},{12,0},{16,28},{20,24},{24,20},{28,16},{32,44},... | collective-permute-start | bytes 393224 | tf_op jit(solution)/shard_map/ppermute | solution.py:302
  73.2 9.4 %collective-permute-start.21 = (bf16[4,128,128]{2,1,0:T(8,128)(2,1)S(1)}, bf16[4,128,128]{2,1,0:T(8,128)(2,1)S(1)}, u32[]{:S(2)}, u32[]{:S(2)}) collective-permute-start(bf16[4,128,128]{2,1,0:T(8,128)(2,1)S(1)} %get-tuple-element.76), channel_id=1, source_target_pairs={{0,16},{4,20},{8,24},{12,28},{16,0},{20,4},{24,8},{28,12},{32,48},... | collective-permute-start | bytes 393224 | tf_op jit(solution)/shard_map/ppermute | solution.py:302
  74.5 11.2 %collective-permute-start.22 = (bf16[4,128,128]{2,1,0:T(8,128)(2,1)S(1)}, bf16[4,128,128]{2,1,0:T(8,128)(2,1)S(1)}, u32[]{:S(2)}, u32[]{:S(2)}) collective-permute-start(bf16[4,128,128]{2,1,0:T(8,128)(2,1)S(1)} %get-tuple-element.77), channel_id=1, source_target_pairs={{0,20},{4,16},{8,28},{12,24},{16,4},{20,0},{24,12},{28,8},{32,52},... | collective-permute-start | bytes 393224 | tf_op jit(solution)/shard_map/ppermute | solution.py:302
  76.5 11.8 %collective-permute-start.23 = (bf16[4,128,128]{2,1,0:T(8,128)(2,1)S(1)}, bf16[4,128,128]{2,1,0:T(8,128)(2,1)S(1)}, u32[]{:S(2)}, u32[]{:S(2)}) collective-permute-start(bf16[4,128,128]{2,1,0:T(8,128)(2,1)S(1)} %get-tuple-element.78), channel_id=1, source_target_pairs={{0,24},{4,28},{8,16},{12,20},{16,8},{20,12},{24,0},{28,4},{32,56},... | collective-permute-start | bytes 393224 | tf_op jit(solution)/shard_map/ppermute | solution.py:302
  77.3 13.8 %collective-permute-start.24 = (bf16[4,128,128]{2,1,0:T(8,128)(2,1)S(1)}, bf16[4,128,128]{2,1,0:T(8,128)(2,1)S(1)}, u32[]{:S(2)}, u32[]{:S(2)}) collective-permute-start(bf16[4,128,128]{2,1,0:T(8,128)(2,1)S(1)} %get-tuple-element.79), channel_id=1, source_target_pairs={{0,28},{4,24},{8,20},{12,16},{16,12},{20,8},{24,4},{28,0},{32,60},... | collective-permute-start | bytes 393224 | tf_op jit(solution)/shard_map/ppermute | solution.py:302

commit v2 on v1

v2 whole, which is shorter than its diff:
```python
import math

import jax
import jax.numpy as jnp
from jax import lax
from jax.experimental import pallas as pl
from jax.experimental.pallas import tpu as pltpu
from jax.sharding import Mesh, PartitionSpec as P

DH = 128
BLOCK = 128
GROUP = 8
CHIPS = 4
HALF = CHIPS * 128
MID = GROUP - 2
TOKENS = GROUP * BLOCK
COARSE = TOKENS // 2 + TOKENS // 4 + TOKENS // 8
START = {1: 0, 2: TOKENS // 2, 3: TOKENS // 2 + TOKENS // 4}
EPS = 1e-06
FLOOR = -1e30
FLOPS = 4 * 10**9
SCALE = 1.0 / math.sqrt(DH)
VMEM = pl.BlockSpec(memory_space=pltpu.VMEM)
HBM = pl.BlockSpec(memory_space=pltpu.HBM)
F32 = jnp.float32
BF16 = jnp.bfloat16


def call(kernel, outs, ins, scratch=(), flops=0, vmem=16):
    return pl.pallas_call(
        kernel,
        out_shape=[jax.ShapeDtypeStruct(*out[:2]) for out in outs],
        in_specs=[VMEM] * ins if isinstance(ins, int) else ins,
        out_specs=[out[2] if len(out) > 2 else VMEM for out in outs],
        scratch_shapes=[pltpu.VMEM(*one) if isinstance(one, tuple) else one for one in scratch],
        compiler_params=pltpu.CompilerParams(vmem_limit_bytes=vmem * 1024 * 1024),
        cost_estimate=pl.CostEstimate(flops=flops, bytes_accessed=0, transcendentals=0),
    )


def run_all(copies):
    for copy in copies:
        copy.start()
    for copy in copies:
        copy.wait()


def at_block(b):
    return pl.ds(pl.multiple_of(b * BLOCK, BLOCK), BLOCK)


def rows(b, n=1):
    return pl.ds(b * BLOCK, n * BLOCK)


def nt(a, b):
    return lax.dot_general(a, b, (((1,), (1,)), ((), ())), preferred_element_type=F32)


def nn(a, b):
    return lax.dot_general(a, b, (((1,), (0,)), ((), ())), preferred_element_type=F32)


def tn(a, b):
    return lax.dot_general(a, b, (((0,), (0,)), ((), ())), preferred_element_type=F32)


def pack_kernel(x, y, got_x, got_y, *messages):
    core, chip = lax.axis_index("c"), lax.axis_index("x")
    mine, theirs = at_block(core), at_block(1 - core)
    for step, message in enumerate(messages):
        here = (chip ^ step) * DH
        cols = pl.ds(pl.multiple_of(core * HALF + here, DH), DH)
        for i, (own, got) in enumerate(((x, got_x), (y, got_y))):
            message[i, mine, :] = own[:, pl.ds(pl.multiple_of(here, DH), DH)]
            message[i, theirs, :] = got[:, cols]


def places():
    chip = lax.axis_index("x")
    return [pl.ds(pl.multiple_of((chip ^ step) * 2 * BLOCK, BLOCK), 2 * BLOCK) for step in range(CHIPS)]


def pool(x, p, f32):
    f32[...] = x[...].astype(F32)
    n = TOKENS
    for level in (1, 2, 3):
        n //= 2
        pooled = f32[pl.ds(0, n, 2), :] + f32[pl.ds(1, n, 2), :]
        p[pl.ds(START[level], n), :] = (pooled * 0.5**level).astype(BF16)
        f32[pl.ds(0, n), :] = pooled


def keys_kernel(*refs):
    parts, (k, v, kp, vp, pair, other, f32) = refs[:CHIPS], refs[CHIPS:]
    odd = lax.rem(lax.axis_index("z"), 2)
    for part, at in zip(parts, places()):
        k[at, :] = part[0]
        v[at, :] = part[1]
    pool(k, kp, f32)
    pool(v, vp, f32)
    near, far = at_block((1 - odd) * (GROUP - 1)), at_block(odd * (GROUP - 1))
    pair[0] = k[near, :]
    pair[1] = v[near, :]
    pair[2] = kp[pl.ds(START[3], BLOCK), :]
    pair[3] = vp[pl.ds(START[3], BLOCK), :]
    other[0] = k[far, :]
    other[1] = v[far, :]


def queries_kernel(*refs):
    parts, (q, d, qp, f32) = refs[:CHIPS], refs[CHIPS:]
    for part, at in zip(parts, places()):
        q[at, :] = part[0]
        d[at, :] = part[1]
    pool(q, qp, f32)


def spread(scratch, x, n, times=2):
    for j in range(times):
        scratch[pl.ds(j, n, times), :] = x
    return scratch[pl.ds(0, n * times), :]


def row_sum(x):
    ones = jnp.ones((8, DH), BF16)
    high = x.astype(BF16)
    low = (x - high.astype(F32)).astype(BF16)
    return (nt(ones, high) + nt(ones, low))[:1]


def attend(queries, keys, values, at, tops, totals, sums, invalid=None):
    scores = nt(queries, keys) * SCALE
    if invalid is not None:
        side, bad = invalid
        lane = lax.broadcasted_iota(jnp.int32, scores.shape, 1) // BLOCK
        scores = jnp.where((lane == side) & bad, FLOOR, scores)
    top = jnp.max(scores, axis=1, keepdims=True)
    weights = jnp.exp(scores - top)
    rounded = weights.astype(BF16)
    tops[at, :] = jnp.broadcast_to(top, (BLOCK, DH))
    totals[at, :] = jnp.broadcast_to(jnp.sum(weights, axis=1, keepdims=True), (BLOCK, DH))
    sums[at, :] = nn(rounded, values)
    return rounded


def forward_inner_kernel(q, k, v, qp, kp, vp, w_mid, w_coarse, tops, totals, sums):
    for b in range(MID):
        w_mid[rows(b), :] = attend(
            q[rows(b + 1), :], k[rows(b, 3), :], v[rows(b, 3), :], rows(b), tops, totals, sums
        )
    for c in range(6):
        w_coarse[rows(c), :] = attend(
            qp[rows(c), :], kp[rows(c ^ 1), :], vp[rows(c ^ 1), :], rows(MID + c), tops, totals, sums
        )


def forward_edge_kernel(
    q, k, v, d, qp, pair, other, gain, tops, totals, sums,
    attn, stats, w_edge, w_top, share, share1, share2, edge_k, edge_v,
    e_tops, e_totals, e_sums, up_m, up_t, up_s,
):
    z = lax.axis_index("z")
    odd = lax.rem(z, 2) == 1
    for x, edge, i in ((k, edge_k, 0), (v, edge_v, 1)):
        edge[0, rows(0), :] = jnp.where(odd, pair[i], other[i])
        edge[0, rows(1, 2), :] = x[rows(0, 2), :]
        edge[1, rows(0, 2), :] = x[rows(GROUP - 2, 2), :]
        edge[1, rows(2), :] = jnp.where(odd, other[i], pair[i])
    last = z == lax.axis_size("z") - 1
    for e, (b, invalid) in enumerate(((0, (0, z == 0)), (GROUP - 1, (2, last)))):
        w_edge[rows(e), :] = attend(
            q[rows(b), :], edge_k[e], edge_v[e], rows(e), e_tops, e_totals, e_sums, invalid
        )
    top3 = rows(2)
    w_top[...] = attend(qp[rows(6), :], pair[2], pair[3], top3, e_tops, e_totals, e_sums)
    m, t, s = e_tops[top3, :], e_totals[top3, :] * 8.0, e_sums[top3, :] * 8.0
    n = TOKENS // 8
    for level, out in ((2, share2), (1, share1)):
        em, et, es = spread(up_m, m, n), spread(up_t, t, n), spread(up_s, s, n)
        n *= 2
        at = pl.ds(MID * BLOCK + START[level], n)
        own = tops[at, :]
        m = jnp.maximum(own, em)
        here = 2.0**level * jnp.exp(own - m)
        up = jnp.exp(em - m)
        t = here * totals[at, :] + up * et
        s = here * sums[at, :] + up * es
        out[0] = here
        out[1] = up
    spread(up_m, m, n), spread(up_t, t, n), spread(up_s, s, n)
    for b in range(GROUP):
        if b in (0, GROUP - 1):
            at, (mm, tt, ss) = rows(b // (GROUP - 1)), (e_tops, e_totals, e_sums)
        else:
            at, (mm, tt, ss) = rows(b - 1), (tops, totals, sums)
        own, em = mm[at, :], up_m[rows(b), :]
        m = jnp.maximum(own, em)
        here, up = jnp.exp(own - m), jnp.exp(em - m)
        inverse = 1.0 / (here * tt[at, :] + up * up_t[rows(b), :])
        here, up = here * inverse, up * inverse
        rounded = (here * ss[at, :] + up * up_s[rows(b), :]).astype(BF16)
        share[0, rows(b), :] = here
        share[1, rows(b), :] = up
        attn[rows(b), :] = rounded
        flat = rounded.astype(F32)
        scaled = d[rows(b), :].astype(F32) * gain[...]
        sums_here = jnp.concatenate([row_sum(flat * flat), row_sum(scaled * flat)], axis=0)
        stats[:, :, pl.ds(b, 1), :] = jnp.broadcast_to(
            sums_here.reshape(1, 2, 1, BLOCK), (stats.shape[0], 2, 1, BLOCK)
        )


def slope_of(grad, values, weights, offset):
    pressure = nt(grad, values)
    wide = jnp.concatenate([offset] * (values.shape[0] // BLOCK), axis=1)
    return (weights.astype(F32) * (pressure - wide)).astype(BF16)


def backward_edge_kernel(
    features,
    stats, d, gain, attn, share, share1, share2, q, qp, pair, edge_k, edge_v, w_edge, w_top,
    out, pair_out, other_out, g0, gc, off0, offc, sl_edge, q_edge, q_top,
    buf, buf2,
):
    odd = lax.rem(lax.axis_index("z"), 2) == 1
    sums = jnp.sum(stats[...], axis=0) * (1.0 / features)
    inv_row = lax.rsqrt(sums[0] + EPS)
    drop_row = inv_row * inv_row * inv_row * sums[1]
    for b in range(GROUP):
        inv = jnp.broadcast_to(inv_row[b : b + 1], (BLOCK, DH)).T
        drop = jnp.broadcast_to(drop_row[b : b + 1], (BLOCK, DH)).T
        flat = attn[rows(b), :].astype(F32)
        out[rows(b), :] = (flat * (inv * gain[...])).astype(BF16)
        scaled = d[rows(b), :].astype(F32) * gain[...]
        grad = (inv * scaled - flat * drop).astype(BF16).astype(F32)
        dot = jnp.broadcast_to(jnp.sum(grad * flat, axis=1, keepdims=True), (BLOCK, DH))
        here, up = share[0, rows(b), :], share[1, rows(b), :]
        g0[rows(b), :] = (here * grad).astype(BF16)
        off0[rows(b), :] = here * dot
        buf[rows(b), :] = up * grad
        buf2[rows(b), :] = up * dot
    n = TOKENS
    for level, sh in ((1, share1), (2, share2), (3, None)):
        n //= 2
        g = buf[pl.ds(0, n, 2), :] + buf[pl.ds(1, n, 2), :]
        o = buf2[pl.ds(0, n, 2), :] + buf2[pl.ds(1, n, 2), :]
        at = pl.ds(START[level], n)
        if sh is None:
            gc[at, :] = (g * 8.0).astype(BF16)
            offc[at, :] = o * 8.0
        else:
            here, up = sh[0], sh[1]
            gc[at, :] = (g * here).astype(BF16)
            offc[at, :] = o * here
            buf[pl.ds(0, n), :] = g * up
            buf2[pl.ds(0, n), :] = o * up
    edges = []
    for e, b in ((0, 0), (1, GROUP - 1)):
        grad = g0[rows(b), :]
        slope = slope_of(grad, edge_v[e], w_edge[rows(e), :], off0[rows(b), :])
        sl_edge[rows(e), :] = slope
        q_edge[rows(e), :] = nn(slope, edge_k[e]) * SCALE
        side = slice(2 * e * BLOCK, (2 * e + 1) * BLOCK)
        edges.append((
            (tn(slope[:, side], q[rows(b), :]) * SCALE).astype(BF16),
            tn(w_edge[rows(e), side], grad).astype(BF16),
        ))
    grad = gc[rows(6), :]
    slope = slope_of(grad, pair[3], w_top[...], offc[rows(6), :])
    q_top[...] = nn(slope, pair[2]) * SCALE
    pair_out[2] = (tn(slope, qp[rows(6), :]) * SCALE).astype(BF16)
    pair_out[3] = tn(w_top[...], grad).astype(BF16)
    for i in range(2):
        pair_out[i] = jnp.where(odd, edges[0][i], edges[1][i])
        other_out[i] = jnp.where(odd, edges[1][i], edges[0][i])


def backward_inner_kernel(
    q, k, v, qp, kp, vp, w_mid, w_coarse, w_edge, g0, gc, off0, offc, sl_edge, q_edge, q_top,
    q_grad, k_grad, v_grad,
    sl_mid, sl_coarse, buf, grads,
):
    for c in range(6):
        slope = slope_of(gc[rows(c), :], vp[rows(c ^ 1), :], w_coarse[rows(c), :], offc[rows(c), :])
        sl_coarse[rows(c), :] = slope
        grads[rows(c), :] = nn(slope, kp[rows(c ^ 1), :]) * SCALE
    e = grads[rows(4, 2), :] * 0.25 + spread(buf, q_top[...] * 0.125, 128)
    e = grads[rows(0, 4), :] * 0.5 + spread(buf, e, 256)
    spread(buf, e, 512)
    for b in range(GROUP):
        if b in (0, GROUP - 1):
            part = q_edge[rows(b // (GROUP - 1)), :]
        else:
            slope = slope_of(
                g0[rows(b), :], v[rows(b - 1, 3), :], w_mid[rows(b - 1), :], off0[rows(b), :]
            )
            sl_mid[rows(b - 1), :] = slope
            part = nn(slope, k[rows(b - 1, 3), :]) * SCALE
        q_grad[rows(b), :] = (part + buf[rows(b), :]).astype(BF16)

    def key_value(factor, edge, mid, mid_c, right, right_c, res):
        for c in range(6):
            grads[rows(c ^ 1), :] = tn(mid_c[rows(c), :], right_c[rows(c), :])
        e = grads[rows(4, 2), :] * (0.25 * factor)
        e = grads[rows(0, 4), :] * (0.5 * factor) + spread(buf, e, 256)
        spread(buf, e, 512)
        for j in range(GROUP):
            total = None
            for side in range(3):
                b = j + 1 - side
                cols = pl.ds(side * BLOCK, BLOCK)
                if b in (0, GROUP - 1):
                    left = edge[rows(b // (GROUP - 1)), cols]
                elif 0 < b < GROUP - 1:
                    left = mid[rows(b - 1), cols]
                else:
                    continue
                part = tn(left, right[rows(b), :])
                total = part if total is None else total + part
            res[rows(j), :] = total * factor + buf[rows(j), :]

    key_value(SCALE, sl_edge, sl_mid, sl_coarse, q, qp, k_grad)
    key_value(1.0, w_edge, w_mid, w_coarse, g0, gc, v_grad)


def collect_kernel(out, q_grad, k_grad, v_grad, pair, other, *refs):
    messages, buf = refs[:-1], refs[-1]
    odd = lax.rem(lax.axis_index("z"), 2) == 1
    for i, x in enumerate((k_grad, v_grad)):
        spread(buf, pair[2 + i].astype(F32) * 0.125, 128, 8)
        buf[...] += x[...]
        buf[rows(0), :] += jnp.where(odd, pair[i], other[i]).astype(F32)
        buf[rows(GROUP - 1), :] += jnp.where(odd, other[i], pair[i]).astype(F32)
        for at, message in zip(places(), messages):
            message[2 + i] = buf[at, :].astype(BF16)
    for at, message in zip(places(), messages):
        message[0] = out[at, :]
        message[1] = q_grad[at, :]


def regroup_kernel(*refs):
    parts, (own, away) = refs[:CHIPS], refs[CHIPS:]
    core, chip = lax.axis_index("c"), lax.axis_index("x")
    mine, theirs = at_block(core), at_block(1 - core)
    for step, part in enumerate(parts):
        cols = pl.ds(pl.multiple_of((chip ^ step) * DH, DH), DH)
        for i in range(4):
            own[i, :, cols] = part[i, mine, :]
            away[i, :, cols] = part[i, theirs, :]


def finish_kernel(own, got, *refs):
    results, sem = refs[:-1], refs[-1]
    core = lax.axis_index("c")
    copies = []
    for i, x in enumerate(results):
        for j, (half, source) in enumerate(((1 - core, got), (core, own))):
            cols = pl.ds(pl.multiple_of(half * HALF, HALF), HALF)
            copies.append(pltpu.make_async_copy(source.at[i], x.at[:, cols], sem.at[j, i]))
    run_all(copies)


def swap_pair(x):
    return lax.ppermute(x, "z", [(i, i ^ 1) for i in range(lax.axis_size("z"))])


def swap_other(x):
    up = [(i, i + 1) for i in range(1, lax.axis_size("z") - 1, 2)]
    return lax.ppermute(x, "z", up + [(target, source) for source, target in up])


def swap_core(x):
    return lax.ppermute(x, "c", [(0, 1), (1, 0)])


def swap_chips(messages):
    return [messages[0]] + [
        lax.ppermute(messages[step], "x", [(i, i ^ step) for i in range(CHIPS)]) for step in (1, 2, 3)
    ]


def exchange(x, axes):
    return lax.all_to_all(x, axes, 0, 0, tiled=True)


def local(query, keys, values, gain, out_grad):
    token = ((BLOCK, query.shape[1]), BF16, HBM)
    part = ((2, 2 * BLOCK, DH), BF16)
    chip_part = ((4, 2 * BLOCK, DH), BF16)
    half = ((4, BLOCK, HALF), BF16)
    partners = GROUP * lax.axis_size("head")
    message = ((4, BLOCK, DH), BF16)
    edge = ((2, BLOCK, DH), BF16)
    whole = ((TOKENS, DH), BF16)
    whole_f = ((TOKENS, DH), F32)
    coarse = ((COARSE, DH), BF16)
    coarse_f = ((COARSE, DH), F32)
    one_f = ((BLOCK, DH), F32)
    two_f = ((2 * BLOCK, DH), F32)
    w_mids = ((MID * BLOCK, 3 * BLOCK), BF16)
    w_coarses = ((6 * BLOCK, BLOCK), BF16)
    w_edges = ((2 * BLOCK, 3 * BLOCK), BF16)
    w_tops = ((BLOCK, BLOCK), BF16)
    inner_f = (((MID + 6) * BLOCK, DH), F32)
    edge_sets = ((2, 3 * BLOCK, DH), BF16)
    shares = [((2, TOKENS >> level, DH), F32) for level in range(3)]
    features = query.shape[1] * lax.axis_size("head")

    head = lax.axis_index("c") * CHIPS + lax.axis_index("x")
    my_gain = lax.dynamic_slice_in_dim(gain, head * DH, DH).reshape(1, DH)

    def send(x, y):
        gots = [swap_core(one) for one in (x, y)]
        own = [lax.dynamic_slice_in_dim(one, lax.axis_index("c") * HALF, HALF, 1) for one in (x, y)]
        return swap_chips(call(pack_kernel, [part] * CHIPS, 4)(*own, *gots))

    got_keys = send(keys, values)
    got_queries = send(query, out_grad)
    k, v, kp, vp, pair, other = call(
        keys_kernel, [whole] * 2 + [coarse] * 2 + [message, edge], CHIPS, [whole_f]
    )(*got_keys)
    pair, other = swap_pair(pair), swap_other(other)
    q, d, qp = call(queries_kernel, [whole] * 2 + [coarse], CHIPS, [whole_f])(*got_queries)
    w_mid, w_coarse, *inner = call(
        forward_inner_kernel, [w_mids, w_coarses] + [inner_f] * 3, 6, flops=FLOPS
    )(q, k, v, qp, kp, vp)
    attn, stats, w_edge, w_top, share, share1, share2, edge_k, edge_v = call(
        forward_edge_kernel,
        [whole, ((partners, 2, GROUP, DH), F32), w_edges, w_tops] + shares + [edge_sets] * 2,
        11,
        [((3 * BLOCK, DH), F32)] * 3 + [whole_f] * 3,
    )(q, k, v, d, qp, pair, other, my_gain, *inner)
    stats = exchange(stats, ("x", "c", "head"))

    def backward_edge(*refs):
        backward_edge_kernel(features, *refs)

    out, pair_back, other_back, g0, gc, off0, offc, sl_edge, q_edge, q_top = call(
        backward_edge,
        [whole, message, edge, whole, coarse, whole_f, coarse_f, w_edges, two_f, one_f],
        14,
        [whole_f] * 2,
    )(stats, d, my_gain, attn, share, share1, share2, q, qp, pair, edge_k, edge_v, w_edge, w_top)
    pair_back, other_back = swap_pair(pair_back), swap_other(other_back)
    grads = call(
        backward_inner_kernel,
        [whole, whole_f, whole_f],
        16,
        [w_mids, w_coarses, whole_f, coarse_f],
        flops=2 * FLOPS,
    )(q, k, v, qp, kp, vp, w_mid, w_coarse, w_edge, g0, gc, off0, offc, sl_edge, q_edge, q_top)
    messages = call(collect_kernel, [chip_part] * CHIPS, 6, [whole_f])(
        out, *grads, pair_back, other_back
    )
    own, away = call(regroup_kernel, [half] * 2, CHIPS)(*swap_chips(messages))
    return call(finish_kernel, [token] * 4, 2, [pltpu.SemaphoreType.DMA((2, 4))])(own, swap_core(away))


def solution(mesh):
    chips = (CHIPS, 2)
    axes = ("z", "x", "c", "head")
    heads = mesh.shape["head"]
    fine = Mesh(mesh.devices.reshape((mesh.shape["seq"] // GROUP, *chips, heads)), axes)
    spec = P(("z", "x", "c"), "head")
    in_specs = (spec, spec, spec, P("head"), spec)
    return jax.shard_map(
        local, mesh=fine, in_specs=in_specs, out_specs=(spec,) * 4, check_vma=False
    )
```

time: 92.8 us -> 78 us (0.84); the launches traced: 92.4 us -> 76.5 us
  blocking collectives: 0 us -> 17.8 us
  starting transfers between devices: 41 us -> 25 us
  waiting for transfers between devices: 33.6 us -> 20.3 us
  local copies, waits for them, and re-layouts: 4.88 us -> 1.09 us
    all_to_all x0 -> x1, blocking collectives: none -> 17.8 us  [exchange(): return lax.all_to_all(x, axes, 0, 0, tiled=True)]
    ppermute x25 -> x18, starting transfers between devices: 41 us -> 25 us  [the longest x9 12.5 us: swap_chips(): lax.ppermute(messages[step], 'x', [(i, i ^ step) for i in range(CHIPS)])]
    ppermute x25 -> x18, waiting for transfers between devices: 33.6 us -> 20.3 us  [the longest x9 17.2 us: swap_chips(): lax.ppermute(messages[step], 'x', [(i, i ^ step) for i in range(CHIPS)])]
    unnamed x12 -> x6, local copies, waits for them, and re-layouts: 4.81 us -> 0.02 us
    dynamic_slice x0 -> x2, local copies, waits for them, and re-layouts: none -> 1 us  [send(): lax.dynamic_slice_in_dim(one, lax.axis_index('c') * HALF, HALF, 1)]
    pallas_call x6 -> x11, Pallas kernels: 12.1 us -> 11.3 us  [the longest x1 3.12 us: local(): call(forward_inner_kernel, [w_mids, w_coarses] + [inner_f] * 3, 6, flops=...]
  transfers between devices with their start and end apart: 25 -> 18, of which waited for: 16 -> 9; matrix products, arithmetic and copies ran while one was open for 0% -> 1% of each run, Pallas kernels for 0% -> 8%
where the time goes in v2:
time: 78 us; the launch traced here: 76.5 us
  starting transfers between devices  25 us (32%)
  waiting for transfers between devices  20.3 us (26%)
  blocking collectives  17.8 us (23%)
  Pallas kernels  11.3 us (14%)
  local copies, waits for them, and re-layouts  1.09 us (1%)
  between operations  0.97 us (1%)
    all_to_all x1, blocking collectives, exchange(): return lax.all_to_all(x, axes, 0, 0, tiled=True)  17.8 us
    ppermute x9, waiting for transfers between devices, swap_chips(): lax.ppermute(messages[step], 'x', [(i, i ^ step) for i in range(CHIPS)])  17.2 us
    ppermute x9, starting transfers between devices, swap_chips(): lax.ppermute(messages[step], 'x', [(i, i ^ step) for i in range(CHIPS)])  12.5 us
    ppermute x2, starting transfers between devices, swap_other(): lax.ppermute(x, 'z', up + [(target, source) for source, target in up])  8.57 us
    ppermute x5, starting transfers between devices, swap_core(): return lax.ppermute(x, 'c', [(0, 1), (1, 0)])  3.64 us
    pallas_call x1, Pallas kernels, local(): call(forward_inner_kernel, [w_mids, w_coarses] + [inner_f] * 3, 6, flops=...  3.12 us
    pallas_call x1, Pallas kernels, local(): call(backward_inner_kernel, [whole, whole_f, whole_f], 16, [w_mids, w_coa...  2.7 us
    pallas_call x1, Pallas kernels, local(): call(forward_edge_kernel, [whole, ((partners, 2, GROUP, DH), F32), w_edge...  2.02 us
  transfers between devices with their start and end apart: 18, of which 9 were waited for; matrix products, arithmetic and copies ran while one was open for 1% of the time, Pallas kernels for 8%

profile of v2, /device:TPU:33, one launch (start us, length us, event | category | flops | bytes accessed | tf_op | source)
XLA Modules:
  0.0 76.5 jit_solution(18277549111104726921)
XLA Ops:
  0.6 0.0 copy-start
  0.6 0.8 collective-permute-start.5
  1.4 0.1 collective-permute-start.6
  1.5 0.4 collective-permute-start
  1.9 0.1 collective-permute-start.1
  2.0 1.0 %constant_dynamic-slice_fusion = (bf16[128,512]{1,0:T(8,128)(2,1)S(1)}, bf16[128,512]{1,0:T(8,128)(2,1)S(1)}) fusion(bf16[128,1024]{1,0:T(8,128)(2,1)} %param.7, s32[]{:T(128)S(6)} %select_n.4, bf16[128,1024]{1,0:T(8,128)(2,1)} %param.6), kind=kLoop, calls=%fused_computation | loop fusion | bytes 524292 | tf_op jit(solution)/shard_map/dynamic_slice | solution.py:415
  3.0 0.1 collective-permute-done.6.got_y
  3.2 0.1 shard_map.86
  3.3 1.3 %collective-permute-start.7 = (bf16[2,256,128]{2,1,0:T(8,128)(2,1)S(1)}, bf16[2,256,128]{2,1,0:T(8,128)(2,1)S(1)}, u32[]{:S(2)}, u32[]{:S(2)}) collective-permute-start(bf16[2,256,128]{2,1,0:T(8,128)(2,1)S(1)} %get-tuple-element.60), channel_id=1, source_target_pairs={{0,8},{8,0},{16,24},{24,16},{1,9},{9,1},{17,25},{25,17},{2,10},{10... | collective-permute-start | bytes 393224 | tf_op jit(solution)/shard_map/ppermute | solution.py:379
  4.6 2.5 %collective-permute-start.8 = (bf16[2,256,128]{2,1,0:T(8,128)(2,1)S(1)}, bf16[2,256,128]{2,1,0:T(8,128)(2,1)S(1)}, u32[]{:S(2)}, u32[]{:S(2)}) collective-permute-start(bf16[2,256,128]{2,1,0:T(8,128)(2,1)S(1)} %get-tuple-element.61), channel_id=1, source_target_pairs={{0,16},{8,24},{16,0},{24,8},{1,17},{9,25},{17,1},{25,9},{2,18},{10... | collective-permute-start | bytes 393224 | tf_op jit(solution)/shard_map/ppermute | solution.py:379
  7.1 0.8 collective-permute-start.9
  7.9 0.0 collective-permute-done.got_x
  7.9 0.0 collective-permute-done.1.got_y
  7.9 0.1 shard_map.84
  8.0 0.1 collective-permute-start.2
  8.1 3.1 %collective-permute-start.3 = (bf16[2,256,128]{2,1,0:T(8,128)(2,1)S(1)}, bf16[2,256,128]{2,1,0:T(8,128)(2,1)S(1)}, u32[]{:S(2)}, u32[]{:S(2)}) collective-permute-start(bf16[2,256,128]{2,1,0:T(8,128)(2,1)S(1)} %get-tuple-element.56), channel_id=1, source_target_pairs={{0,16},{8,24},{16,0},{24,8},{1,17},{9,25},{17,1},{25,9},{2,18},{10... | collective-permute-start | bytes 393224 | tf_op jit(solution)/shard_map/ppermute | solution.py:379
  11.2 0.0 collective-permute-done.7.refs_1_
  11.2 0.8 collective-permute-start.4
  12.0 0.1 dynamic-slice_bitcast_fusion.gain.refs_2_
  12.0 1.1 %collective-permute-done.8.refs_2_ = bf16[2,256,128]{2,1,0:T(8,128)(2,1)S(1)} collective-permute-done((bf16[2,256,128]{2,1,0:T(8,128)(2,1)S(1)}, bf16[2,256,128]{2,1,0:T(8,128)(2,1)S(1)}, u32[]{:S(2)}, u32[]{:S(2)}) %collective-permute-start.8) | collective-permute-done | bytes 131104 | tf_op jit(solution)/shard_map/ppermute | solution.py:379
  13.1 2.6 %collective-permute-done.9.refs_3_ = bf16[2,256,128]{2,1,0:T(8,128)(2,1)S(1)} collective-permute-done((bf16[2,256,128]{2,1,0:T(8,128)(2,1)S(1)}, bf16[2,256,128]{2,1,0:T(8,128)(2,1)S(1)}, u32[]{:S(2)}, u32[]{:S(2)}) %collective-permute-start.9) | collective-permute-done | bytes 131104 | tf_op jit(solution)/shard_map/ppermute | solution.py:379
  15.7 0.3 shard_map.87
  16.0 3.5 %collective-permute-start.11 = (bf16[2,128,128]{2,1,0:T(8,128)(2,1)S(1)}, bf16[2,128,128]{2,1,0:T(8,128)(2,1)S(1)}, u32[]{:S(2)}, u32[]{:S(2)}) collective-permute-start(bf16[2,128,128]{2,1,0:T(8,128)(2,1)S(1)} %get-tuple-element.68), channel_id=1, source_target_pairs={{32,64},{96,128},{160,192},{64,32},{128,96},{192,160},{33,65},{97,... | collective-permute-start | bytes 196616 | tf_op jit(solution)/shard_map/ppermute | solution.py:370
  19.5 0.1 collective-permute-start.10
  19.6 0.0 collective-permute-done.2.refs_1_
  19.6 0.0 collective-permute-done.3.refs_2_
  19.7 1.7 %collective-permute-done.4.refs_3_ = bf16[2,256,128]{2,1,0:T(8,128)(2,1)S(1)} collective-permute-done((bf16[2,256,128]{2,1,0:T(8,128)(2,1)S(1)}, bf16[2,256,128]{2,1,0:T(8,128)(2,1)S(1)}, u32[]{:S(2)}, u32[]{:S(2)}) %collective-permute-start.4) | collective-permute-done | bytes 131104 | tf_op jit(solution)/shard_map/ppermute | solution.py:379
  21.3 0.1 shard_map.85
  21.5 3.1 %shard_map.88 = (bf16[768,384]{1,0:T(8,128)(2,1)S(1)}, bf16[768,128]{1,0:T(8,128)(2,1)S(1)}, f32[1536,128]{1,0:T(8,128)S(1)}, f32[1536,128]{1,0:T(8,128)S(1)}, f32[1536,128]{1,0:T(8,128)S(1)}) custom-call(bf16[1024,128]{1,0:T(8,128)(2,1)S(1)} %get-tuple-element.58.q.refs_7_, bf16[1024,128]{1,0:T(8,128)(2,1)S(1)} %get-tuple-element.63.k, ...), custom_call_target="tpu_custom_call" | custom-call | flops 4000000000 | tf_op jit(solution)/shard_map/pallas_call | solution.py:425
  24.6 0.0 collective-permute-done.11.other
  24.6 2.0 %shard_map.89 = (bf16[1024,128]{1,0:T(8,128)(2,1)S(1)}, f32[32,2,8,128]{3,2,1,0:T(8,128)S(1)}, bf16[256,384]{1,0:T(8,128)(2,1)S(1)}, bf16[128,128]{1,0:T(8,128)(...) custom-call(bf16[1024,128]{1,0:T(8,128)(2,1)S(1)} %get-tuple-element, ...), custom_call_target="tpu_custom_call" | custom-call | tf_op jit(solution)/shard_map/pallas_call | solution.py:428
  26.7 17.8 %all_to_all.5.refs_0_ = f32[32,2,8,128]{3,2,1,0:T(8,128)S(1)} all-to-all(f32[32,2,8,128]{3,2,1,0:T(8,128)S(1)} %get-tuple-element.74), channel_id=1, replica_groups=mesh['z'=8,'x'=4,'c'=2,'head'=4] {'x','c','head'}, dimensions={0} | all-to-all | bytes 524288 | tf_op jit(solution)/shard_map/all_to_all | solution.py:384
  44.4 1.2 %shard_map.90 = (bf16[1024,128]{1,0:T(8,128)(2,1)S(1)}, bf16[4,128,128]{2,1,0:T(8,128)(2,1)S(1)}, bf16[2,128,128]{2,1,0:T(8,128)(2,1)S(1)}, bf16[1024,128]{1,0:T...) custom-call(f32[32,2,8,128]{3,2,1,0:T(8,128)S(1)} %all_to_all.5.refs, ...), custom_call_target="tpu_custom_call" | custom-call | tf_op jit(solution)/shard_map/pallas_call | solution.py:439
  45.6 5.0 %collective-permute-start.13 = (bf16[2,128,128]{2,1,0:T(8,128)(2,1)S(1)}, bf16[2,128,128]{2,1,0:T(8,128)(2,1)S(1)}, u32[]{:S(2)}, u32[]{:S(2)}) collective-permute-start(bf16[2,128,128]{2,1,0:T(8,128)(2,1)S(1)} %get-tuple-element.97), channel_id=1, source_target_pairs={{32,64},{96,128},{160,192},{64,32},{128,96},{192,160},{33,65},{97,... | collective-permute-start | bytes 196616 | tf_op jit(solution)/shard_map/ppermute | solution.py:370
  50.7 0.3 collective-permute-start.12
  50.9 2.7 %shard_map.91 = (bf16[1024,128]{1,0:T(8,128)(2,1)S(1)}, f32[1024,128]{1,0:T(8,128)S(1)}, f32[1024,128]{1,0:T(8,128)S(1)}) custom-call(bf16[1024,128]{1,0:T(8,128)(2,1)S(1)} %get-tuple-element.58.q.refs_7_, bf16[1024,128]{1,0:T(8,128)(2,1)S(1)} %get-tuple-element.63.k, bf16[1024,128]{1,0:T(8,128)(2,1)S(1)} %get-tuple-element.64.v, ...), custom_call_target="tpu_custom_call" | custom-call | flops 8000000000 | tf_op jit(solution)/shard_map/pallas_call | solution.py:446
  53.7 1.4 %collective-permute-done.12.pair = bf16[4,128,128]{2,1,0:T(8,128)(2,1)S(1)} collective-permute-done((bf16[4,128,128]{2,1,0:T(8,128)(2,1)S(1)}, bf16[4,128,128]{2,1,0:T(8,128)(2,1)S(1)}, u32[]{:S(2)}, u32[]{:S(2)}) %collective-permute-start.12) | collective-permute-done | bytes 131104 | tf_op jit(solution)/shard_map/ppermute | solution.py:365
  55.1 0.4 shard_map.92
  55.5 0.7 collective-permute-start.14
  56.2 1.7 %collective-permute-start.15 = (bf16[4,256,128]{2,1,0:T(8,128)(2,1)S(1)}, bf16[4,256,128]{2,1,0:T(8,128)(2,1)S(1)}, u32[]{:S(2)}, u32[]{:S(2)}) collective-permute-start(bf16[4,256,128]{2,1,0:T(8,128)(2,1)S(1)} %get-tuple-element.100), channel_id=1, source_target_pairs={{0,16},{8,24},{16,0},{24,8},{1,17},{9,25},{17,1},{25,9},{2,18},{10... | collective-permute-start | bytes 786440 | tf_op jit(solution)/shard_map/ppermute | solution.py:379
  58.0 1.5 %collective-permute-start.16 = (bf16[4,256,128]{2,1,0:T(8,128)(2,1)S(1)}, bf16[4,256,128]{2,1,0:T(8,128)(2,1)S(1)}, u32[]{:S(2)}, u32[]{:S(2)}) collective-permute-start(bf16[4,256,128]{2,1,0:T(8,128)(2,1)S(1)} %get-tuple-element.101), channel_id=1, source_target_pairs={{0,24},{8,16},{16,8},{24,0},{1,25},{9,17},{17,9},{25,1},{2,26},{10... | collective-permute-start | bytes 786440 | tf_op jit(solution)/shard_map/ppermute | solution.py:379
  59.5 2.2 %collective-permute-done.14.refs_1_ = bf16[4,256,128]{2,1,0:T(8,128)(2,1)S(1)} collective-permute-done((bf16[4,256,128]{2,1,0:T(8,128)(2,1)S(1)}, bf16[4,256,128]{2,1,0:T(8,128)(2,1)S(1)}, u32[]{:S(2)}, u32[]{:S(2)}) %collective-permute-start.14) | collective-permute-done | bytes 262176 | tf_op jit(solution)/shard_map/ppermute | solution.py:379
  61.6 6.8 %collective-permute-done.15.refs_2_ = bf16[4,256,128]{2,1,0:T(8,128)(2,1)S(1)} collective-permute-done((bf16[4,256,128]{2,1,0:T(8,128)(2,1)S(1)}, bf16[4,256,128]{2,1,0:T(8,128)(2,1)S(1)}, u32[]{:S(2)}, u32[]{:S(2)}) %collective-permute-start.15) | collective-permute-done | bytes 262176 | tf_op jit(solution)/shard_map/ppermute | solution.py:379
  68.4 2.9 %collective-permute-done.16.refs_3_ = bf16[4,256,128]{2,1,0:T(8,128)(2,1)S(1)} collective-permute-done((bf16[4,256,128]{2,1,0:T(8,128)(2,1)S(1)}, bf16[4,256,128]{2,1,0:T(8,128)(2,1)S(1)}, u32[]{:S(2)}, u32[]{:S(2)}) %collective-permute-start.16) | collective-permute-done | bytes 262176 | tf_op jit(solution)/shard_map/ppermute | solution.py:379
  71.3 0.2 shard_map.93
  71.5 2.3 %collective-permute-start.17 = (bf16[4,128,512]{2,1,0:T(8,128)(2,1)S(1)}, bf16[4,128,512]{2,1,0:T(8,128)(2,1)S(1)}, u32[]{:S(2)}, u32[]{:S(2)}) collective-permute-start(bf16[4,128,512]{2,1,0:T(8,128)(2,1)S(1)} %get-tuple-element.103), channel_id=1, source_target_pairs={{0,4},{4,0},{1,5},{5,1},{2,6},{6,2},{3,7},{7,3},{8,12},{12,8},{9,1... | collective-permute-start | bytes 1572872 | tf_op jit(solution)/shard_map/ppermute | solution.py:374
  73.8 1.5 %collective-permute-done.17.got = bf16[4,128,512]{2,1,0:T(8,128)(2,1)S(1)} collective-permute-done((bf16[4,128,512]{2,1,0:T(8,128)(2,1)S(1)}, bf16[4,128,512]{2,1,0:T(8,128)(2,1)S(1)}, u32[]{:S(2)}, u32[]{:S(2)}) %collective-permute-start.17) | collective-permute-done | bytes 524320 | tf_op jit(solution)/shard_map/ppermute | solution.py:374
  75.3 1.0 %shard_map.94 = (bf16[128,1024]{1,0:T(8,128)(2,1)}, bf16[128,1024]{1,0:T(8,128)(2,1)}, bf16[128,1024]{1,0:T(8,128)(2,1)}, bf16[128,1024]{1,0:T(8,128)(2,1)}) custom-call(bf16[4,128,512]{2,1,0:T(8,128)(2,1)S(1)} %get-tuple-element.102.own, bf16[4,128,512]{2,1,0:T(8,128)(2,1)S(1)} %collective-permute-done.17.got), custom_call_target="tpu_custom_call" | custom-call | tf_op jit(solution)/shard_map/pallas_call | solution.py:457
  (9 shorter events, 0.0 us)
Async XLA Ops:
  0.6 11.3 %copy-start = (f32[1024]{0:T(1024)S(1)}, f32[1024]{0:T(1024)}, u32[]{:S(2)}) copy-start(f32[1024]{0:T(1024)} %param.8) | copy-start | bytes 12292
  0.6 2.4 %collective-permute-start.5 = (bf16[128,1024]{1,0:T(8,128)(2,1)}, bf16[128,1024]{1,0:T(8,128)(2,1)S(1)}, u32[]{:S(2)}, u32[]{:S(2)}) collective-permute-start(bf16[128,1024]{1,0:T(8,128)(2,1)} %param.6), channel_id=1, source_target_pairs={{0,4},{4,0},{1,5},{5,1},{2,6},{6,2},{3,7},{7,3},{8,12},{12,8},{9,1... | collective-permute-start | bytes 786440 | tf_op jit(solution)/shard_map/ppermute | solution.py:374
  1.4 1.7 %collective-permute-start.6 = (bf16[128,1024]{1,0:T(8,128)(2,1)}, bf16[128,1024]{1,0:T(8,128)(2,1)S(1)}, u32[]{:S(2)}, u32[]{:S(2)}) collective-permute-start(bf16[128,1024]{1,0:T(8,128)(2,1)} %param.7), channel_id=1, source_target_pairs={{0,4},{4,0},{1,5},{5,1},{2,6},{6,2},{3,7},{7,3},{8,12},{12,8},{9,1... | collective-permute-start | bytes 786440 | tf_op jit(solution)/shard_map/ppermute | solution.py:374
  1.5 6.4 %collective-permute-start = (bf16[128,1024]{1,0:T(8,128)(2,1)}, bf16[128,1024]{1,0:T(8,128)(2,1)S(1)}, u32[]{:S(2)}, u32[]{:S(2)}) collective-permute-start(bf16[128,1024]{1,0:T(8,128)(2,1)} %param.5), channel_id=1, source_target_pairs={{0,4},{4,0},{1,5},{5,1},{2,6},{6,2},{3,7},{7,3},{8,12},{12,8},{9,1... | collective-permute-start | bytes 786440 | tf_op jit(solution)/shard_map/ppermute | solution.py:374
  1.9 6.0 %collective-permute-start.1 = (bf16[128,1024]{1,0:T(8,128)(2,1)}, bf16[128,1024]{1,0:T(8,128)(2,1)S(1)}, u32[]{:S(2)}, u32[]{:S(2)}) collective-permute-start(bf16[128,1024]{1,0:T(8,128)(2,1)} %param.9), channel_id=1, source_target_pairs={{0,4},{4,0},{1,5},{5,1},{2,6},{6,2},{3,7},{7,3},{8,12},{12,8},{9,1... | collective-permute-start | bytes 786440 | tf_op jit(solution)/shard_map/ppermute | solution.py:374
  3.2 1.4 %copy-start.1 = (bf16[128,1024]{1,0:T(8,128)(2,1)S(1)}, bf16[128,1024]{1,0:T(8,128)(2,1)}, u32[]{:S(2)}) copy-start(bf16[128,1024]{1,0:T(8,128)(2,1)} %param.5) | copy-start | bytes 786436
  3.2 1.4 %copy-start.2 = (bf16[128,1024]{1,0:T(8,128)(2,1)S(1)}, bf16[128,1024]{1,0:T(8,128)(2,1)}, u32[]{:S(2)}) copy-start(bf16[128,1024]{1,0:T(8,128)(2,1)} %param.9) | copy-start | bytes 786436
  3.3 7.9 %collective-permute-start.7 = (bf16[2,256,128]{2,1,0:T(8,128)(2,1)S(1)}, bf16[2,256,128]{2,1,0:T(8,128)(2,1)S(1)}, u32[]{:S(2)}, u32[]{:S(2)}) collective-permute-start(bf16[2,256,128]{2,1,0:T(8,128)(2,1)S(1)} %get-tuple-element.60), channel_id=1, source_target_pairs={{0,8},{8,0},{16,24},{24,16},{1,9},{9,1},{17,25},{25,17},{2,10},{10... | collective-permute-start | bytes 393224 | tf_op jit(solution)/shard_map/ppermute | solution.py:379
  4.6 8.5 %collective-permute-start.8 = (bf16[2,256,128]{2,1,0:T(8,128)(2,1)S(1)}, bf16[2,256,128]{2,1,0:T(8,128)(2,1)S(1)}, u32[]{:S(2)}, u32[]{:S(2)}) collective-permute-start(bf16[2,256,128]{2,1,0:T(8,128)(2,1)S(1)} %get-tuple-element.61), channel_id=1, source_target_pairs={{0,16},{8,24},{16,0},{24,8},{1,17},{9,25},{17,1},{25,9},{2,18},{10... | collective-permute-start | bytes 393224 | tf_op jit(solution)/shard_map/ppermute | solution.py:379
  7.1 8.6 %collective-permute-start.9 = (bf16[2,256,128]{2,1,0:T(8,128)(2,1)S(1)}, bf16[2,256,128]{2,1,0:T(8,128)(2,1)S(1)}, u32[]{:S(2)}, u32[]{:S(2)}) collective-permute-start(bf16[2,256,128]{2,1,0:T(8,128)(2,1)S(1)} %get-tuple-element.62), channel_id=1, source_target_pairs={{0,24},{8,16},{16,8},{24,0},{1,25},{9,17},{17,9},{25,1},{2,26},{10... | collective-permute-start | bytes 393224 | tf_op jit(solution)/shard_map/ppermute | solution.py:379
  8.0 11.6 %collective-permute-start.2 = (bf16[2,256,128]{2,1,0:T(8,128)(2,1)S(1)}, bf16[2,256,128]{2,1,0:T(8,128)(2,1)S(1)}, u32[]{:S(2)}, u32[]{:S(2)}) collective-permute-start(bf16[2,256,128]{2,1,0:T(8,128)(2,1)S(1)} %get-tuple-element.55), channel_id=1, source_target_pairs={{0,8},{8,0},{16,24},{24,16},{1,9},{9,1},{17,25},{25,17},{2,10},{10... | collective-permute-start | bytes 393224 | tf_op jit(solution)/shard_map/ppermute | solution.py:379
  8.1 11.5 %collective-permute-start.3 = (bf16[2,256,128]{2,1,0:T(8,128)(2,1)S(1)}, bf16[2,256,128]{2,1,0:T(8,128)(2,1)S(1)}, u32[]{:S(2)}, u32[]{:S(2)}) collective-permute-start(bf16[2,256,128]{2,1,0:T(8,128)(2,1)S(1)} %get-tuple-element.56), channel_id=1, source_target_pairs={{0,16},{8,24},{16,0},{24,8},{1,17},{9,25},{17,1},{25,9},{2,18},{10... | collective-permute-start | bytes 393224 | tf_op jit(solution)/shard_map/ppermute | solution.py:379
  11.2 10.1 %collective-permute-start.4 = (bf16[2,256,128]{2,1,0:T(8,128)(2,1)S(1)}, bf16[2,256,128]{2,1,0:T(8,128)(2,1)S(1)}, u32[]{:S(2)}, u32[]{:S(2)}) collective-permute-start(bf16[2,256,128]{2,1,0:T(8,128)(2,1)S(1)} %get-tuple-element.57), channel_id=1, source_target_pairs={{0,24},{8,16},{16,8},{24,0},{1,25},{9,17},{17,9},{25,1},{2,26},{10... | collective-permute-start | bytes 393224 | tf_op jit(solution)/shard_map/ppermute | solution.py:379
  16.0 8.6 %collective-permute-start.11 = (bf16[2,128,128]{2,1,0:T(8,128)(2,1)S(1)}, bf16[2,128,128]{2,1,0:T(8,128)(2,1)S(1)}, u32[]{:S(2)}, u32[]{:S(2)}) collective-permute-start(bf16[2,128,128]{2,1,0:T(8,128)(2,1)S(1)} %get-tuple-element.68), channel_id=1, source_target_pairs={{32,64},{96,128},{160,192},{64,32},{128,96},{192,160},{33,65},{97,... | collective-permute-start | bytes 196616 | tf_op jit(solution)/shard_map/ppermute | solution.py:370
  19.5 5.1 %collective-permute-start.10 = (bf16[4,128,128]{2,1,0:T(8,128)(2,1)S(1)}, bf16[4,128,128]{2,1,0:T(8,128)(2,1)S(1)}, u32[]{:S(2)}, u32[]{:S(2)}) collective-permute-start(bf16[4,128,128]{2,1,0:T(8,128)(2,1)S(1)} %get-tuple-element.67), channel_id=1, source_target_pairs={{0,32},{32,0},{64,96},{96,64},{128,160},{160,128},{192,224},{224,1... | collective-permute-start | bytes 393224 | tf_op jit(solution)/shard_map/ppermute | solution.py:365
  45.6 8.0 %collective-permute-start.13 = (bf16[2,128,128]{2,1,0:T(8,128)(2,1)S(1)}, bf16[2,128,128]{2,1,0:T(8,128)(2,1)S(1)}, u32[]{:S(2)}, u32[]{:S(2)}) collective-permute-start(bf16[2,128,128]{2,1,0:T(8,128)(2,1)S(1)} %get-tuple-element.97), channel_id=1, source_target_pairs={{32,64},{96,128},{160,192},{64,32},{128,96},{192,160},{33,65},{97,... | collective-permute-start | bytes 196616 | tf_op jit(solution)/shard_map/ppermute | solution.py:370
  50.7 4.4 %collective-permute-start.12 = (bf16[4,128,128]{2,1,0:T(8,128)(2,1)S(1)}, bf16[4,128,128]{2,1,0:T(8,128)(2,1)S(1)}, u32[]{:S(2)}, u32[]{:S(2)}) collective-permute-start(bf16[4,128,128]{2,1,0:T(8,128)(2,1)S(1)} %get-tuple-element.96), channel_id=1, source_target_pairs={{0,32},{32,0},{64,96},{96,64},{128,160},{160,128},{192,224},{224,1... | collective-permute-start | bytes 393224 | tf_op jit(solution)/shard_map/ppermute | solution.py:365
  55.5 6.1 %collective-permute-start.14 = (bf16[4,256,128]{2,1,0:T(8,128)(2,1)S(1)}, bf16[4,256,128]{2,1,0:T(8,128)(2,1)S(1)}, u32[]{:S(2)}, u32[]{:S(2)}) collective-permute-start(bf16[4,256,128]{2,1,0:T(8,128)(2,1)S(1)} %get-tuple-element.99), channel_id=1, source_target_pairs={{0,8},{8,0},{16,24},{24,16},{1,9},{9,1},{17,25},{25,17},{2,10},{10... | collective-permute-start | bytes 786440 | tf_op jit(solution)/shard_map/ppermute | solution.py:379
  56.2 12.2 %collective-permute-start.15 = (bf16[4,256,128]{2,1,0:T(8,128)(2,1)S(1)}, bf16[4,256,128]{2,1,0:T(8,128)(2,1)S(1)}, u32[]{:S(2)}, u32[]{:S(2)}) collective-permute-start(bf16[4,256,128]{2,1,0:T(8,128)(2,1)S(1)} %get-tuple-element.100), channel_id=1, source_target_pairs={{0,16},{8,24},{16,0},{24,8},{1,17},{9,25},{17,1},{25,9},{2,18},{10... | collective-permute-start | bytes 786440 | tf_op jit(solution)/shard_map/ppermute | solution.py:379
  58.0 13.4 %collective-permute-start.16 = (bf16[4,256,128]{2,1,0:T(8,128)(2,1)S(1)}, bf16[4,256,128]{2,1,0:T(8,128)(2,1)S(1)}, u32[]{:S(2)}, u32[]{:S(2)}) collective-permute-start(bf16[4,256,128]{2,1,0:T(8,128)(2,1)S(1)} %get-tuple-element.101), channel_id=1, source_target_pairs={{0,24},{8,16},{16,8},{24,0},{1,25},{9,17},{17,9},{25,1},{2,26},{10... | collective-permute-start | bytes 786440 | tf_op jit(solution)/shard_map/ppermute | solution.py:379
  71.5 3.8 %collective-permute-start.17 = (bf16[4,128,512]{2,1,0:T(8,128)(2,1)S(1)}, bf16[4,128,512]{2,1,0:T(8,128)(2,1)S(1)}, u32[]{:S(2)}, u32[]{:S(2)}) collective-permute-start(bf16[4,128,512]{2,1,0:T(8,128)(2,1)S(1)} %get-tuple-element.103), channel_id=1, source_target_pairs={{0,4},{4,0},{1,5},{5,1},{2,6},{6,2},{3,7},{7,3},{8,12},{12,8},{9,1... | collective-permute-start | bytes 1572872 | tf_op jit(solution)/shard_map/ppermute | solution.py:374

commit v3 on v2

--- a/solution.py
+++ b/solution.py
@@ -11,6 +11,7 @@
 BLOCK = 128
 GROUP = 8
 CHIPS = 4
+STEPS = (0, 2, 3, 1)
 HALF = CHIPS * 128
 MID = GROUP - 2
 TOKENS = GROUP * BLOCK
@@ -20,6 +21,7 @@
 FLOOR = -1e30
 FLOPS = 4 * 10**9
 SCALE = 1.0 / math.sqrt(DH)
+SHARP = SCALE * math.log2(math.e)
 VMEM = pl.BlockSpec(memory_space=pltpu.VMEM)
 HBM = pl.BlockSpec(memory_space=pltpu.HBM)
 F32 = jnp.float32
@@ -68,7 +70,7 @@
 def pack_kernel(x, y, got_x, got_y, *messages):
     core, chip = lax.axis_index("c"), lax.axis_index("x")
     mine, theirs = at_block(core), at_block(1 - core)
-    for step, message in enumerate(messages):
+    for step, message in zip(STEPS, messages):
         here = (chip ^ step) * DH
         cols = pl.ds(pl.multiple_of(core * HALF + here, DH), DH)
         for i, (own, got) in enumerate(((x, got_x), (y, got_y))):
@@ -78,7 +80,7 @@
 
 def places():
     chip = lax.axis_index("x")
-    return [pl.ds(pl.multiple_of((chip ^ step) * 2 * BLOCK, BLOCK), 2 * BLOCK) for step in range(CHIPS)]
+    return [pl.ds(pl.multiple_of((chip ^ step) * 2 * BLOCK, BLOCK), 2 * BLOCK) for step in STEPS]
 
 
 def pool(x, p, f32):
@@ -122,37 +124,43 @@
     return scratch[pl.ds(0, n * times), :]
 
 
-def row_sum(x):
-    ones = jnp.ones((8, DH), BF16)
-    high = x.astype(BF16)
-    low = (x - high.astype(F32)).astype(BF16)
-    return (nt(ones, high) + nt(ones, low))[:1]
-
-
-def attend(queries, keys, values, at, tops, totals, sums, invalid=None):
-    scores = nt(queries, keys) * SCALE
-    if invalid is not None:
-        side, bad = invalid
-        lane = lax.broadcasted_iota(jnp.int32, scores.shape, 1) // BLOCK
-        scores = jnp.where((lane == side) & bad, FLOOR, scores)
-    top = jnp.max(scores, axis=1, keepdims=True)
-    weights = jnp.exp(scores - top)
-    rounded = weights.astype(BF16)
-    tops[at, :] = jnp.broadcast_to(top, (BLOCK, DH))
-    totals[at, :] = jnp.broadcast_to(jnp.sum(weights, axis=1, keepdims=True), (BLOCK, DH))
-    sums[at, :] = nn(rounded, values)
+def column(x):
+    return jnp.sum(x, axis=1, keepdims=True)
+
+
+def attend(items, tops, totals, sums):
+    scores = []
+    for queries, keys, _, _, invalid in items:
+        one = nt(queries, keys)
+        if invalid is not None:
+            side, bad = invalid
+            lane = lax.broadcasted_iota(jnp.int32, one.shape, 1) // BLOCK
+            one = jnp.where((lane == side) & bad, FLOOR, one)
+        scores.append(one)
+    weights = []
+    for one, (_, _, _, at, _) in zip(scores, items):
+        top = jnp.max(one, axis=1, keepdims=True)
+        tops[at, :] = jnp.broadcast_to(top, (BLOCK, DH))
+        weights.append(jnp.exp2((one - top) * SHARP))
+    rounded = [one.astype(BF16) for one in weights]
+    for one, (_, _, values, at, _) in zip(rounded, items):
+        both = nn(one, jnp.concatenate([values, jnp.ones_like(values)], axis=1))
+        sums[at, :] = both[:, :DH]
+        totals[at, :] = both[:, DH:]
     return rounded
 
 
 def forward_inner_kernel(q, k, v, qp, kp, vp, w_mid, w_coarse, tops, totals, sums):
-    for b in range(MID):
-        w_mid[rows(b), :] = attend(
-            q[rows(b + 1), :], k[rows(b, 3), :], v[rows(b, 3), :], rows(b), tops, totals, sums
-        )
-    for c in range(6):
-        w_coarse[rows(c), :] = attend(
-            qp[rows(c), :], kp[rows(c ^ 1), :], vp[rows(c ^ 1), :], rows(MID + c), tops, totals, sums
-        )
+    inner = [
+        (q[rows(b + 1), :], k[rows(b, 3), :], v[rows(b, 3), :], rows(b), None) for b in range(MID)
+    ]
+    for b, one in enumerate(attend(inner, tops, totals, sums)):
+        w_mid[rows(b), :] = one
+    coarse = [
+        (qp[rows(c), :], kp[rows(c ^ 1), :], vp[rows(c ^ 1), :], rows(MID + c), None) for c in range(6)
+    ]
+    for c, one in enumerate(attend(coarse, tops, totals, sums)):
+        w_coarse[rows(c), :] = one
 
 
 def forward_edge_kernel(
@@ -168,12 +176,13 @@
         edge[1, rows(0, 2), :] = x[rows(GROUP - 2, 2), :]
         edge[1, rows(2), :] = jnp.where(odd, other[i], pair[i])
     last = z == lax.axis_size("z") - 1
-    for e, (b, invalid) in enumerate(((0, (0, z == 0)), (GROUP - 1, (2, last)))):
-        w_edge[rows(e), :] = attend(
-            q[rows(b), :], edge_k[e], edge_v[e], rows(e), e_tops, e_totals, e_sums, invalid
-        )
     top3 = rows(2)
-    w_top[...] = attend(qp[rows(6), :], pair[2], pair[3], top3, e_tops, e_totals, e_sums)
+    items = [
+        (q[rows(b), :], edge_k[e], edge_v[e], rows(e), invalid)
+        for e, (b, invalid) in enumerate(((0, (0, z == 0)), (GROUP - 1, (2, last))))
+    ]
+    items.append((qp[rows(6), :], pair[2], pair[3], top3, None))
+    w_edge[rows(0), :], w_edge[rows(1), :], w_top[...] = attend(items, e_tops, e_totals, e_sums)
     m, t, s = e_tops[top3, :], e_totals[top3, :] * 8.0, e_sums[top3, :] * 8.0
     n = TOKENS // 8
     for level, out in ((2, share2), (1, share1)):
@@ -182,13 +191,15 @@
         at = pl.ds(MID * BLOCK + START[level], n)
         own = tops[at, :]
         m = jnp.maximum(own, em)
-        here = 2.0**level * jnp.exp(own - m)
-        up = jnp.exp(em - m)
+        here = 2.0**level * jnp.exp2((own - m) * SHARP)
+        up = jnp.exp2((em - m) * SHARP)
         t = here * totals[at, :] + up * et
         s = here * sums[at, :] + up * es
         out[0] = here
         out[1] = up
     spread(up_m, m, n), spread(up_t, t, n), spread(up_s, s, n)
+    lane = lax.broadcasted_iota(jnp.int32, (BLOCK, DH), 1)
+    columns = jnp.zeros((BLOCK, DH), F32)
     for b in range(GROUP):
         if b in (0, GROUP - 1):
             at, (mm, tt, ss) = rows(b // (GROUP - 1)), (e_tops, e_totals, e_sums)
@@ -196,7 +207,7 @@
             at, (mm, tt, ss) = rows(b - 1), (tops, totals, sums)
         own, em = mm[at, :], up_m[rows(b), :]
         m = jnp.maximum(own, em)
-        here, up = jnp.exp(own - m), jnp.exp(em - m)
+        here, up = jnp.exp2((own - m) * SHARP), jnp.exp2((em - m) * SHARP)
         inverse = 1.0 / (here * tt[at, :] + up * up_t[rows(b), :])
         here, up = here * inverse, up * inverse
         rounded = (here * ss[at, :] + up * up_s[rows(b), :]).astype(BF16)
@@ -205,16 +216,19 @@
         attn[rows(b), :] = rounded
         flat = rounded.astype(F32)
         scaled = d[rows(b), :].astype(F32) * gain[...]
-        sums_here = jnp.concatenate([row_sum(flat * flat), row_sum(scaled * flat)], axis=0)
-        stats[:, :, pl.ds(b, 1), :] = jnp.broadcast_to(
-            sums_here.reshape(1, 2, 1, BLOCK), (stats.shape[0], 2, 1, BLOCK)
-        )
-
-
-def slope_of(grad, values, weights, offset):
-    pressure = nt(grad, values)
-    wide = jnp.concatenate([offset] * (values.shape[0] // BLOCK), axis=1)
-    return (weights.astype(F32) * (pressure - wide)).astype(BF16)
+        for i, one in enumerate((column(flat * flat), column(scaled * flat))):
+            columns = jnp.where(lane == i * GROUP + b, one, columns)
+    turned = columns.T[: 2 * GROUP].reshape(1, 2, GROUP, BLOCK)
+    stats[...] = jnp.broadcast_to(turned, stats.shape)
+
+
+def slopes_of(items):
+    pressures = [nt(grad, values) for grad, values, _, _ in items]
+    slopes = []
+    for pressure, (_, values, weights, offset) in zip(pressures, items):
+        wide = jnp.concatenate([offset] * (values.shape[0] // BLOCK), axis=1)
+        slopes.append((weights.astype(F32) * (pressure - wide)).astype(BF16))
+    return slopes
 
 
 def backward_edge_kernel(
@@ -234,7 +248,7 @@
         out[rows(b), :] = (flat * (inv * gain[...])).astype(BF16)
         scaled = d[rows(b), :].astype(F32) * gain[...]
         grad = (inv * scaled - flat * drop).astype(BF16).astype(F32)
-        dot = jnp.broadcast_to(jnp.sum(grad * flat, axis=1, keepdims=True), (BLOCK, DH))
+        dot = jnp.broadcast_to(column(grad * flat), (BLOCK, DH))
         here, up = share[0, rows(b), :], share[1, rows(b), :]
         g0[rows(b), :] = (here * grad).astype(BF16)
         off0[rows(b), :] = here * dot
@@ -255,36 +269,47 @@
             offc[at, :] = o * here
             buf[pl.ds(0, n), :] = g * up
             buf2[pl.ds(0, n), :] = o * up
+    items = [
+        (g0[rows(b), :], edge_v[e], w_edge[rows(e), :], off0[rows(b), :])
+        for e, b in ((0, 0), (1, GROUP - 1))
+    ]
+    top_grad = gc[rows(6), :]
+    items.append((top_grad, pair[3], w_top[...], offc[rows(6), :]))
+    slopes = slopes_of(items)
     edges = []
     for e, b in ((0, 0), (1, GROUP - 1)):
-        grad = g0[rows(b), :]
-        slope = slope_of(grad, edge_v[e], w_edge[rows(e), :], off0[rows(b), :])
-        sl_edge[rows(e), :] = slope
-        q_edge[rows(e), :] = nn(slope, edge_k[e]) * SCALE
+        sl_edge[rows(e), :] = slopes[e]
+        q_edge[rows(e), :] = nn(slopes[e], edge_k[e]) * SCALE
         side = slice(2 * e * BLOCK, (2 * e + 1) * BLOCK)
         edges.append((
-            (tn(slope[:, side], q[rows(b), :]) * SCALE).astype(BF16),
-            tn(w_edge[rows(e), side], grad).astype(BF16),
+            (tn(slopes[e][:, side], q[rows(b), :]) * SCALE).astype(BF16),
+            tn(w_edge[rows(e), side], items[e][0]).astype(BF16),
         ))
-    grad = gc[rows(6), :]
-    slope = slope_of(grad, pair[3], w_top[...], offc[rows(6), :])
-    q_top[...] = nn(slope, pair[2]) * SCALE
-    pair_out[2] = (tn(slope, qp[rows(6), :]) * SCALE).astype(BF16)
-    pair_out[3] = tn(w_top[...], grad).astype(BF16)
+    q_top[...] = nn(slopes[2], pair[2]) * SCALE
+    pair_out[2] = (tn(slopes[2], qp[rows(6), :]) * SCALE).astype(BF16)
+    pair_out[3] = tn(w_top[...], top_grad).astype(BF16)
     for i in range(2):
         pair_out[i] = jnp.where(odd, edges[0][i], edges[1][i])
         other_out[i] = jnp.where(odd, edges[1][i], edges[0][i])
 
 
 def backward_inner_kernel(
-    q, k, v, qp, kp, vp, w_mid, w_coarse, w_edge, g0, gc, off0, offc, sl_edge, q_edge, q_top,
-    q_grad, k_grad, v_grad,
-    sl_mid, sl_coarse, buf, grads,
+    q, k, v, qp, kp, vp, w_mid, w_coarse, w_edge, g0, gc, off0, offc, sl_edge, q_edge, q_top, out,
+    k_grad, v_grad, m0, m1, m2, m3,
+    sl_mid, sl_coarse, buf, grads, q_grad,
 ):
-    for c in range(6):
-        slope = slope_of(gc[rows(c), :], vp[rows(c ^ 1), :], w_coarse[rows(c), :], offc[rows(c), :])
+    coarse = slopes_of([
+        (gc[rows(c), :], vp[rows(c ^ 1), :], w_coarse[rows(c), :], offc[rows(c), :]) for c in range(6)
+    ])
+    for c, slope in enumerate(coarse):
         sl_coarse[rows(c), :] = slope
         grads[rows(c), :] = nn(slope, kp[rows(c ^ 1), :]) * SCALE
+    inner = slopes_of([
+        (g0[rows(b + 1), :], v[rows(b, 3), :], w_mid[rows(b), :], off0[rows(b + 1), :])
+        for b in range(MID)
+    ])
+    for b, slope in enumerate(inner):
+        sl_mid[rows(b), :] = slope
     e = grads[rows(4, 2), :] * 0.25 + spread(buf, q_top[...] * 0.125, 128)
     e = grads[rows(0, 4), :] * 0.5 + spread(buf, e, 256)
     spread(buf, e, 512)
@@ -292,12 +317,12 @@
         if b in (0, GROUP - 1):
             part = q_edge[rows(b // (GROUP - 1)), :]
         else:
-            slope = slope_of(
-                g0[rows(b), :], v[rows(b - 1, 3), :], w_mid[rows(b - 1), :], off0[rows(b), :]
-            )
-            sl_mid[rows(b - 1), :] = slope
-            part = nn(slope, k[rows(b - 1, 3), :]) * SCALE
+            part = nn(inner[b - 1], k[rows(b - 1, 3), :]) * SCALE
         q_grad[rows(b), :] = (part + buf[rows(b), :]).astype(BF16)
+
+    for at, message in zip(places(), (m0, m1, m2, m3)):
+        message[0] = out[at, :]
+        message[1] = q_grad[at, :]
 
     def key_value(factor, edge, mid, mid_c, right, right_c, res):
         for c in range(6):
@@ -324,7 +349,7 @@
     key_value(1.0, w_edge, w_mid, w_coarse, g0, gc, v_grad)
 
 
-def collect_kernel(out, q_grad, k_grad, v_grad, pair, other, *refs):
+def collect_kernel(k_grad, v_grad, pair, other, *refs):
     messages, buf = refs[:-1], refs[-1]
     odd = lax.rem(lax.axis_index("z"), 2) == 1
     for i, x in enumerate((k_grad, v_grad)):
@@ -333,19 +358,16 @@
         buf[rows(0), :] += jnp.where(odd, pair[i], other[i]).astype(F32)
         buf[rows(GROUP - 1), :] += jnp.where(odd, other[i], pair[i]).astype(F32)
         for at, message in zip(places(), messages):
-            message[2 + i] = buf[at, :].astype(BF16)
-    for at, message in zip(places(), messages):
-        message[0] = out[at, :]
-        message[1] = q_grad[at, :]
+            message[i] = buf[at, :].astype(BF16)
 
 
 def regroup_kernel(*refs):
     parts, (own, away) = refs[:CHIPS], refs[CHIPS:]
     core, chip = lax.axis_index("c"), lax.axis_index("x")
     mine, theirs = at_block(core), at_block(1 - core)
-    for step, part in enumerate(parts):
+    for step, part in zip(STEPS, parts):
         cols = pl.ds(pl.multiple_of((chip ^ step) * DH, DH), DH)
-        for i in range(4):
+        for i in range(2):
             own[i, :, cols] = part[i, mine, :]
             away[i, :, cols] = part[i, theirs, :]
 
@@ -376,7 +398,8 @@
 
 def swap_chips(messages):
     return [messages[0]] + [
-        lax.ppermute(messages[step], "x", [(i, i ^ step) for i in range(CHIPS)]) for step in (1, 2, 3)
+        lax.ppermute(message, "x", [(i, i ^ step) for i in range(CHIPS)])
+        for step, message in zip(STEPS[1:], messages[1:])
     ]
 
 
@@ -387,8 +410,7 @@
 def local(query, keys, values, gain, out_grad):
     token = ((BLOCK, query.shape[1]), BF16, HBM)
     part = ((2, 2 * BLOCK, DH), BF16)
-    chip_part = ((4, 2 * BLOCK, DH), BF16)
-    half = ((4, BLOCK, HALF), BF16)
+    half = ((2, BLOCK, HALF), BF16)
     partners = GROUP * lax.axis_size("head")
     message = ((4, BLOCK, DH), BF16)
     edge = ((2, BLOCK, DH), BF16)
@@ -443,18 +465,22 @@
         [whole_f] * 2,
     )(stats, d, my_gain, attn, share, share1, share2, q, qp, pair, edge_k, edge_v, w_edge, w_top)
     pair_back, other_back = swap_pair(pair_back), swap_other(other_back)
-    grads = call(
+    k_grad, v_grad, *messages = call(
         backward_inner_kernel,
-        [whole, whole_f, whole_f],
-        16,
-        [w_mids, w_coarses, whole_f, coarse_f],
+        [whole_f, whole_f] + [part] * CHIPS,
+        17,
+        [w_mids, w_coarses, whole_f, coarse_f, whole],
         flops=2 * FLOPS,
-    )(q, k, v, qp, kp, vp, w_mid, w_coarse, w_edge, g0, gc, off0, offc, sl_edge, q_edge, q_top)
-    messages = call(collect_kernel, [chip_part] * CHIPS, 6, [whole_f])(
-        out, *grads, pair_back, other_back
-    )
-    own, away = call(regroup_kernel, [half] * 2, CHIPS)(*swap_chips(messages))
-    return call(finish_kernel, [token] * 4, 2, [pltpu.SemaphoreType.DMA((2, 4))])(own, swap_core(away))
+    )(q, k, v, qp, kp, vp, w_mid, w_coarse, w_edge, g0, gc, off0, offc, sl_edge, q_edge, q_top, out)
+
+    def deliver(messages):
+        own, away = call(regroup_kernel, [half] * 2, CHIPS)(*swap_chips(messages))
+        finish = call(finish_kernel, [token] * 2, 2, [pltpu.SemaphoreType.DMA((2, 2))])
+        return finish(own, swap_core(away))
+
+    out, q_grad = deliver(messages)
+    messages = call(collect_kernel, [part] * CHIPS, 4, [whole_f])(k_grad, v_grad, pair_back, other_back)
+    return (out, q_grad, *deliver(messages))
 
 
 def solution(mesh):

time: 78 us -> 67.1 us (0.86); the launches traced: 76.5 us -> 66.9 us
  waiting for transfers between devices: 20.3 us -> 6.83 us
  starting transfers between devices: 25 us -> 31.3 us
  Pallas kernels: 11.3 us -> 7.78 us
  blocking collectives: 17.8 us -> 18.9 us
    ppermute x9 -> x12, waiting for transfers between devices: 17.2 us -> 5.24 us  [swap_chips(): lax.ppermute(message, 'x', [(i, i ^ step) for i in range(CHIPS)])]
    ppermute x5 -> x6, starting transfers between devices: 3.64 us -> 6.43 us  [swap_core(): return lax.ppermute(x, 'c', [(0, 1), (1, 0)])]
    ppermute x9 -> x12, starting transfers between devices: 12.5 us -> 14.8 us  [swap_chips(): lax.ppermute(message, 'x', [(i, i ^ step) for i in range(CHIPS)])]
    pallas_call x1, Pallas kernels: 3.12 us -> 1.02 us  [local(): call(forward_inner_kernel, [w_mids, w_coarses] + [inner_f] * 3, 6, flops=...]
    ppermute x2, starting transfers between devices: 8.57 us -> 9.9 us  [swap_other(): lax.ppermute(x, 'z', up + [(target, source) for source, target in up])]
    ppermute x5 -> x6, waiting for transfers between devices: 1.68 us -> 0.48 us  [swap_core(): return lax.ppermute(x, 'c', [(0, 1), (1, 0)])]
    all_to_all x1, blocking collectives: 17.8 us -> 18.9 us  [exchange(): return lax.all_to_all(x, axes, 0, 0, tiled=True)]
    pallas_call x4 -> x6, Pallas kernels: 4.33 us -> 3.75 us  [the longest x2 1.63 us: deliver(): return finish(own, swap_core(away))]
  transfers between devices with their start and end apart: 18 -> 22, of which waited for: 9 -> 9; matrix products, arithmetic and copies ran while one was open for 1% -> 2% of each run, Pallas kernels for 8% -> 7%
where the time goes in v3:
time: 67.1 us; the launch traced here: 66.9 us
  starting transfers between devices  31.3 us (47%)
  blocking collectives  18.9 us (28%)
  Pallas kernels  7.78 us (12%)
  waiting for transfers between devices  6.83 us (10%)
  local copies, waits for them, and re-layouts  1.1 us (2%)
  between operations  0.97 us (1%)
    all_to_all x1, blocking collectives, exchange(): return lax.all_to_all(x, axes, 0, 0, tiled=True)  18.9 us
    ppermute x12, starting transfers between devices, swap_chips(): lax.ppermute(message, 'x', [(i, i ^ step) for i in range(CHIPS)])  14.8 us
    ppermute x2, starting transfers between devices, swap_other(): lax.ppermute(x, 'z', up + [(target, source) for source, target in up])  9.9 us
    ppermute x6, starting transfers between devices, swap_core(): return lax.ppermute(x, 'c', [(0, 1), (1, 0)])  6.43 us
    ppermute x12, waiting for transfers between devices, swap_chips(): lax.ppermute(message, 'x', [(i, i ^ step) for i in range(CHIPS)])  5.24 us
    pallas_call x2, Pallas kernels, deliver(): return finish(own, swap_core(away))  1.63 us
    pallas_call x1, Pallas kernels, local(): call(backward_inner_kernel, [whole_f, whole_f] + [part] * CHIPS, 17, [w_m...  1.53 us
  transfers between devices with their start and end apart: 22, of which 9 were waited for; matrix products, arithmetic and copies ran while one was open for 2% of the time, Pallas kernels for 7%

profile of v3, /device:TPU:33, one launch (start us, length us, event | category | flops | bytes accessed | tf_op | source)
XLA Modules:
  0.0 66.9 jit_solution(17416168631987467904)
XLA Ops:
  0.6 0.0 copy-start
  0.6 0.8 %collective-permute-start.5 = (bf16[128,1024]{1,0:T(8,128)(2,1)}, bf16[128,1024]{1,0:T(8,128)(2,1)S(1)}, u32[]{:S(2)}, u32[]{:S(2)}) collective-permute-start(bf16[128,1024]{1,0:T(8,128)(2,1)} %param.6), channel_id=1, source_target_pairs={{0,4},{4,0},{1,5},{5,1},{2,6},{6,2},{3,7},{7,3},{8,12},{12,8},{9,1... | collective-permute-start | bytes 786440 | tf_op jit(solution)/shard_map/ppermute | solution.py:396
  1.4 0.1 collective-permute-start.6
  1.5 0.4 collective-permute-start
  1.9 0.1 collective-permute-start.1
  2.0 1.0 %constant_dynamic-slice_fusion = (bf16[128,512]{1,0:T(8,128)(2,1)S(1)}, bf16[128,512]{1,0:T(8,128)(2,1)S(1)}) fusion(bf16[128,1024]{1,0:T(8,128)(2,1)} %param.7, s32[]{:T(128)S(6)} %select_n.4, bf16[128,1024]{1,0:T(8,128)(2,1)} %param.6), kind=kLoop, calls=%fused_computation | loop fusion | bytes 524292 | tf_op jit(solution)/shard_map/dynamic_slice | solution.py:437
  3.0 0.0 collective-permute-done.5.got_x
  3.0 0.1 collective-permute-done.6.got_y
  3.2 0.1 shard_map.86
  3.3 2.8 %collective-permute-start.7 = (bf16[2,256,128]{2,1,0:T(8,128)(2,1)S(1)}, bf16[2,256,128]{2,1,0:T(8,128)(2,1)S(1)}, u32[]{:S(2)}, u32[]{:S(2)}) collective-permute-start(bf16[2,256,128]{2,1,0:T(8,128)(2,1)S(1)} %get-tuple-element.69), channel_id=1, source_target_pairs={{0,16},{8,24},{16,0},{24,8},{1,17},{9,25},{17,1},{25,9},{2,18},{10... | collective-permute-start | bytes 393224 | tf_op jit(solution)/shard_map/ppermute | solution.py:401
  6.1 0.9 %collective-permute-start.8 = (bf16[2,256,128]{2,1,0:T(8,128)(2,1)S(1)}, bf16[2,256,128]{2,1,0:T(8,128)(2,1)S(1)}, u32[]{:S(2)}, u32[]{:S(2)}) collective-permute-start(bf16[2,256,128]{2,1,0:T(8,128)(2,1)S(1)} %get-tuple-element.70), channel_id=1, source_target_pairs={{0,24},{8,16},{16,8},{24,0},{1,25},{9,17},{17,9},{25,1},{2,26},{10... | collective-permute-start | bytes 393224 | tf_op jit(solution)/shard_map/ppermute | solution.py:401
  7.1 0.0 collective-permute-start.9
  7.1 0.0 collective-permute-done.got_x
  7.1 0.0 collective-permute-done.1.got_y
  7.1 0.1 shard_map.84
  7.2 3.1 %collective-permute-start.2 = (bf16[2,256,128]{2,1,0:T(8,128)(2,1)S(1)}, bf16[2,256,128]{2,1,0:T(8,128)(2,1)S(1)}, u32[]{:S(2)}, u32[]{:S(2)}) collective-permute-start(bf16[2,256,128]{2,1,0:T(8,128)(2,1)S(1)} %get-tuple-element.64), channel_id=1, source_target_pairs={{0,16},{8,24},{16,0},{24,8},{1,17},{9,25},{17,1},{25,9},{2,18},{10... | collective-permute-start | bytes 393224 | tf_op jit(solution)/shard_map/ppermute | solution.py:401
  10.3 0.9 %collective-permute-start.3 = (bf16[2,256,128]{2,1,0:T(8,128)(2,1)S(1)}, bf16[2,256,128]{2,1,0:T(8,128)(2,1)S(1)}, u32[]{:S(2)}, u32[]{:S(2)}) collective-permute-start(bf16[2,256,128]{2,1,0:T(8,128)(2,1)S(1)} %get-tuple-element.65), channel_id=1, source_target_pairs={{0,24},{8,16},{16,8},{24,0},{1,25},{9,17},{17,9},{25,1},{2,26},{10... | collective-permute-start | bytes 393224 | tf_op jit(solution)/shard_map/ppermute | solution.py:401
  11.2 0.1 dynamic-slice_bitcast_fusion.gain.refs_2_
  11.2 1.1 %collective-permute-done.8.refs_2_ = bf16[2,256,128]{2,1,0:T(8,128)(2,1)S(1)} collective-permute-done((bf16[2,256,128]{2,1,0:T(8,128)(2,1)S(1)}, bf16[2,256,128]{2,1,0:T(8,128)(2,1)S(1)}, u32[]{:S(2)}, u32[]{:S(2)}) %collective-permute-start.8) | collective-permute-done | bytes 131104 | tf_op jit(solution)/shard_map/ppermute | solution.py:401
  12.3 0.2 collective-permute-done.9.refs_3_
  12.5 0.3 shard_map.87
  12.8 3.5 %collective-permute-start.11 = (bf16[2,128,128]{2,1,0:T(8,128)(2,1)S(1)}, bf16[2,128,128]{2,1,0:T(8,128)(2,1)S(1)}, u32[]{:S(2)}, u32[]{:S(2)}) collective-permute-start(bf16[2,128,128]{2,1,0:T(8,128)(2,1)S(1)} %get-tuple-element.81), channel_id=1, source_target_pairs={{32,64},{96,128},{160,192},{64,32},{128,96},{192,160},{33,65},{97,... | collective-permute-start | bytes 196616 | tf_op jit(solution)/shard_map/ppermute | solution.py:392
  16.3 0.1 collective-permute-start.10
  16.4 1.3 %collective-permute-done.3.refs_2_ = bf16[2,256,128]{2,1,0:T(8,128)(2,1)S(1)} collective-permute-done((bf16[2,256,128]{2,1,0:T(8,128)(2,1)S(1)}, bf16[2,256,128]{2,1,0:T(8,128)(2,1)S(1)}, u32[]{:S(2)}, u32[]{:S(2)}) %collective-permute-start.3) | collective-permute-done | bytes 131104 | tf_op jit(solution)/shard_map/ppermute | solution.py:401
  17.7 0.5 collective-permute-done.4.refs_3_
  18.2 0.1 shard_map.85
  18.3 1.0 %shard_map.88 = (bf16[768,384]{1,0:T(8,128)(2,1)S(1)}, bf16[768,128]{1,0:T(8,128)(2,1)S(1)}, f32[1536,128]{1,0:T(8,128)S(1)}, f32[1536,128]{1,0:T(8,128)S(1)}, f32[1536,128]{1,0:T(8,128)S(1)}) custom-call(bf16[1024,128]{1,0:T(8,128)(2,1)S(1)} %get-tuple-element.67.q.refs_7_, bf16[1024,128]{1,0:T(8,128)(2,1)S(1)} %get-tuple-element.72.k, ...), custom_call_target="tpu_custom_call" | custom-call | flops 4000000000 | tf_op jit(solution)/shard_map/pallas_call | solution.py:447
  19.4 1.1 %collective-permute-done.10.pair.refs_9_ = bf16[4,128,128]{2,1,0:T(8,128)(2,1)S(1)} collective-permute-done((bf16[4,128,128]{2,1,0:T(8,128)(2,1)S(1)}, bf16[4,128,128]{2,1,0:T(8,128)(2,1)S(1)}, u32[]{:S(2)}, u32[]{:S(2)}) %collective-permute-start.10) | collective-permute-done | bytes 131104 | tf_op jit(solution)/shard_map/ppermute | solution.py:387
  20.5 1.3 %shard_map.89 = (bf16[1024,128]{1,0:T(8,128)(2,1)S(1)}, f32[32,2,8,128]{3,2,1,0:T(8,128)S(1)}, bf16[256,384]{1,0:T(8,128)(2,1)S(1)}, bf16[128,128]{1,0:T(8,128)(...) custom-call(bf16[1024,128]{1,0:T(8,128)(2,1)S(1)} %get-tuple-element, ...), custom_call_target="tpu_custom_call" | custom-call | tf_op jit(solution)/shard_map/pallas_call | solution.py:450
  21.8 18.9 %all_to_all.5.refs_0_ = f32[32,2,8,128]{3,2,1,0:T(8,128)S(1)} all-to-all(f32[32,2,8,128]{3,2,1,0:T(8,128)S(1)} %get-tuple-element.86), channel_id=1, replica_groups=mesh['z'=8,'x'=4,'c'=2,'head'=4] {'x','c','head'}, dimensions={0} | all-to-all | bytes 524288 | tf_op jit(solution)/shard_map/all_to_all | solution.py:407
  40.6 1.1 %shard_map.90 = (bf16[1024,128]{1,0:T(8,128)(2,1)S(1)}, bf16[4,128,128]{2,1,0:T(8,128)(2,1)S(1)}, bf16[2,128,128]{2,1,0:T(8,128)(2,1)S(1)}, bf16[1024,128]{1,0:T...) custom-call(f32[32,2,8,128]{3,2,1,0:T(8,128)S(1)} %all_to_all.5.refs, ...), custom_call_target="tpu_custom_call" | custom-call | tf_op jit(solution)/shard_map/pallas_call | solution.py:461
  41.7 0.1 collective-permute-start.16
  41.8 1.5 %shard_map.91 = (f32[1024,128]{1,0:T(8,128)S(1)}, f32[1024,128]{1,0:T(8,128)S(1)}, bf16[2,256,128]{2,1,0:T(8,128)(2,1)S(1)}, bf16[2,256,128]{2,1,0:T(8,128)(2,1)...) custom-call(bf16[1024,128]{1,0:T(8,128)(2,1)S(1)} %get-tuple-element.67.q.refs_7_, ...), custom_call_target="tpu_custom_call" | custom-call | flops 8000000000 | tf_op jit(solution)/shard_map/pallas_call | solution.py:468
  43.3 1.4 %collective-permute-start.12 = (bf16[2,256,128]{2,1,0:T(8,128)(2,1)S(1)}, bf16[2,256,128]{2,1,0:T(8,128)(2,1)S(1)}, u32[]{:S(2)}, u32[]{:S(2)}) collective-permute-start(bf16[2,256,128]{2,1,0:T(8,128)(2,1)S(1)} %get-tuple-element.103), channel_id=1, source_target_pairs={{0,16},{8,24},{16,0},{24,8},{1,17},{9,25},{17,1},{25,9},{2,18},{10... | collective-permute-start | bytes 393224 | tf_op jit(solution)/shard_map/ppermute | solution.py:401
  44.7 6.4 %collective-permute-start.17 = (bf16[2,128,128]{2,1,0:T(8,128)(2,1)S(1)}, bf16[2,128,128]{2,1,0:T(8,128)(2,1)S(1)}, u32[]{:S(2)}, u32[]{:S(2)}) collective-permute-start(bf16[2,128,128]{2,1,0:T(8,128)(2,1)S(1)} %get-tuple-element.113), channel_id=1, source_target_pairs={{32,64},{96,128},{160,192},{64,32},{128,96},{192,160},{33,65},{97,... | collective-permute-start | bytes 196616 | tf_op jit(solution)/shard_map/ppermute | solution.py:392
  51.1 1.8 %collective-permute-start.13 = (bf16[2,256,128]{2,1,0:T(8,128)(2,1)S(1)}, bf16[2,256,128]{2,1,0:T(8,128)(2,1)S(1)}, u32[]{:S(2)}, u32[]{:S(2)}) collective-permute-start(bf16[2,256,128]{2,1,0:T(8,128)(2,1)S(1)} %get-tuple-element.104), channel_id=1, source_target_pairs={{0,24},{8,16},{16,8},{24,0},{1,25},{9,17},{17,9},{25,1},{2,26},{10... | collective-permute-start | bytes 393224 | tf_op jit(solution)/shard_map/ppermute | solution.py:401
  52.9 0.4 shard_map.94
  53.3 2.2 %collective-permute-start.18 = (bf16[2,256,128]{2,1,0:T(8,128)(2,1)S(1)}, bf16[2,256,128]{2,1,0:T(8,128)(2,1)S(1)}, u32[]{:S(2)}, u32[]{:S(2)}) collective-permute-start(bf16[2,256,128]{2,1,0:T(8,128)(2,1)S(1)} %get-tuple-element.115), channel_id=1, source_target_pairs={{0,16},{8,24},{16,0},{24,8},{1,17},{9,25},{17,1},{25,9},{2,18},{10... | collective-permute-start | bytes 393224 | tf_op jit(solution)/shard_map/ppermute | solution.py:401
  55.5 1.7 %collective-permute-start.19 = (bf16[2,256,128]{2,1,0:T(8,128)(2,1)S(1)}, bf16[2,256,128]{2,1,0:T(8,128)(2,1)S(1)}, u32[]{:S(2)}, u32[]{:S(2)}) collective-permute-start(bf16[2,256,128]{2,1,0:T(8,128)(2,1)S(1)} %get-tuple-element.116), channel_id=1, source_target_pairs={{0,24},{8,16},{16,8},{24,0},{1,25},{9,17},{17,9},{25,1},{2,26},{10... | collective-permute-start | bytes 393224 | tf_op jit(solution)/shard_map/ppermute | solution.py:401
  57.2 0.1 shard_map.92
  57.3 3.0 %collective-permute-start.15 = (bf16[2,128,512]{2,1,0:T(8,128)(2,1)S(1)}, bf16[2,128,512]{2,1,0:T(8,128)(2,1)S(1)}, u32[]{:S(2)}, u32[]{:S(2)}) collective-permute-start(bf16[2,128,512]{2,1,0:T(8,128)(2,1)S(1)} %get-tuple-element.107), channel_id=1, source_target_pairs={{0,4},{4,0},{1,5},{5,1},{2,6},{6,2},{3,7},{7,3},{8,12},{12,8},{9,1... | collective-permute-start | bytes 786440 | tf_op jit(solution)/shard_map/ppermute | solution.py:396
  60.4 1.5 %collective-permute-done.19.refs_2_ = bf16[2,256,128]{2,1,0:T(8,128)(2,1)S(1)} collective-permute-done((bf16[2,256,128]{2,1,0:T(8,128)(2,1)S(1)}, bf16[2,256,128]{2,1,0:T(8,128)(2,1)S(1)}, u32[]{:S(2)}, u32[]{:S(2)}) %collective-permute-start.19) | collective-permute-done | bytes 131104 | tf_op jit(solution)/shard_map/ppermute | solution.py:401
  61.9 0.7 %collective-permute-done.20.refs_3_ = bf16[2,256,128]{2,1,0:T(8,128)(2,1)S(1)} collective-permute-done((bf16[2,256,128]{2,1,0:T(8,128)(2,1)S(1)}, bf16[2,256,128]{2,1,0:T(8,128)(2,1)S(1)}, u32[]{:S(2)}, u32[]{:S(2)}) %collective-permute-start.20) | collective-permute-done | bytes 131104 | tf_op jit(solution)/shard_map/ppermute | solution.py:401
  62.6 0.1 shard_map.95
  62.7 2.0 %collective-permute-start.21 = (bf16[2,128,512]{2,1,0:T(8,128)(2,1)S(1)}, bf16[2,128,512]{2,1,0:T(8,128)(2,1)S(1)}, u32[]{:S(2)}, u32[]{:S(2)}) collective-permute-start(bf16[2,128,512]{2,1,0:T(8,128)(2,1)S(1)} %get-tuple-element.119), channel_id=1, source_target_pairs={{0,4},{4,0},{1,5},{5,1},{2,6},{6,2},{3,7},{7,3},{8,12},{12,8},{9,1... | collective-permute-start | bytes 786440 | tf_op jit(solution)/shard_map/ppermute | solution.py:396
  64.7 0.8 %shard_map.93 = (bf16[128,1024]{1,0:T(8,128)(2,1)}, bf16[128,1024]{1,0:T(8,128)(2,1)}) custom-call(bf16[2,128,512]{2,1,0:T(8,128)(2,1)S(1)} %get-tuple-element.106.own, bf16[2,128,512]{2,1,0:T(8,128)(2,1)S(1)} %collective-permute-done.15.got), custom_call_target="tpu_custom_call" | custom-call | tf_op jit(solution)/shard_map/pallas_call | solution.py:479
  65.6 0.3 collective-permute-done.21.got
  65.9 0.8 %shard_map.96 = (bf16[128,1024]{1,0:T(8,128)(2,1)}, bf16[128,1024]{1,0:T(8,128)(2,1)}) custom-call(bf16[2,128,512]{2,1,0:T(8,128)(2,1)S(1)} %get-tuple-element.118.own, bf16[2,128,512]{2,1,0:T(8,128)(2,1)S(1)} %collective-permute-done.21.got), custom_call_target="tpu_custom_call" | custom-call | tf_op jit(solution)/shard_map/pallas_call | solution.py:479
  (19 shorter events, 0.1 us)
Async XLA Ops:
  0.6 10.5 %copy-start = (f32[1024]{0:T(1024)S(1)}, f32[1024]{0:T(1024)}, u32[]{:S(2)}) copy-start(f32[1024]{0:T(1024)} %param.8) | copy-start | bytes 12292
  0.6 2.4 %collective-permute-start.5 = (bf16[128,1024]{1,0:T(8,128)(2,1)}, bf16[128,1024]{1,0:T(8,128)(2,1)S(1)}, u32[]{:S(2)}, u32[]{:S(2)}) collective-permute-start(bf16[128,1024]{1,0:T(8,128)(2,1)} %param.6), channel_id=1, source_target_pairs={{0,4},{4,0},{1,5},{5,1},{2,6},{6,2},{3,7},{7,3},{8,12},{12,8},{9,1... | collective-permute-start | bytes 786440 | tf_op jit(solution)/shard_map/ppermute | solution.py:396
  1.4 1.7 %collective-permute-start.6 = (bf16[128,1024]{1,0:T(8,128)(2,1)}, bf16[128,1024]{1,0:T(8,128)(2,1)S(1)}, u32[]{:S(2)}, u32[]{:S(2)}) collective-permute-start(bf16[128,1024]{1,0:T(8,128)(2,1)} %param.7), channel_id=1, source_target_pairs={{0,4},{4,0},{1,5},{5,1},{2,6},{6,2},{3,7},{7,3},{8,12},{12,8},{9,1... | collective-permute-start | bytes 786440 | tf_op jit(solution)/shard_map/ppermute | solution.py:396
  1.5 5.6 %collective-permute-start = (bf16[128,1024]{1,0:T(8,128)(2,1)}, bf16[128,1024]{1,0:T(8,128)(2,1)S(1)}, u32[]{:S(2)}, u32[]{:S(2)}) collective-permute-start(bf16[128,1024]{1,0:T(8,128)(2,1)} %param.5), channel_id=1, source_target_pairs={{0,4},{4,0},{1,5},{5,1},{2,6},{6,2},{3,7},{7,3},{8,12},{12,8},{9,1... | collective-permute-start | bytes 786440 | tf_op jit(solution)/shard_map/ppermute | solution.py:396
  1.9 5.2 %collective-permute-start.1 = (bf16[128,1024]{1,0:T(8,128)(2,1)}, bf16[128,1024]{1,0:T(8,128)(2,1)S(1)}, u32[]{:S(2)}, u32[]{:S(2)}) collective-permute-start(bf16[128,1024]{1,0:T(8,128)(2,1)} %param.9), channel_id=1, source_target_pairs={{0,4},{4,0},{1,5},{5,1},{2,6},{6,2},{3,7},{7,3},{8,12},{12,8},{9,1... | collective-permute-start | bytes 786440 | tf_op jit(solution)/shard_map/ppermute | solution.py:396
  3.2 2.9 %copy-start.1 = (bf16[128,1024]{1,0:T(8,128)(2,1)S(1)}, bf16[128,1024]{1,0:T(8,128)(2,1)}, u32[]{:S(2)}) copy-start(bf16[128,1024]{1,0:T(8,128)(2,1)} %param.5) | copy-start | bytes 786436
  3.2 2.9 %copy-start.2 = (bf16[128,1024]{1,0:T(8,128)(2,1)S(1)}, bf16[128,1024]{1,0:T(8,128)(2,1)}, u32[]{:S(2)}) copy-start(bf16[128,1024]{1,0:T(8,128)(2,1)} %param.9) | copy-start | bytes 786436
  3.3 7.9 %collective-permute-start.7 = (bf16[2,256,128]{2,1,0:T(8,128)(2,1)S(1)}, bf16[2,256,128]{2,1,0:T(8,128)(2,1)S(1)}, u32[]{:S(2)}, u32[]{:S(2)}) collective-permute-start(bf16[2,256,128]{2,1,0:T(8,128)(2,1)S(1)} %get-tuple-element.69), channel_id=1, source_target_pairs={{0,16},{8,24},{16,0},{24,8},{1,17},{9,25},{17,1},{25,9},{2,18},{10... | collective-permute-start | bytes 393224 | tf_op jit(solution)/shard_map/ppermute | solution.py:401
  6.1 6.2 %collective-permute-start.8 = (bf16[2,256,128]{2,1,0:T(8,128)(2,1)S(1)}, bf16[2,256,128]{2,1,0:T(8,128)(2,1)S(1)}, u32[]{:S(2)}, u32[]{:S(2)}) collective-permute-start(bf16[2,256,128]{2,1,0:T(8,128)(2,1)S(1)} %get-tuple-element.70), channel_id=1, source_target_pairs={{0,24},{8,16},{16,8},{24,0},{1,25},{9,17},{17,9},{25,1},{2,26},{10... | collective-permute-start | bytes 393224 | tf_op jit(solution)/shard_map/ppermute | solution.py:401
  7.1 5.4 %collective-permute-start.9 = (bf16[2,256,128]{2,1,0:T(8,128)(2,1)S(1)}, bf16[2,256,128]{2,1,0:T(8,128)(2,1)S(1)}, u32[]{:S(2)}, u32[]{:S(2)}) collective-permute-start(bf16[2,256,128]{2,1,0:T(8,128)(2,1)S(1)} %get-tuple-element.71), channel_id=1, source_target_pairs={{0,8},{8,0},{16,24},{24,16},{1,9},{9,1},{17,25},{25,17},{2,10},{10... | collective-permute-start | bytes 393224 | tf_op jit(solution)/shard_map/ppermute | solution.py:401
  7.2 9.2 %collective-permute-start.2 = (bf16[2,256,128]{2,1,0:T(8,128)(2,1)S(1)}, bf16[2,256,128]{2,1,0:T(8,128)(2,1)S(1)}, u32[]{:S(2)}, u32[]{:S(2)}) collective-permute-start(bf16[2,256,128]{2,1,0:T(8,128)(2,1)S(1)} %get-tuple-element.64), channel_id=1, source_target_pairs={{0,16},{8,24},{16,0},{24,8},{1,17},{9,25},{17,1},{25,9},{2,18},{10... | collective-permute-start | bytes 393224 | tf_op jit(solution)/shard_map/ppermute | solution.py:401
  10.3 7.4 %collective-permute-start.3 = (bf16[2,256,128]{2,1,0:T(8,128)(2,1)S(1)}, bf16[2,256,128]{2,1,0:T(8,128)(2,1)S(1)}, u32[]{:S(2)}, u32[]{:S(2)}) collective-permute-start(bf16[2,256,128]{2,1,0:T(8,128)(2,1)S(1)} %get-tuple-element.65), channel_id=1, source_target_pairs={{0,24},{8,16},{16,8},{24,0},{1,25},{9,17},{17,9},{25,1},{2,26},{10... | collective-permute-start | bytes 393224 | tf_op jit(solution)/shard_map/ppermute | solution.py:401
  11.2 7.0 %collective-permute-start.4 = (bf16[2,256,128]{2,1,0:T(8,128)(2,1)S(1)}, bf16[2,256,128]{2,1,0:T(8,128)(2,1)S(1)}, u32[]{:S(2)}, u32[]{:S(2)}) collective-permute-start(bf16[2,256,128]{2,1,0:T(8,128)(2,1)S(1)} %get-tuple-element.66), channel_id=1, source_target_pairs={{0,8},{8,0},{16,24},{24,16},{1,9},{9,1},{17,25},{25,17},{2,10},{10... | collective-permute-start | bytes 393224 | tf_op jit(solution)/shard_map/ppermute | solution.py:401
  12.8 6.6 %collective-permute-start.11 = (bf16[2,128,128]{2,1,0:T(8,128)(2,1)S(1)}, bf16[2,128,128]{2,1,0:T(8,128)(2,1)S(1)}, u32[]{:S(2)}, u32[]{:S(2)}) collective-permute-start(bf16[2,128,128]{2,1,0:T(8,128)(2,1)S(1)} %get-tuple-element.81), channel_id=1, source_target_pairs={{32,64},{96,128},{160,192},{64,32},{128,96},{192,160},{33,65},{97,... | collective-permute-start | bytes 196616 | tf_op jit(solution)/shard_map/ppermute | solution.py:392
  16.3 4.1 %collective-permute-start.10 = (bf16[4,128,128]{2,1,0:T(8,128)(2,1)S(1)}, bf16[4,128,128]{2,1,0:T(8,128)(2,1)S(1)}, u32[]{:S(2)}, u32[]{:S(2)}) collective-permute-start(bf16[4,128,128]{2,1,0:T(8,128)(2,1)S(1)} %get-tuple-element.80), channel_id=1, source_target_pairs={{0,32},{32,0},{64,96},{96,64},{128,160},{160,128},{192,224},{224,1... | collective-permute-start | bytes 393224 | tf_op jit(solution)/shard_map/ppermute | solution.py:387
  41.7 11.2 %collective-permute-start.16 = (bf16[4,128,128]{2,1,0:T(8,128)(2,1)S(1)}, bf16[4,128,128]{2,1,0:T(8,128)(2,1)S(1)}, u32[]{:S(2)}, u32[]{:S(2)}) collective-permute-start(bf16[4,128,128]{2,1,0:T(8,128)(2,1)S(1)} %get-tuple-element.112), channel_id=1, source_target_pairs={{0,32},{32,0},{64,96},{96,64},{128,160},{160,128},{192,224},{224,1... | collective-permute-start | bytes 393224 | tf_op jit(solution)/shard_map/ppermute | solution.py:387
  43.3 13.9 %collective-permute-start.12 = (bf16[2,256,128]{2,1,0:T(8,128)(2,1)S(1)}, bf16[2,256,128]{2,1,0:T(8,128)(2,1)S(1)}, u32[]{:S(2)}, u32[]{:S(2)}) collective-permute-start(bf16[2,256,128]{2,1,0:T(8,128)(2,1)S(1)} %get-tuple-element.103), channel_id=1, source_target_pairs={{0,16},{8,24},{16,0},{24,8},{1,17},{9,25},{17,1},{25,9},{2,18},{10... | collective-permute-start | bytes 393224 | tf_op jit(solution)/shard_map/ppermute | solution.py:401
  44.7 8.2 %collective-permute-start.17 = (bf16[2,128,128]{2,1,0:T(8,128)(2,1)S(1)}, bf16[2,128,128]{2,1,0:T(8,128)(2,1)S(1)}, u32[]{:S(2)}, u32[]{:S(2)}) collective-permute-start(bf16[2,128,128]{2,1,0:T(8,128)(2,1)S(1)} %get-tuple-element.113), channel_id=1, source_target_pairs={{32,64},{96,128},{160,192},{64,32},{128,96},{192,160},{33,65},{97,... | collective-permute-start | bytes 196616 | tf_op jit(solution)/shard_map/ppermute | solution.py:392
  51.1 6.2 %collective-permute-start.13 = (bf16[2,256,128]{2,1,0:T(8,128)(2,1)S(1)}, bf16[2,256,128]{2,1,0:T(8,128)(2,1)S(1)}, u32[]{:S(2)}, u32[]{:S(2)}) collective-permute-start(bf16[2,256,128]{2,1,0:T(8,128)(2,1)S(1)} %get-tuple-element.104), channel_id=1, source_target_pairs={{0,24},{8,16},{16,8},{24,0},{1,25},{9,17},{17,9},{25,1},{2,26},{10... | collective-permute-start | bytes 393224 | tf_op jit(solution)/shard_map/ppermute | solution.py:401
  52.9 4.4 %collective-permute-start.14 = (bf16[2,256,128]{2,1,0:T(8,128)(2,1)S(1)}, bf16[2,256,128]{2,1,0:T(8,128)(2,1)S(1)}, u32[]{:S(2)}, u32[]{:S(2)}) collective-permute-start(bf16[2,256,128]{2,1,0:T(8,128)(2,1)S(1)} %get-tuple-element.105), channel_id=1, source_target_pairs={{0,8},{8,0},{16,24},{24,16},{1,9},{9,1},{17,25},{25,17},{2,10},{10... | collective-permute-start | bytes 393224 | tf_op jit(solution)/shard_map/ppermute | solution.py:401
  53.3 7.1 %collective-permute-start.18 = (bf16[2,256,128]{2,1,0:T(8,128)(2,1)S(1)}, bf16[2,256,128]{2,1,0:T(8,128)(2,1)S(1)}, u32[]{:S(2)}, u32[]{:S(2)}) collective-permute-start(bf16[2,256,128]{2,1,0:T(8,128)(2,1)S(1)} %get-tuple-element.115), channel_id=1, source_target_pairs={{0,16},{8,24},{16,0},{24,8},{1,17},{9,25},{17,1},{25,9},{2,18},{10... | collective-permute-start | bytes 393224 | tf_op jit(solution)/shard_map/ppermute | solution.py:401
  55.5 6.4 %collective-permute-start.19 = (bf16[2,256,128]{2,1,0:T(8,128)(2,1)S(1)}, bf16[2,256,128]{2,1,0:T(8,128)(2,1)S(1)}, u32[]{:S(2)}, u32[]{:S(2)}) collective-permute-start(bf16[2,256,128]{2,1,0:T(8,128)(2,1)S(1)} %get-tuple-element.116), channel_id=1, source_target_pairs={{0,24},{8,16},{16,8},{24,0},{1,25},{9,17},{17,9},{25,1},{2,26},{10... | collective-permute-start | bytes 393224 | tf_op jit(solution)/shard_map/ppermute | solution.py:401
  57.2 5.4 %collective-permute-start.20 = (bf16[2,256,128]{2,1,0:T(8,128)(2,1)S(1)}, bf16[2,256,128]{2,1,0:T(8,128)(2,1)S(1)}, u32[]{:S(2)}, u32[]{:S(2)}) collective-permute-start(bf16[2,256,128]{2,1,0:T(8,128)(2,1)S(1)} %get-tuple-element.117), channel_id=1, source_target_pairs={{0,8},{8,0},{16,24},{24,16},{1,9},{9,1},{17,25},{25,17},{2,10},{10... | collective-permute-start | bytes 393224 | tf_op jit(solution)/shard_map/ppermute | solution.py:401
  57.3 7.4 %collective-permute-start.15 = (bf16[2,128,512]{2,1,0:T(8,128)(2,1)S(1)}, bf16[2,128,512]{2,1,0:T(8,128)(2,1)S(1)}, u32[]{:S(2)}, u32[]{:S(2)}) collective-permute-start(bf16[2,128,512]{2,1,0:T(8,128)(2,1)S(1)} %get-tuple-element.107), channel_id=1, source_target_pairs={{0,4},{4,0},{1,5},{5,1},{2,6},{6,2},{3,7},{7,3},{8,12},{12,8},{9,1... | collective-permute-start | bytes 786440 | tf_op jit(solution)/shard_map/ppermute | solution.py:396
  62.7 3.2 %collective-permute-start.21 = (bf16[2,128,512]{2,1,0:T(8,128)(2,1)S(1)}, bf16[2,128,512]{2,1,0:T(8,128)(2,1)S(1)}, u32[]{:S(2)}, u32[]{:S(2)}) collective-permute-start(bf16[2,128,512]{2,1,0:T(8,128)(2,1)S(1)} %get-tuple-element.119), channel_id=1, source_target_pairs={{0,4},{4,0},{1,5},{5,1},{2,6},{6,2},{3,7},{7,3},{8,12},{12,8},{9,1... | collective-permute-start | bytes 786440 | tf_op jit(solution)/shard_map/ppermute | solution.py:396

commit v4 on v3

--- a/solution.py
+++ b/solution.py
@@ -218,8 +218,8 @@
         scaled = d[rows(b), :].astype(F32) * gain[...]
         for i, one in enumerate((column(flat * flat), column(scaled * flat))):
             columns = jnp.where(lane == i * GROUP + b, one, columns)
-    turned = columns.T[: 2 * GROUP].reshape(1, 2, GROUP, BLOCK)
-    stats[...] = jnp.broadcast_to(turned, stats.shape)
+    turned = columns.T[: 2 * GROUP].astype(BF16)
+    stats[...] = jnp.broadcast_to(turned[None], stats.shape)
 
 
 def slopes_of(items):
@@ -238,7 +238,8 @@
     buf, buf2,
 ):
     odd = lax.rem(lax.axis_index("z"), 2) == 1
-    sums = jnp.sum(stats[...], axis=0) * (1.0 / features)
+    sums = jnp.sum(stats[...].astype(F32), axis=0) * (1.0 / features)
+    sums = sums.reshape(2, GROUP, BLOCK)
     inv_row = lax.rsqrt(sums[0] + EPS)
     drop_row = inv_row * inv_row * inv_row * sums[1]
     for b in range(GROUP):
@@ -295,7 +296,7 @@
 
 def backward_inner_kernel(
     q, k, v, qp, kp, vp, w_mid, w_coarse, w_edge, g0, gc, off0, offc, sl_edge, q_edge, q_top, out,
-    k_grad, v_grad, m0, m1, m2, m3,
+    pair, other, k_grad, v_grad, m0, m1, m2, m3, pair_out, other_out,
     sl_mid, sl_coarse, buf, grads, q_grad,
 ):
     coarse = slopes_of([
@@ -320,6 +321,8 @@
             part = nn(inner[b - 1], k[rows(b - 1, 3), :]) * SCALE
         q_grad[rows(b), :] = (part + buf[rows(b), :]).astype(BF16)
 
+    pair_out[...] = pair[...]
+    other_out[...] = other[...]
     for at, message in zip(places(), (m0, m1, m2, m3)):
         message[0] = out[at, :]
         message[1] = q_grad[at, :]
@@ -449,7 +452,7 @@
     )(q, k, v, qp, kp, vp)
     attn, stats, w_edge, w_top, share, share1, share2, edge_k, edge_v = call(
         forward_edge_kernel,
-        [whole, ((partners, 2, GROUP, DH), F32), w_edges, w_tops] + shares + [edge_sets] * 2,
+        [whole, ((partners, 2 * GROUP, DH), BF16), w_edges, w_tops] + shares + [edge_sets] * 2,
         11,
         [((3 * BLOCK, DH), F32)] * 3 + [whole_f] * 3,
     )(q, k, v, d, qp, pair, other, my_gain, *inner)
@@ -464,14 +467,15 @@
         14,
         [whole_f] * 2,
     )(stats, d, my_gain, attn, share, share1, share2, q, qp, pair, edge_k, edge_v, w_edge, w_top)
-    pair_back, other_back = swap_pair(pair_back), swap_other(other_back)
-    k_grad, v_grad, *messages = call(
+    k_grad, v_grad, *messages, pair_back, other_back = call(
         backward_inner_kernel,
-        [whole_f, whole_f] + [part] * CHIPS,
-        17,
+        [whole_f, whole_f] + [part] * CHIPS + [message, edge],
+        19,
         [w_mids, w_coarses, whole_f, coarse_f, whole],
         flops=2 * FLOPS,
-    )(q, k, v, qp, kp, vp, w_mid, w_coarse, w_edge, g0, gc, off0, offc, sl_edge, q_edge, q_top, out)
+    )(q, k, v, qp, kp, vp, w_mid, w_coarse, w_edge, g0, gc, off0, offc, sl_edge, q_edge, q_top, out,
+      pair_back, other_back)
+    pair_back, other_back = swap_pair(pair_back), swap_other(other_back)
 
     def deliver(messages):
         own, away = call(regroup_kernel, [half] * 2, CHIPS)(*swap_chips(messages))

time: 67.1 us -> 65.6 us (0.978)
  blocking collectives: 18.9 us -> 17.6 us
    all_to_all x1, blocking collectives: 18.9 us -> 17.6 us  [exchange(): return lax.all_to_all(x, axes, 0, 0, tiled=True)]
  transfers between devices with their start and end apart: 22 -> 22, of which waited for: 9 -> 9; matrix products, arithmetic and copies ran while one was open for 2% -> 2% of each run, Pallas kernels for 7% -> 5%
where the time goes in v4:
time: 65.6 us; the launch traced here: 65.4 us
  starting transfers between devices  31 us (47%)
  blocking collectives  17.6 us (27%)
  Pallas kernels  7.79 us (12%)
  waiting for transfers between devices  6.83 us (10%)
  local copies, waits for them, and re-layouts  1.1 us (2%)
  between operations  0.97 us (1%)
    all_to_all x1, blocking collectives, exchange(): return lax.all_to_all(x, axes, 0, 0, tiled=True)  17.6 us
    ppermute x12, starting transfers between devices, swap_chips(): lax.ppermute(message, 'x', [(i, i ^ step) for i in range(CHIPS)])  14.8 us
    ppermute x2, starting transfers between devices, swap_other(): lax.ppermute(x, 'z', up + [(target, source) for source, target in up])  9.65 us
    ppermute x6, starting transfers between devices, swap_core(): return lax.ppermute(x, 'c', [(0, 1), (1, 0)])  6.43 us
    ppermute x12, waiting for transfers between devices, swap_chips(): lax.ppermute(message, 'x', [(i, i ^ step) for i in range(CHIPS)])  5.24 us
    pallas_call x2, Pallas kernels, deliver(): return finish(own, swap_core(away))  1.63 us
    pallas_call x1, Pallas kernels, local(): call(backward_inner_kernel, [whole_f, whole_f] + [part] * CHIPS + [messag...  1.54 us
  transfers between devices with their start and end apart: 22, of which 9 were waited for; matrix products, arithmetic and copies ran while one was open for 2% of the time, Pallas kernels for 5%

profile of v4, /device:TPU:33, one launch (start us, length us, event | category | flops | bytes accessed | tf_op | source)
XLA Modules:
  0.0 65.4 jit_solution(14619763818043712603)
XLA Ops:
  0.6 0.0 copy-start
  0.6 0.8 %collective-permute-start.5 = (bf16[128,1024]{1,0:T(8,128)(2,1)}, bf16[128,1024]{1,0:T(8,128)(2,1)S(1)}, u32[]{:S(2)}, u32[]{:S(2)}) collective-permute-start(bf16[128,1024]{1,0:T(8,128)(2,1)} %param.6), channel_id=1, source_target_pairs={{0,4},{4,0},{1,5},{5,1},{2,6},{6,2},{3,7},{7,3},{8,12},{12,8},{9,1... | collective-permute-start | bytes 786440 | tf_op jit(solution)/shard_map/ppermute | solution.py:399
  1.4 0.1 collective-permute-start.6
  1.5 0.4 collective-permute-start
  1.9 0.1 collective-permute-start.1
  2.0 1.0 %constant_dynamic-slice_fusion = (bf16[128,512]{1,0:T(8,128)(2,1)S(1)}, bf16[128,512]{1,0:T(8,128)(2,1)S(1)}) fusion(bf16[128,1024]{1,0:T(8,128)(2,1)} %param.7, s32[]{:T(128)S(6)} %select_n.4, bf16[128,1024]{1,0:T(8,128)(2,1)} %param.6), kind=kLoop, calls=%fused_computation | loop fusion | bytes 524292 | tf_op jit(solution)/shard_map/dynamic_slice | solution.py:440
  3.0 0.1 collective-permute-done.6.got_y
  3.2 0.1 shard_map.86
  3.3 2.8 %collective-permute-start.7 = (bf16[2,256,128]{2,1,0:T(8,128)(2,1)S(1)}, bf16[2,256,128]{2,1,0:T(8,128)(2,1)S(1)}, u32[]{:S(2)}, u32[]{:S(2)}) collective-permute-start(bf16[2,256,128]{2,1,0:T(8,128)(2,1)S(1)} %get-tuple-element.71), channel_id=1, source_target_pairs={{0,16},{8,24},{16,0},{24,8},{1,17},{9,25},{17,1},{25,9},{2,18},{10... | collective-permute-start | bytes 393224 | tf_op jit(solution)/shard_map/ppermute | solution.py:404
  6.1 0.9 %collective-permute-start.8 = (bf16[2,256,128]{2,1,0:T(8,128)(2,1)S(1)}, bf16[2,256,128]{2,1,0:T(8,128)(2,1)S(1)}, u32[]{:S(2)}, u32[]{:S(2)}) collective-permute-start(bf16[2,256,128]{2,1,0:T(8,128)(2,1)S(1)} %get-tuple-element.72), channel_id=1, source_target_pairs={{0,24},{8,16},{16,8},{24,0},{1,25},{9,17},{17,9},{25,1},{2,26},{10... | collective-permute-start | bytes 393224 | tf_op jit(solution)/shard_map/ppermute | solution.py:404
  7.1 0.0 collective-permute-done.got_x
  7.1 0.0 collective-permute-done.1.got_y
  7.1 0.1 shard_map.84
  7.2 3.1 %collective-permute-start.2 = (bf16[2,256,128]{2,1,0:T(8,128)(2,1)S(1)}, bf16[2,256,128]{2,1,0:T(8,128)(2,1)S(1)}, u32[]{:S(2)}, u32[]{:S(2)}) collective-permute-start(bf16[2,256,128]{2,1,0:T(8,128)(2,1)S(1)} %get-tuple-element.66), channel_id=1, source_target_pairs={{0,16},{8,24},{16,0},{24,8},{1,17},{9,25},{17,1},{25,9},{2,18},{10... | collective-permute-start | bytes 393224 | tf_op jit(solution)/shard_map/ppermute | solution.py:404
  10.3 0.9 %collective-permute-start.3 = (bf16[2,256,128]{2,1,0:T(8,128)(2,1)S(1)}, bf16[2,256,128]{2,1,0:T(8,128)(2,1)S(1)}, u32[]{:S(2)}, u32[]{:S(2)}) collective-permute-start(bf16[2,256,128]{2,1,0:T(8,128)(2,1)S(1)} %get-tuple-element.67), channel_id=1, source_target_pairs={{0,24},{8,16},{16,8},{24,0},{1,25},{9,17},{17,9},{25,1},{2,26},{10... | collective-permute-start | bytes 393224 | tf_op jit(solution)/shard_map/ppermute | solution.py:404
  11.2 0.0 collective-permute-done.7.refs_1_
  11.2 0.0 collective-permute-start.4
  11.2 0.1 dynamic-slice_bitcast_fusion.gain.refs_2_
  11.2 1.1 %collective-permute-done.8.refs_2_ = bf16[2,256,128]{2,1,0:T(8,128)(2,1)S(1)} collective-permute-done((bf16[2,256,128]{2,1,0:T(8,128)(2,1)S(1)}, bf16[2,256,128]{2,1,0:T(8,128)(2,1)S(1)}, u32[]{:S(2)}, u32[]{:S(2)}) %collective-permute-start.8) | collective-permute-done | bytes 131104 | tf_op jit(solution)/shard_map/ppermute | solution.py:404
  12.3 0.2 collective-permute-done.9.refs_3_
  12.5 0.3 shard_map.87
  12.8 3.5 %collective-permute-start.11 = (bf16[2,128,128]{2,1,0:T(8,128)(2,1)S(1)}, bf16[2,128,128]{2,1,0:T(8,128)(2,1)S(1)}, u32[]{:S(2)}, u32[]{:S(2)}) collective-permute-start(bf16[2,128,128]{2,1,0:T(8,128)(2,1)S(1)} %get-tuple-element.83), channel_id=1, source_target_pairs={{32,64},{96,128},{160,192},{64,32},{128,96},{192,160},{33,65},{97,... | collective-permute-start | bytes 196616 | tf_op jit(solution)/shard_map/ppermute | solution.py:395
  16.3 0.1 collective-permute-start.10
  16.4 1.3 %collective-permute-done.3.refs_2_ = bf16[2,256,128]{2,1,0:T(8,128)(2,1)S(1)} collective-permute-done((bf16[2,256,128]{2,1,0:T(8,128)(2,1)S(1)}, bf16[2,256,128]{2,1,0:T(8,128)(2,1)S(1)}, u32[]{:S(2)}, u32[]{:S(2)}) %collective-permute-start.3) | collective-permute-done | bytes 131104 | tf_op jit(solution)/shard_map/ppermute | solution.py:404
  17.7 0.5 collective-permute-done.4.refs_3_
  18.2 0.1 shard_map.85
  18.3 1.0 %shard_map.88 = (bf16[768,384]{1,0:T(8,128)(2,1)S(1)}, bf16[768,128]{1,0:T(8,128)(2,1)S(1)}, f32[1536,128]{1,0:T(8,128)S(1)}, f32[1536,128]{1,0:T(8,128)S(1)}, f32[1536,128]{1,0:T(8,128)S(1)}) custom-call(bf16[1024,128]{1,0:T(8,128)(2,1)S(1)} %get-tuple-element.69.q.refs_7_, bf16[1024,128]{1,0:T(8,128)(2,1)S(1)} %get-tuple-element.74.k, ...), custom_call_target="tpu_custom_call" | custom-call | flops 4000000000 | tf_op jit(solution)/shard_map/pallas_call | solution.py:450
  19.4 1.1 %collective-permute-done.10.pair.refs_9_ = bf16[4,128,128]{2,1,0:T(8,128)(2,1)S(1)} collective-permute-done((bf16[4,128,128]{2,1,0:T(8,128)(2,1)S(1)}, bf16[4,128,128]{2,1,0:T(8,128)(2,1)S(1)}, u32[]{:S(2)}, u32[]{:S(2)}) %collective-permute-start.10) | collective-permute-done | bytes 131104 | tf_op jit(solution)/shard_map/ppermute | solution.py:390
  20.5 1.3 %shard_map.89 = (bf16[1024,128]{1,0:T(8,128)(2,1)S(1)}, bf16[32,16,128]{2,1,0:T(8,128)(2,1)S(1)}, bf16[256,384]{1,0:T(8,128)(2,1)S(1)}, bf16[128,128]{1,0:T(8,12...) custom-call(bf16[1024,128]{1,0:T(8,128)(2,1)S(1)} %get-tuple-element, ...), custom_call_target="tpu_custom_call" | custom-call | tf_op jit(solution)/shard_map/pallas_call | solution.py:453
  21.8 17.6 %all_to_all.5.refs_0_ = bf16[32,16,128]{2,1,0:T(8,128)(2,1)S(1)} all-to-all(bf16[32,16,128]{2,1,0:T(8,128)(2,1)S(1)} %get-tuple-element.88), channel_id=1, replica_groups=mesh['z'=8,'x'=4,'c'=2,'head'=4] {'x','c','head'}, dimensions={0} | all-to-all | bytes 262144 | tf_op jit(solution)/shard_map/all_to_all | solution.py:410
  39.4 1.1 %shard_map.90 = (bf16[1024,128]{1,0:T(8,128)(2,1)S(1)}, bf16[4,128,128]{2,1,0:T(8,128)(2,1)S(1)}, bf16[2,128,128]{2,1,0:T(8,128)(2,1)S(1)}, bf16[1024,128]{1,0:T...) custom-call(bf16[32,16,128]{2,1,0:T(8,128)(2,1)S(1)} %all_to_all.5.r, ...), custom_call_target="tpu_custom_call" | custom-call | tf_op jit(solution)/shard_map/pallas_call | solution.py:464
  40.5 1.5 %shard_map.91 = (f32[1024,128]{1,0:T(8,128)S(1)}, f32[1024,128]{1,0:T(8,128)S(1)}, bf16[2,256,128]{2,1,0:T(8,128)(2,1)S(1)}, bf16[2,256,128]{2,1,0:T(8,128)(2,1)...) custom-call(bf16[1024,128]{1,0:T(8,128)(2,1)S(1)} %get-tuple-element, ...), custom_call_target="tpu_custom_call" | custom-call | flops 8000000000 | tf_op jit(solution)/shard_map/pallas_call | solution.py:470
  42.0 0.1 collective-permute-start.16
  42.1 1.3 %collective-permute-start.12 = (bf16[2,256,128]{2,1,0:T(8,128)(2,1)S(1)}, bf16[2,256,128]{2,1,0:T(8,128)(2,1)S(1)}, u32[]{:S(2)}, u32[]{:S(2)}) collective-permute-start(bf16[2,256,128]{2,1,0:T(8,128)(2,1)S(1)} %get-tuple-element.107), channel_id=1, source_target_pairs={{0,16},{8,24},{16,0},{24,8},{1,17},{9,25},{17,1},{25,9},{2,18},{10... | collective-permute-start | bytes 393224 | tf_op jit(solution)/shard_map/ppermute | solution.py:404
  43.4 6.1 %collective-permute-start.17 = (bf16[2,128,128]{2,1,0:T(8,128)(2,1)S(1)}, bf16[2,128,128]{2,1,0:T(8,128)(2,1)S(1)}, u32[]{:S(2)}, u32[]{:S(2)}) collective-permute-start(bf16[2,128,128]{2,1,0:T(8,128)(2,1)S(1)} %get-tuple-element.117), channel_id=1, source_target_pairs={{32,64},{96,128},{160,192},{64,32},{128,96},{192,160},{33,65},{97,... | collective-permute-start | bytes 196616 | tf_op jit(solution)/shard_map/ppermute | solution.py:395
  49.5 1.8 %collective-permute-start.13 = (bf16[2,256,128]{2,1,0:T(8,128)(2,1)S(1)}, bf16[2,256,128]{2,1,0:T(8,128)(2,1)S(1)}, u32[]{:S(2)}, u32[]{:S(2)}) collective-permute-start(bf16[2,256,128]{2,1,0:T(8,128)(2,1)S(1)} %get-tuple-element.108), channel_id=1, source_target_pairs={{0,24},{8,16},{16,8},{24,0},{1,25},{9,17},{17,9},{25,1},{2,26},{10... | collective-permute-start | bytes 393224 | tf_op jit(solution)/shard_map/ppermute | solution.py:404
  51.4 0.4 shard_map.94
  51.8 2.2 %collective-permute-start.18 = (bf16[2,256,128]{2,1,0:T(8,128)(2,1)S(1)}, bf16[2,256,128]{2,1,0:T(8,128)(2,1)S(1)}, u32[]{:S(2)}, u32[]{:S(2)}) collective-permute-start(bf16[2,256,128]{2,1,0:T(8,128)(2,1)S(1)} %get-tuple-element.119), channel_id=1, source_target_pairs={{0,16},{8,24},{16,0},{24,8},{1,17},{9,25},{17,1},{25,9},{2,18},{10... | collective-permute-start | bytes 393224 | tf_op jit(solution)/shard_map/ppermute | solution.py:404
  53.9 1.7 %collective-permute-start.19 = (bf16[2,256,128]{2,1,0:T(8,128)(2,1)S(1)}, bf16[2,256,128]{2,1,0:T(8,128)(2,1)S(1)}, u32[]{:S(2)}, u32[]{:S(2)}) collective-permute-start(bf16[2,256,128]{2,1,0:T(8,128)(2,1)S(1)} %get-tuple-element.120), channel_id=1, source_target_pairs={{0,24},{8,16},{16,8},{24,0},{1,25},{9,17},{17,9},{25,1},{2,26},{10... | collective-permute-start | bytes 393224 | tf_op jit(solution)/shard_map/ppermute | solution.py:404
  55.7 0.1 shard_map.92
  55.8 3.0 %collective-permute-start.15 = (bf16[2,128,512]{2,1,0:T(8,128)(2,1)S(1)}, bf16[2,128,512]{2,1,0:T(8,128)(2,1)S(1)}, u32[]{:S(2)}, u32[]{:S(2)}) collective-permute-start(bf16[2,128,512]{2,1,0:T(8,128)(2,1)S(1)} %get-tuple-element.111), channel_id=1, source_target_pairs={{0,4},{4,0},{1,5},{5,1},{2,6},{6,2},{3,7},{7,3},{8,12},{12,8},{9,1... | collective-permute-start | bytes 786440 | tf_op jit(solution)/shard_map/ppermute | solution.py:399
  58.8 1.4 %collective-permute-done.19.refs_2_ = bf16[2,256,128]{2,1,0:T(8,128)(2,1)S(1)} collective-permute-done((bf16[2,256,128]{2,1,0:T(8,128)(2,1)S(1)}, bf16[2,256,128]{2,1,0:T(8,128)(2,1)S(1)}, u32[]{:S(2)}, u32[]{:S(2)}) %collective-permute-start.19) | collective-permute-done | bytes 131104 | tf_op jit(solution)/shard_map/ppermute | solution.py:404
  60.2 0.8 %collective-permute-done.20.refs_3_ = bf16[2,256,128]{2,1,0:T(8,128)(2,1)S(1)} collective-permute-done((bf16[2,256,128]{2,1,0:T(8,128)(2,1)S(1)}, bf16[2,256,128]{2,1,0:T(8,128)(2,1)S(1)}, u32[]{:S(2)}, u32[]{:S(2)}) %collective-permute-start.20) | collective-permute-done | bytes 131104 | tf_op jit(solution)/shard_map/ppermute | solution.py:404
  61.1 0.1 shard_map.95
  61.2 2.0 %collective-permute-start.21 = (bf16[2,128,512]{2,1,0:T(8,128)(2,1)S(1)}, bf16[2,128,512]{2,1,0:T(8,128)(2,1)S(1)}, u32[]{:S(2)}, u32[]{:S(2)}) collective-permute-start(bf16[2,128,512]{2,1,0:T(8,128)(2,1)S(1)} %get-tuple-element.123), channel_id=1, source_target_pairs={{0,4},{4,0},{1,5},{5,1},{2,6},{6,2},{3,7},{7,3},{8,12},{12,8},{9,1... | collective-permute-start | bytes 786440 | tf_op jit(solution)/shard_map/ppermute | solution.py:399
  63.2 0.8 %shard_map.93 = (bf16[128,1024]{1,0:T(8,128)(2,1)}, bf16[128,1024]{1,0:T(8,128)(2,1)}) custom-call(bf16[2,128,512]{2,1,0:T(8,128)(2,1)S(1)} %get-tuple-element.110.own, bf16[2,128,512]{2,1,0:T(8,128)(2,1)S(1)} %collective-permute-done.15.got), custom_call_target="tpu_custom_call" | custom-call | tf_op jit(solution)/shard_map/pallas_call | solution.py:483
  64.0 0.3 collective-permute-done.21.got
  64.4 0.8 %shard_map.96 = (bf16[128,1024]{1,0:T(8,128)(2,1)}, bf16[128,1024]{1,0:T(8,128)(2,1)}) custom-call(bf16[2,128,512]{2,1,0:T(8,128)(2,1)S(1)} %get-tuple-element.122.own, bf16[2,128,512]{2,1,0:T(8,128)(2,1)S(1)} %collective-permute-done.21.got), custom_call_target="tpu_custom_call" | custom-call | tf_op jit(solution)/shard_map/pallas_call | solution.py:483
  (19 shorter events, 0.1 us)
Async XLA Ops:
  0.6 10.5 %copy-start = (f32[1024]{0:T(1024)S(1)}, f32[1024]{0:T(1024)}, u32[]{:S(2)}) copy-start(f32[1024]{0:T(1024)} %param.8) | copy-start | bytes 12292
  0.6 2.4 %collective-permute-start.5 = (bf16[128,1024]{1,0:T(8,128)(2,1)}, bf16[128,1024]{1,0:T(8,128)(2,1)S(1)}, u32[]{:S(2)}, u32[]{:S(2)}) collective-permute-start(bf16[128,1024]{1,0:T(8,128)(2,1)} %param.6), channel_id=1, source_target_pairs={{0,4},{4,0},{1,5},{5,1},{2,6},{6,2},{3,7},{7,3},{8,12},{12,8},{9,1... | collective-permute-start | bytes 786440 | tf_op jit(solution)/shard_map/ppermute | solution.py:399
  1.4 1.7 %collective-permute-start.6 = (bf16[128,1024]{1,0:T(8,128)(2,1)}, bf16[128,1024]{1,0:T(8,128)(2,1)S(1)}, u32[]{:S(2)}, u32[]{:S(2)}) collective-permute-start(bf16[128,1024]{1,0:T(8,128)(2,1)} %param.7), channel_id=1, source_target_pairs={{0,4},{4,0},{1,5},{5,1},{2,6},{6,2},{3,7},{7,3},{8,12},{12,8},{9,1... | collective-permute-start | bytes 786440 | tf_op jit(solution)/shard_map/ppermute | solution.py:399
  1.5 5.6 %collective-permute-start = (bf16[128,1024]{1,0:T(8,128)(2,1)}, bf16[128,1024]{1,0:T(8,128)(2,1)S(1)}, u32[]{:S(2)}, u32[]{:S(2)}) collective-permute-start(bf16[128,1024]{1,0:T(8,128)(2,1)} %param.5), channel_id=1, source_target_pairs={{0,4},{4,0},{1,5},{5,1},{2,6},{6,2},{3,7},{7,3},{8,12},{12,8},{9,1... | collective-permute-start | bytes 786440 | tf_op jit(solution)/shard_map/ppermute | solution.py:399
  1.9 5.2 %collective-permute-start.1 = (bf16[128,1024]{1,0:T(8,128)(2,1)}, bf16[128,1024]{1,0:T(8,128)(2,1)S(1)}, u32[]{:S(2)}, u32[]{:S(2)}) collective-permute-start(bf16[128,1024]{1,0:T(8,128)(2,1)} %param.9), channel_id=1, source_target_pairs={{0,4},{4,0},{1,5},{5,1},{2,6},{6,2},{3,7},{7,3},{8,12},{12,8},{9,1... | collective-permute-start | bytes 786440 | tf_op jit(solution)/shard_map/ppermute | solution.py:399
  3.2 2.9 %copy-start.1 = (bf16[128,1024]{1,0:T(8,128)(2,1)S(1)}, bf16[128,1024]{1,0:T(8,128)(2,1)}, u32[]{:S(2)}) copy-start(bf16[128,1024]{1,0:T(8,128)(2,1)} %param.5) | copy-start | bytes 786436
  3.2 2.9 %copy-start.2 = (bf16[128,1024]{1,0:T(8,128)(2,1)S(1)}, bf16[128,1024]{1,0:T(8,128)(2,1)}, u32[]{:S(2)}) copy-start(bf16[128,1024]{1,0:T(8,128)(2,1)} %param.9) | copy-start | bytes 786436
  3.3 7.9 %collective-permute-start.7 = (bf16[2,256,128]{2,1,0:T(8,128)(2,1)S(1)}, bf16[2,256,128]{2,1,0:T(8,128)(2,1)S(1)}, u32[]{:S(2)}, u32[]{:S(2)}) collective-permute-start(bf16[2,256,128]{2,1,0:T(8,128)(2,1)S(1)} %get-tuple-element.71), channel_id=1, source_target_pairs={{0,16},{8,24},{16,0},{24,8},{1,17},{9,25},{17,1},{25,9},{2,18},{10... | collective-permute-start | bytes 393224 | tf_op jit(solution)/shard_map/ppermute | solution.py:404
  6.1 6.2 %collective-permute-start.8 = (bf16[2,256,128]{2,1,0:T(8,128)(2,1)S(1)}, bf16[2,256,128]{2,1,0:T(8,128)(2,1)S(1)}, u32[]{:S(2)}, u32[]{:S(2)}) collective-permute-start(bf16[2,256,128]{2,1,0:T(8,128)(2,1)S(1)} %get-tuple-element.72), channel_id=1, source_target_pairs={{0,24},{8,16},{16,8},{24,0},{1,25},{9,17},{17,9},{25,1},{2,26},{10... | collective-permute-start | bytes 393224 | tf_op jit(solution)/shard_map/ppermute | solution.py:404
  7.1 5.4 %collective-permute-start.9 = (bf16[2,256,128]{2,1,0:T(8,128)(2,1)S(1)}, bf16[2,256,128]{2,1,0:T(8,128)(2,1)S(1)}, u32[]{:S(2)}, u32[]{:S(2)}) collective-permute-start(bf16[2,256,128]{2,1,0:T(8,128)(2,1)S(1)} %get-tuple-element.73), channel_id=1, source_target_pairs={{0,8},{8,0},{16,24},{24,16},{1,9},{9,1},{17,25},{25,17},{2,10},{10... | collective-permute-start | bytes 393224 | tf_op jit(solution)/shard_map/ppermute | solution.py:404
  7.2 9.2 %collective-permute-start.2 = (bf16[2,256,128]{2,1,0:T(8,128)(2,1)S(1)}, bf16[2,256,128]{2,1,0:T(8,128)(2,1)S(1)}, u32[]{:S(2)}, u32[]{:S(2)}) collective-permute-start(bf16[2,256,128]{2,1,0:T(8,128)(2,1)S(1)} %get-tuple-element.66), channel_id=1, source_target_pairs={{0,16},{8,24},{16,0},{24,8},{1,17},{9,25},{17,1},{25,9},{2,18},{10... | collective-permute-start | bytes 393224 | tf_op jit(solution)/shard_map/ppermute | solution.py:404
  10.3 7.4 %collective-permute-start.3 = (bf16[2,256,128]{2,1,0:T(8,128)(2,1)S(1)}, bf16[2,256,128]{2,1,0:T(8,128)(2,1)S(1)}, u32[]{:S(2)}, u32[]{:S(2)}) collective-permute-start(bf16[2,256,128]{2,1,0:T(8,128)(2,1)S(1)} %get-tuple-element.67), channel_id=1, source_target_pairs={{0,24},{8,16},{16,8},{24,0},{1,25},{9,17},{17,9},{25,1},{2,26},{10... | collective-permute-start | bytes 393224 | tf_op jit(solution)/shard_map/ppermute | solution.py:404
  11.2 7.0 %collective-permute-start.4 = (bf16[2,256,128]{2,1,0:T(8,128)(2,1)S(1)}, bf16[2,256,128]{2,1,0:T(8,128)(2,1)S(1)}, u32[]{:S(2)}, u32[]{:S(2)}) collective-permute-start(bf16[2,256,128]{2,1,0:T(8,128)(2,1)S(1)} %get-tuple-element.68), channel_id=1, source_target_pairs={{0,8},{8,0},{16,24},{24,16},{1,9},{9,1},{17,25},{25,17},{2,10},{10... | collective-permute-start | bytes 393224 | tf_op jit(solution)/shard_map/ppermute | solution.py:404
  12.8 6.6 %collective-permute-start.11 = (bf16[2,128,128]{2,1,0:T(8,128)(2,1)S(1)}, bf16[2,128,128]{2,1,0:T(8,128)(2,1)S(1)}, u32[]{:S(2)}, u32[]{:S(2)}) collective-permute-start(bf16[2,128,128]{2,1,0:T(8,128)(2,1)S(1)} %get-tuple-element.83), channel_id=1, source_target_pairs={{32,64},{96,128},{160,192},{64,32},{128,96},{192,160},{33,65},{97,... | collective-permute-start | bytes 196616 | tf_op jit(solution)/shard_map/ppermute | solution.py:395
  16.3 4.1 %collective-permute-start.10 = (bf16[4,128,128]{2,1,0:T(8,128)(2,1)S(1)}, bf16[4,128,128]{2,1,0:T(8,128)(2,1)S(1)}, u32[]{:S(2)}, u32[]{:S(2)}) collective-permute-start(bf16[4,128,128]{2,1,0:T(8,128)(2,1)S(1)} %get-tuple-element.82), channel_id=1, source_target_pairs={{0,32},{32,0},{64,96},{96,64},{128,160},{160,128},{192,224},{224,1... | collective-permute-start | bytes 393224 | tf_op jit(solution)/shard_map/ppermute | solution.py:390
  42.0 9.3 %collective-permute-start.16 = (bf16[4,128,128]{2,1,0:T(8,128)(2,1)S(1)}, bf16[4,128,128]{2,1,0:T(8,128)(2,1)S(1)}, u32[]{:S(2)}, u32[]{:S(2)}) collective-permute-start(bf16[4,128,128]{2,1,0:T(8,128)(2,1)S(1)} %get-tuple-element.116), channel_id=1, source_target_pairs={{0,32},{32,0},{64,96},{96,64},{128,160},{160,128},{192,224},{224,1... | collective-permute-start | bytes 393224 | tf_op jit(solution)/shard_map/ppermute | solution.py:390
  42.1 13.6 %collective-permute-start.12 = (bf16[2,256,128]{2,1,0:T(8,128)(2,1)S(1)}, bf16[2,256,128]{2,1,0:T(8,128)(2,1)S(1)}, u32[]{:S(2)}, u32[]{:S(2)}) collective-permute-start(bf16[2,256,128]{2,1,0:T(8,128)(2,1)S(1)} %get-tuple-element.107), channel_id=1, source_target_pairs={{0,16},{8,24},{16,0},{24,8},{1,17},{9,25},{17,1},{25,9},{2,18},{10... | collective-permute-start | bytes 393224 | tf_op jit(solution)/shard_map/ppermute | solution.py:404
  43.4 7.9 %collective-permute-start.17 = (bf16[2,128,128]{2,1,0:T(8,128)(2,1)S(1)}, bf16[2,128,128]{2,1,0:T(8,128)(2,1)S(1)}, u32[]{:S(2)}, u32[]{:S(2)}) collective-permute-start(bf16[2,128,128]{2,1,0:T(8,128)(2,1)S(1)} %get-tuple-element.117), channel_id=1, source_target_pairs={{32,64},{96,128},{160,192},{64,32},{128,96},{192,160},{33,65},{97,... | collective-permute-start | bytes 196616 | tf_op jit(solution)/shard_map/ppermute | solution.py:395
  49.5 6.2 %collective-permute-start.13 = (bf16[2,256,128]{2,1,0:T(8,128)(2,1)S(1)}, bf16[2,256,128]{2,1,0:T(8,128)(2,1)S(1)}, u32[]{:S(2)}, u32[]{:S(2)}) collective-permute-start(bf16[2,256,128]{2,1,0:T(8,128)(2,1)S(1)} %get-tuple-element.108), channel_id=1, source_target_pairs={{0,24},{8,16},{16,8},{24,0},{1,25},{9,17},{17,9},{25,1},{2,26},{10... | collective-permute-start | bytes 393224 | tf_op jit(solution)/shard_map/ppermute | solution.py:404
  51.3 4.4 %collective-permute-start.14 = (bf16[2,256,128]{2,1,0:T(8,128)(2,1)S(1)}, bf16[2,256,128]{2,1,0:T(8,128)(2,1)S(1)}, u32[]{:S(2)}, u32[]{:S(2)}) collective-permute-start(bf16[2,256,128]{2,1,0:T(8,128)(2,1)S(1)} %get-tuple-element.109), channel_id=1, source_target_pairs={{0,8},{8,0},{16,24},{24,16},{1,9},{9,1},{17,25},{25,17},{2,10},{10... | collective-permute-start | bytes 393224 | tf_op jit(solution)/shard_map/ppermute | solution.py:404
  51.8 7.1 %collective-permute-start.18 = (bf16[2,256,128]{2,1,0:T(8,128)(2,1)S(1)}, bf16[2,256,128]{2,1,0:T(8,128)(2,1)S(1)}, u32[]{:S(2)}, u32[]{:S(2)}) collective-permute-start(bf16[2,256,128]{2,1,0:T(8,128)(2,1)S(1)} %get-tuple-element.119), channel_id=1, source_target_pairs={{0,16},{8,24},{16,0},{24,8},{1,17},{9,25},{17,1},{25,9},{2,18},{10... | collective-permute-start | bytes 393224 | tf_op jit(solution)/shard_map/ppermute | solution.py:404
  53.9 6.3 %collective-permute-start.19 = (bf16[2,256,128]{2,1,0:T(8,128)(2,1)S(1)}, bf16[2,256,128]{2,1,0:T(8,128)(2,1)S(1)}, u32[]{:S(2)}, u32[]{:S(2)}) collective-permute-start(bf16[2,256,128]{2,1,0:T(8,128)(2,1)S(1)} %get-tuple-element.120), channel_id=1, source_target_pairs={{0,24},{8,16},{16,8},{24,0},{1,25},{9,17},{17,9},{25,1},{2,26},{10... | collective-permute-start | bytes 393224 | tf_op jit(solution)/shard_map/ppermute | solution.py:404
  55.7 5.4 %collective-permute-start.20 = (bf16[2,256,128]{2,1,0:T(8,128)(2,1)S(1)}, bf16[2,256,128]{2,1,0:T(8,128)(2,1)S(1)}, u32[]{:S(2)}, u32[]{:S(2)}) collective-permute-start(bf16[2,256,128]{2,1,0:T(8,128)(2,1)S(1)} %get-tuple-element.121), channel_id=1, source_target_pairs={{0,8},{8,0},{16,24},{24,16},{1,9},{9,1},{17,25},{25,17},{2,10},{10... | collective-permute-start | bytes 393224 | tf_op jit(solution)/shard_map/ppermute | solution.py:404
  55.8 7.4 %collective-permute-start.15 = (bf16[2,128,512]{2,1,0:T(8,128)(2,1)S(1)}, bf16[2,128,512]{2,1,0:T(8,128)(2,1)S(1)}, u32[]{:S(2)}, u32[]{:S(2)}) collective-permute-start(bf16[2,128,512]{2,1,0:T(8,128)(2,1)S(1)} %get-tuple-element.111), channel_id=1, source_target_pairs={{0,4},{4,0},{1,5},{5,1},{2,6},{6,2},{3,7},{7,3},{8,12},{12,8},{9,1... | collective-permute-start | bytes 786440 | tf_op jit(solution)/shard_map/ppermute | solution.py:399
  61.2 3.2 %collective-permute-start.21 = (bf16[2,128,512]{2,1,0:T(8,128)(2,1)S(1)}, bf16[2,128,512]{2,1,0:T(8,128)(2,1)S(1)}, u32[]{:S(2)}, u32[]{:S(2)}) collective-permute-start(bf16[2,128,512]{2,1,0:T(8,128)(2,1)S(1)} %get-tuple-element.123), channel_id=1, source_target_pairs={{0,4},{4,0},{1,5},{5,1},{2,6},{6,2},{3,7},{7,3},{8,12},{12,8},{9,1... | collective-permute-start | bytes 786440 | tf_op jit(solution)/shard_map/ppermute | solution.py:399

commit v5 on v4

--- a/solution.py
+++ b/solution.py
@@ -19,7 +19,7 @@
 START = {1: 0, 2: TOKENS // 2, 3: TOKENS // 2 + TOKENS // 4}
 EPS = 1e-06
 FLOOR = -1e30
-FLOPS = 4 * 10**9
+FLOPS = 10**8
 SCALE = 1.0 / math.sqrt(DH)
 SHARP = SCALE * math.log2(math.e)
 VMEM = pl.BlockSpec(memory_space=pltpu.VMEM)

time: 65.6 us -> 63.5 us (0.968)
  blocking collectives: 17.6 us -> 16.3 us
  waiting for transfers between devices: 6.83 us -> 5.54 us
  starting transfers between devices: 31 us -> 31.7 us
    ppermute x2, starting transfers between devices: 0.19 us -> 3.04 us  [swap_pair(): return lax.ppermute(x, 'z', [(i, i ^ 1) for i in range(lax.axis_size('z'))])]
    ppermute x2, starting transfers between devices: 9.65 us -> 7.51 us  [swap_other(): lax.ppermute(x, 'z', up + [(target, source) for source, target in up])]
    ppermute x12, waiting for transfers between devices: 5.24 us -> 3.69 us  [swap_chips(): lax.ppermute(message, 'x', [(i, i ^ step) for i in range(CHIPS)])]
    ppermute x2, waiting for transfers between devices: 0.01 us -> 1.37 us  [swap_other(): lax.ppermute(x, 'z', up + [(target, source) for source, target in up])]
    all_to_all x1, blocking collectives: 17.6 us -> 16.3 us  [exchange(): return lax.all_to_all(x, axes, 0, 0, tiled=True)]
    ppermute x2, waiting for transfers between devices: 1.11 us -> 0.01 us  [swap_pair(): return lax.ppermute(x, 'z', [(i, i ^ 1) for i in range(lax.axis_size('z'))])]
  transfers between devices with their start and end apart: 22 -> 22, of which waited for: 9 -> 7; matrix products, arithmetic and copies ran while one was open for 2% -> 2% of each run, Pallas kernels for 5% -> 5%
where the time goes in v5:
time: 63.5 us; the launch traced here: 63.3 us
  starting transfers between devices  31.7 us (50%)
  blocking collectives  16.3 us (26%)
  Pallas kernels  7.77 us (12%)
  waiting for transfers between devices  5.54 us (9%)
  local copies, waits for them, and re-layouts  1.11 us (2%)
  between operations  0.97 us (2%)
    all_to_all x1, blocking collectives, exchange(): return lax.all_to_all(x, axes, 0, 0, tiled=True)  16.3 us
    ppermute x12, starting transfers between devices, swap_chips(): lax.ppermute(message, 'x', [(i, i ^ step) for i in range(CHIPS)])  14.7 us
    ppermute x2, starting transfers between devices, swap_other(): lax.ppermute(x, 'z', up + [(target, source) for source, target in up])  7.51 us
    ppermute x6, starting transfers between devices, swap_core(): return lax.ppermute(x, 'c', [(0, 1), (1, 0)])  6.42 us
    ppermute x12, waiting for transfers between devices, swap_chips(): lax.ppermute(message, 'x', [(i, i ^ step) for i in range(CHIPS)])  3.69 us
    ppermute x2, starting transfers between devices, swap_pair(): return lax.ppermute(x, 'z', [(i, i ^ 1) for i in range(lax.axis_size('z'))])  3.04 us
    pallas_call x2, Pallas kernels, deliver(): return finish(own, swap_core(away))  1.63 us
    pallas_call x1, Pallas kernels, local(): call(backward_inner_kernel, [whole_f, whole_f] + [part] * CHIPS + [messag...  1.53 us
  transfers between devices with their start and end apart: 22, of which 7 were waited for; matrix products, arithmetic and copies ran while one was open for 2% of the time, Pallas kernels for 5%

profile of v5, /device:TPU:33, one launch (start us, length us, event | category | flops | bytes accessed | tf_op | source)
XLA Modules:
  0.0 63.3 jit_solution(18069612817004776385)
XLA Ops:
  0.6 0.0 copy-start
  0.6 0.8 %collective-permute-start.5 = (bf16[128,1024]{1,0:T(8,128)(2,1)}, bf16[128,1024]{1,0:T(8,128)(2,1)S(1)}, u32[]{:S(2)}, u32[]{:S(2)}) collective-permute-start(bf16[128,1024]{1,0:T(8,128)(2,1)} %param.6), channel_id=1, source_target_pairs={{0,4},{4,0},{1,5},{5,1},{2,6},{6,2},{3,7},{7,3},{8,12},{12,8},{9,1... | collective-permute-start | bytes 786440 | tf_op jit(solution)/shard_map/ppermute | solution.py:399
  1.4 0.1 collective-permute-start.6
  1.5 0.4 collective-permute-start
  1.9 0.1 collective-permute-start.1
  2.0 1.0 %constant_dynamic-slice_fusion = (bf16[128,512]{1,0:T(8,128)(2,1)S(1)}, bf16[128,512]{1,0:T(8,128)(2,1)S(1)}) fusion(bf16[128,1024]{1,0:T(8,128)(2,1)} %param.7, s32[]{:T(128)S(6)} %select_n.4, bf16[128,1024]{1,0:T(8,128)(2,1)} %param.6), kind=kLoop, calls=%fused_computation | loop fusion | bytes 524292 | tf_op jit(solution)/shard_map/dynamic_slice | solution.py:440
  3.0 0.0 collective-permute-done.5.got_x
  3.0 0.1 collective-permute-done.6.got_y
  3.2 0.1 shard_map.86
  3.3 2.8 %collective-permute-start.7 = (bf16[2,256,128]{2,1,0:T(8,128)(2,1)S(1)}, bf16[2,256,128]{2,1,0:T(8,128)(2,1)S(1)}, u32[]{:S(2)}, u32[]{:S(2)}) collective-permute-start(bf16[2,256,128]{2,1,0:T(8,128)(2,1)S(1)} %get-tuple-element.71), channel_id=1, source_target_pairs={{0,16},{8,24},{16,0},{24,8},{1,17},{9,25},{17,1},{25,9},{2,18},{10... | collective-permute-start | bytes 393224 | tf_op jit(solution)/shard_map/ppermute | solution.py:404
  6.1 0.9 %collective-permute-start.8 = (bf16[2,256,128]{2,1,0:T(8,128)(2,1)S(1)}, bf16[2,256,128]{2,1,0:T(8,128)(2,1)S(1)}, u32[]{:S(2)}, u32[]{:S(2)}) collective-permute-start(bf16[2,256,128]{2,1,0:T(8,128)(2,1)S(1)} %get-tuple-element.72), channel_id=1, source_target_pairs={{0,24},{8,16},{16,8},{24,0},{1,25},{9,17},{17,9},{25,1},{2,26},{10... | collective-permute-start | bytes 393224 | tf_op jit(solution)/shard_map/ppermute | solution.py:404
  7.0 0.0 collective-permute-done.got_x
  7.0 0.1 shard_map.84
  7.2 3.1 %collective-permute-start.2 = (bf16[2,256,128]{2,1,0:T(8,128)(2,1)S(1)}, bf16[2,256,128]{2,1,0:T(8,128)(2,1)S(1)}, u32[]{:S(2)}, u32[]{:S(2)}) collective-permute-start(bf16[2,256,128]{2,1,0:T(8,128)(2,1)S(1)} %get-tuple-element.66), channel_id=1, source_target_pairs={{0,16},{8,24},{16,0},{24,8},{1,17},{9,25},{17,1},{25,9},{2,18},{10... | collective-permute-start | bytes 393224 | tf_op jit(solution)/shard_map/ppermute | solution.py:404
  10.2 0.9 %collective-permute-start.3 = (bf16[2,256,128]{2,1,0:T(8,128)(2,1)S(1)}, bf16[2,256,128]{2,1,0:T(8,128)(2,1)S(1)}, u32[]{:S(2)}, u32[]{:S(2)}) collective-permute-start(bf16[2,256,128]{2,1,0:T(8,128)(2,1)S(1)} %get-tuple-element.67), channel_id=1, source_target_pairs={{0,24},{8,16},{16,8},{24,0},{1,25},{9,17},{17,9},{25,1},{2,26},{10... | collective-permute-start | bytes 393224 | tf_op jit(solution)/shard_map/ppermute | solution.py:404
  11.1 1.3 %collective-permute-done.8.refs_2_ = bf16[2,256,128]{2,1,0:T(8,128)(2,1)S(1)} collective-permute-done((bf16[2,256,128]{2,1,0:T(8,128)(2,1)S(1)}, bf16[2,256,128]{2,1,0:T(8,128)(2,1)S(1)}, u32[]{:S(2)}, u32[]{:S(2)}) %collective-permute-start.8) | collective-permute-done | bytes 131104 | tf_op jit(solution)/shard_map/ppermute | solution.py:404
  12.4 0.1 collective-permute-done.9.refs_3_
  12.5 0.3 shard_map.87
  12.8 3.0 %collective-permute-start.10 = (bf16[4,128,128]{2,1,0:T(8,128)(2,1)S(1)}, bf16[4,128,128]{2,1,0:T(8,128)(2,1)S(1)}, u32[]{:S(2)}, u32[]{:S(2)}) collective-permute-start(bf16[4,128,128]{2,1,0:T(8,128)(2,1)S(1)} %get-tuple-element.82), channel_id=1, source_target_pairs={{0,32},{32,0},{64,96},{96,64},{128,160},{160,128},{192,224},{224,1... | collective-permute-start | bytes 393224 | tf_op jit(solution)/shard_map/ppermute | solution.py:390
  15.7 2.3 %collective-permute-start.11 = (bf16[2,128,128]{2,1,0:T(8,128)(2,1)S(1)}, bf16[2,128,128]{2,1,0:T(8,128)(2,1)S(1)}, u32[]{:S(2)}, u32[]{:S(2)}) collective-permute-start(bf16[2,128,128]{2,1,0:T(8,128)(2,1)S(1)} %get-tuple-element.83), channel_id=1, source_target_pairs={{32,64},{96,128},{160,192},{64,32},{128,96},{192,160},{33,65},{97,... | collective-permute-start | bytes 196616 | tf_op jit(solution)/shard_map/ppermute | solution.py:395
  18.0 0.1 dynamic-slice_bitcast_fusion.gain.refs_2_
  18.1 0.0 collective-permute-done.4.refs_3_
  18.2 0.1 shard_map.85
  18.3 1.0 %shard_map.88 = (bf16[768,384]{1,0:T(8,128)(2,1)S(1)}, bf16[768,128]{1,0:T(8,128)(2,1)S(1)}, f32[1536,128]{1,0:T(8,128)S(1)}, f32[1536,128]{1,0:T(8,128)S(1)}, f32[1536,128]{1,0:T(8,128)S(1)}) custom-call(bf16[1024,128]{1,0:T(8,128)(2,1)S(1)} %get-tuple-element.69.q.refs_7_, bf16[1024,128]{1,0:T(8,128)(2,1)S(1)} %get-tuple-element.74.k, ...), custom_call_target="tpu_custom_call" | custom-call | flops 100000000 | tf_op jit(solution)/shard_map/pallas_call | solution.py:450
  19.3 1.4 %collective-permute-done.11.other = bf16[2,128,128]{2,1,0:T(8,128)(2,1)S(1)} collective-permute-done((bf16[2,128,128]{2,1,0:T(8,128)(2,1)S(1)}, bf16[2,128,128]{2,1,0:T(8,128)(2,1)S(1)}, u32[]{:S(2)}, u32[]{:S(2)}) %collective-permute-start.11) | collective-permute-done | bytes 65568 | tf_op jit(solution)/shard_map/ppermute | solution.py:395
  20.7 0.0 collective-permute-done.10.pair.refs_9_
  20.7 1.3 %shard_map.89 = (bf16[1024,128]{1,0:T(8,128)(2,1)S(1)}, bf16[32,16,128]{2,1,0:T(8,128)(2,1)S(1)}, bf16[256,384]{1,0:T(8,128)(2,1)S(1)}, bf16[128,128]{1,0:T(8,12...) custom-call(bf16[1024,128]{1,0:T(8,128)(2,1)S(1)} %get-tuple-element, ...), custom_call_target="tpu_custom_call" | custom-call | tf_op jit(solution)/shard_map/pallas_call | solution.py:453
  22.0 16.3 %all_to_all.5.refs_0_ = bf16[32,16,128]{2,1,0:T(8,128)(2,1)S(1)} all-to-all(bf16[32,16,128]{2,1,0:T(8,128)(2,1)S(1)} %get-tuple-element.88), channel_id=1, replica_groups=mesh['z'=8,'x'=4,'c'=2,'head'=4] {'x','c','head'}, dimensions={0} | all-to-all | bytes 262144 | tf_op jit(solution)/shard_map/all_to_all | solution.py:410
  38.3 1.1 %shard_map.90 = (bf16[1024,128]{1,0:T(8,128)(2,1)S(1)}, bf16[4,128,128]{2,1,0:T(8,128)(2,1)S(1)}, bf16[2,128,128]{2,1,0:T(8,128)(2,1)S(1)}, bf16[1024,128]{1,0:T...) custom-call(bf16[32,16,128]{2,1,0:T(8,128)(2,1)S(1)} %all_to_all.5.r, ...), custom_call_target="tpu_custom_call" | custom-call | tf_op jit(solution)/shard_map/pallas_call | solution.py:464
  39.4 1.5 %shard_map.91 = (f32[1024,128]{1,0:T(8,128)S(1)}, f32[1024,128]{1,0:T(8,128)S(1)}, bf16[2,256,128]{2,1,0:T(8,128)(2,1)S(1)}, bf16[2,256,128]{2,1,0:T(8,128)(2,1)...) custom-call(bf16[1024,128]{1,0:T(8,128)(2,1)S(1)} %get-tuple-element, ...), custom_call_target="tpu_custom_call" | custom-call | flops 200000000 | tf_op jit(solution)/shard_map/pallas_call | solution.py:470
  40.9 0.1 collective-permute-start.16
  41.0 1.3 %collective-permute-start.12 = (bf16[2,256,128]{2,1,0:T(8,128)(2,1)S(1)}, bf16[2,256,128]{2,1,0:T(8,128)(2,1)S(1)}, u32[]{:S(2)}, u32[]{:S(2)}) collective-permute-start(bf16[2,256,128]{2,1,0:T(8,128)(2,1)S(1)} %get-tuple-element.107), channel_id=1, source_target_pairs={{0,16},{8,24},{16,0},{24,8},{1,17},{9,25},{17,1},{25,9},{2,18},{10... | collective-permute-start | bytes 393224 | tf_op jit(solution)/shard_map/ppermute | solution.py:404
  42.3 5.2 %collective-permute-start.17 = (bf16[2,128,128]{2,1,0:T(8,128)(2,1)S(1)}, bf16[2,128,128]{2,1,0:T(8,128)(2,1)S(1)}, u32[]{:S(2)}, u32[]{:S(2)}) collective-permute-start(bf16[2,128,128]{2,1,0:T(8,128)(2,1)S(1)} %get-tuple-element.117), channel_id=1, source_target_pairs={{32,64},{96,128},{160,192},{64,32},{128,96},{192,160},{33,65},{97,... | collective-permute-start | bytes 196616 | tf_op jit(solution)/shard_map/ppermute | solution.py:395
  47.5 1.8 %collective-permute-start.13 = (bf16[2,256,128]{2,1,0:T(8,128)(2,1)S(1)}, bf16[2,256,128]{2,1,0:T(8,128)(2,1)S(1)}, u32[]{:S(2)}, u32[]{:S(2)}) collective-permute-start(bf16[2,256,128]{2,1,0:T(8,128)(2,1)S(1)} %get-tuple-element.108), channel_id=1, source_target_pairs={{0,24},{8,16},{16,8},{24,0},{1,25},{9,17},{17,9},{25,1},{2,26},{10... | collective-permute-start | bytes 393224 | tf_op jit(solution)/shard_map/ppermute | solution.py:404
  49.3 0.0 collective-permute-start.14
  49.3 0.0 collective-permute-done.17.other
  49.3 0.4 shard_map.94
  49.8 2.2 %collective-permute-start.18 = (bf16[2,256,128]{2,1,0:T(8,128)(2,1)S(1)}, bf16[2,256,128]{2,1,0:T(8,128)(2,1)S(1)}, u32[]{:S(2)}, u32[]{:S(2)}) collective-permute-start(bf16[2,256,128]{2,1,0:T(8,128)(2,1)S(1)} %get-tuple-element.119), channel_id=1, source_target_pairs={{0,16},{8,24},{16,0},{24,8},{1,17},{9,25},{17,1},{25,9},{2,18},{10... | collective-permute-start | bytes 393224 | tf_op jit(solution)/shard_map/ppermute | solution.py:404
  51.9 1.7 %collective-permute-start.19 = (bf16[2,256,128]{2,1,0:T(8,128)(2,1)S(1)}, bf16[2,256,128]{2,1,0:T(8,128)(2,1)S(1)}, u32[]{:S(2)}, u32[]{:S(2)}) collective-permute-start(bf16[2,256,128]{2,1,0:T(8,128)(2,1)S(1)} %get-tuple-element.120), channel_id=1, source_target_pairs={{0,24},{8,16},{16,8},{24,0},{1,25},{9,17},{17,9},{25,1},{2,26},{10... | collective-permute-start | bytes 393224 | tf_op jit(solution)/shard_map/ppermute | solution.py:404
  53.7 0.1 shard_map.92
  53.8 3.0 %collective-permute-start.15 = (bf16[2,128,512]{2,1,0:T(8,128)(2,1)S(1)}, bf16[2,128,512]{2,1,0:T(8,128)(2,1)S(1)}, u32[]{:S(2)}, u32[]{:S(2)}) collective-permute-start(bf16[2,128,512]{2,1,0:T(8,128)(2,1)S(1)} %get-tuple-element.111), channel_id=1, source_target_pairs={{0,4},{4,0},{1,5},{5,1},{2,6},{6,2},{3,7},{7,3},{8,12},{12,8},{9,1... | collective-permute-start | bytes 786440 | tf_op jit(solution)/shard_map/ppermute | solution.py:399
  56.8 1.4 %collective-permute-done.19.refs_2_ = bf16[2,256,128]{2,1,0:T(8,128)(2,1)S(1)} collective-permute-done((bf16[2,256,128]{2,1,0:T(8,128)(2,1)S(1)}, bf16[2,256,128]{2,1,0:T(8,128)(2,1)S(1)}, u32[]{:S(2)}, u32[]{:S(2)}) %collective-permute-start.19) | collective-permute-done | bytes 131104 | tf_op jit(solution)/shard_map/ppermute | solution.py:404
  58.2 0.8 %collective-permute-done.20.refs_3_ = bf16[2,256,128]{2,1,0:T(8,128)(2,1)S(1)} collective-permute-done((bf16[2,256,128]{2,1,0:T(8,128)(2,1)S(1)}, bf16[2,256,128]{2,1,0:T(8,128)(2,1)S(1)}, u32[]{:S(2)}, u32[]{:S(2)}) %collective-permute-start.20) | collective-permute-done | bytes 131104 | tf_op jit(solution)/shard_map/ppermute | solution.py:404
  59.1 0.1 shard_map.95
  59.2 2.0 %collective-permute-start.21 = (bf16[2,128,512]{2,1,0:T(8,128)(2,1)S(1)}, bf16[2,128,512]{2,1,0:T(8,128)(2,1)S(1)}, u32[]{:S(2)}, u32[]{:S(2)}) collective-permute-start(bf16[2,128,512]{2,1,0:T(8,128)(2,1)S(1)} %get-tuple-element.123), channel_id=1, source_target_pairs={{0,4},{4,0},{1,5},{5,1},{2,6},{6,2},{3,7},{7,3},{8,12},{12,8},{9,1... | collective-permute-start | bytes 786440 | tf_op jit(solution)/shard_map/ppermute | solution.py:399
  61.2 0.8 %shard_map.93 = (bf16[128,1024]{1,0:T(8,128)(2,1)}, bf16[128,1024]{1,0:T(8,128)(2,1)}) custom-call(bf16[2,128,512]{2,1,0:T(8,128)(2,1)S(1)} %get-tuple-element.110.own, bf16[2,128,512]{2,1,0:T(8,128)(2,1)S(1)} %collective-permute-done.15.got), custom_call_target="tpu_custom_call" | custom-call | tf_op jit(solution)/shard_map/pallas_call | solution.py:483
  62.0 0.3 collective-permute-done.21.got
  62.4 0.8 %shard_map.96 = (bf16[128,1024]{1,0:T(8,128)(2,1)}, bf16[128,1024]{1,0:T(8,128)(2,1)}) custom-call(bf16[2,128,512]{2,1,0:T(8,128)(2,1)S(1)} %get-tuple-element.122.own, bf16[2,128,512]{2,1,0:T(8,128)(2,1)S(1)} %collective-permute-done.21.got), custom_call_target="tpu_custom_call" | custom-call | tf_op jit(solution)/shard_map/pallas_call | solution.py:483
  (19 shorter events, 0.1 us)
Async XLA Ops:
  0.6 17.4 %copy-start = (f32[1024]{0:T(1024)S(1)}, f32[1024]{0:T(1024)}, u32[]{:S(2)}) copy-start(f32[1024]{0:T(1024)} %param.8) | copy-start | bytes 12292
  0.6 2.4 %collective-permute-start.5 = (bf16[128,1024]{1,0:T(8,128)(2,1)}, bf16[128,1024]{1,0:T(8,128)(2,1)S(1)}, u32[]{:S(2)}, u32[]{:S(2)}) collective-permute-start(bf16[128,1024]{1,0:T(8,128)(2,1)} %param.6), channel_id=1, source_target_pairs={{0,4},{4,0},{1,5},{5,1},{2,6},{6,2},{3,7},{7,3},{8,12},{12,8},{9,1... | collective-permute-start | bytes 786440 | tf_op jit(solution)/shard_map/ppermute | solution.py:399
  1.4 1.7 %collective-permute-start.6 = (bf16[128,1024]{1,0:T(8,128)(2,1)}, bf16[128,1024]{1,0:T(8,128)(2,1)S(1)}, u32[]{:S(2)}, u32[]{:S(2)}) collective-permute-start(bf16[128,1024]{1,0:T(8,128)(2,1)} %param.7), channel_id=1, source_target_pairs={{0,4},{4,0},{1,5},{5,1},{2,6},{6,2},{3,7},{7,3},{8,12},{12,8},{9,1... | collective-permute-start | bytes 786440 | tf_op jit(solution)/shard_map/ppermute | solution.py:399
  1.5 5.5 %collective-permute-start = (bf16[128,1024]{1,0:T(8,128)(2,1)}, bf16[128,1024]{1,0:T(8,128)(2,1)S(1)}, u32[]{:S(2)}, u32[]{:S(2)}) collective-permute-start(bf16[128,1024]{1,0:T(8,128)(2,1)} %param.5), channel_id=1, source_target_pairs={{0,4},{4,0},{1,5},{5,1},{2,6},{6,2},{3,7},{7,3},{8,12},{12,8},{9,1... | collective-permute-start | bytes 786440 | tf_op jit(solution)/shard_map/ppermute | solution.py:399
  1.9 5.1 %collective-permute-start.1 = (bf16[128,1024]{1,0:T(8,128)(2,1)}, bf16[128,1024]{1,0:T(8,128)(2,1)S(1)}, u32[]{:S(2)}, u32[]{:S(2)}) collective-permute-start(bf16[128,1024]{1,0:T(8,128)(2,1)} %param.9), channel_id=1, source_target_pairs={{0,4},{4,0},{1,5},{5,1},{2,6},{6,2},{3,7},{7,3},{8,12},{12,8},{9,1... | collective-permute-start | bytes 786440 | tf_op jit(solution)/shard_map/ppermute | solution.py:399
  3.2 3.8 %copy-start.1 = (bf16[128,1024]{1,0:T(8,128)(2,1)S(1)}, bf16[128,1024]{1,0:T(8,128)(2,1)}, u32[]{:S(2)}) copy-start(bf16[128,1024]{1,0:T(8,128)(2,1)} %param.5) | copy-start | bytes 786436
  3.2 3.8 %copy-start.2 = (bf16[128,1024]{1,0:T(8,128)(2,1)S(1)}, bf16[128,1024]{1,0:T(8,128)(2,1)}, u32[]{:S(2)}) copy-start(bf16[128,1024]{1,0:T(8,128)(2,1)} %param.9) | copy-start | bytes 786436
  3.3 7.8 %collective-permute-start.7 = (bf16[2,256,128]{2,1,0:T(8,128)(2,1)S(1)}, bf16[2,256,128]{2,1,0:T(8,128)(2,1)S(1)}, u32[]{:S(2)}, u32[]{:S(2)}) collective-permute-start(bf16[2,256,128]{2,1,0:T(8,128)(2,1)S(1)} %get-tuple-element.71), channel_id=1, source_target_pairs={{0,16},{8,24},{16,0},{24,8},{1,17},{9,25},{17,1},{25,9},{2,18},{10... | collective-permute-start | bytes 393224 | tf_op jit(solution)/shard_map/ppermute | solution.py:404
  6.1 6.3 %collective-permute-start.8 = (bf16[2,256,128]{2,1,0:T(8,128)(2,1)S(1)}, bf16[2,256,128]{2,1,0:T(8,128)(2,1)S(1)}, u32[]{:S(2)}, u32[]{:S(2)}) collective-permute-start(bf16[2,256,128]{2,1,0:T(8,128)(2,1)S(1)} %get-tuple-element.72), channel_id=1, source_target_pairs={{0,24},{8,16},{16,8},{24,0},{1,25},{9,17},{17,9},{25,1},{2,26},{10... | collective-permute-start | bytes 393224 | tf_op jit(solution)/shard_map/ppermute | solution.py:404
  7.0 5.5 %collective-permute-start.9 = (bf16[2,256,128]{2,1,0:T(8,128)(2,1)S(1)}, bf16[2,256,128]{2,1,0:T(8,128)(2,1)S(1)}, u32[]{:S(2)}, u32[]{:S(2)}) collective-permute-start(bf16[2,256,128]{2,1,0:T(8,128)(2,1)S(1)} %get-tuple-element.73), channel_id=1, source_target_pairs={{0,8},{8,0},{16,24},{24,16},{1,9},{9,1},{17,25},{25,17},{2,10},{10... | collective-permute-start | bytes 393224 | tf_op jit(solution)/shard_map/ppermute | solution.py:404
  7.2 11.0 %collective-permute-start.2 = (bf16[2,256,128]{2,1,0:T(8,128)(2,1)S(1)}, bf16[2,256,128]{2,1,0:T(8,128)(2,1)S(1)}, u32[]{:S(2)}, u32[]{:S(2)}) collective-permute-start(bf16[2,256,128]{2,1,0:T(8,128)(2,1)S(1)} %get-tuple-element.66), channel_id=1, source_target_pairs={{0,16},{8,24},{16,0},{24,8},{1,17},{9,25},{17,1},{25,9},{2,18},{10... | collective-permute-start | bytes 393224 | tf_op jit(solution)/shard_map/ppermute | solution.py:404
  10.2 7.9 %collective-permute-start.3 = (bf16[2,256,128]{2,1,0:T(8,128)(2,1)S(1)}, bf16[2,256,128]{2,1,0:T(8,128)(2,1)S(1)}, u32[]{:S(2)}, u32[]{:S(2)}) collective-permute-start(bf16[2,256,128]{2,1,0:T(8,128)(2,1)S(1)} %get-tuple-element.67), channel_id=1, source_target_pairs={{0,24},{8,16},{16,8},{24,0},{1,25},{9,17},{17,9},{25,1},{2,26},{10... | collective-permute-start | bytes 393224 | tf_op jit(solution)/shard_map/ppermute | solution.py:404
  11.1 7.1 %collective-permute-start.4 = (bf16[2,256,128]{2,1,0:T(8,128)(2,1)S(1)}, bf16[2,256,128]{2,1,0:T(8,128)(2,1)S(1)}, u32[]{:S(2)}, u32[]{:S(2)}) collective-permute-start(bf16[2,256,128]{2,1,0:T(8,128)(2,1)S(1)} %get-tuple-element.68), channel_id=1, source_target_pairs={{0,8},{8,0},{16,24},{24,16},{1,9},{9,1},{17,25},{25,17},{2,10},{10... | collective-permute-start | bytes 393224 | tf_op jit(solution)/shard_map/ppermute | solution.py:404
  12.8 8.0 %collective-permute-start.10 = (bf16[4,128,128]{2,1,0:T(8,128)(2,1)S(1)}, bf16[4,128,128]{2,1,0:T(8,128)(2,1)S(1)}, u32[]{:S(2)}, u32[]{:S(2)}) collective-permute-start(bf16[4,128,128]{2,1,0:T(8,128)(2,1)S(1)} %get-tuple-element.82), channel_id=1, source_target_pairs={{0,32},{32,0},{64,96},{96,64},{128,160},{160,128},{192,224},{224,1... | collective-permute-start | bytes 393224 | tf_op jit(solution)/shard_map/ppermute | solution.py:390
  15.7 5.0 %collective-permute-start.11 = (bf16[2,128,128]{2,1,0:T(8,128)(2,1)S(1)}, bf16[2,128,128]{2,1,0:T(8,128)(2,1)S(1)}, u32[]{:S(2)}, u32[]{:S(2)}) collective-permute-start(bf16[2,128,128]{2,1,0:T(8,128)(2,1)S(1)} %get-tuple-element.83), channel_id=1, source_target_pairs={{32,64},{96,128},{160,192},{64,32},{128,96},{192,160},{33,65},{97,... | collective-permute-start | bytes 196616 | tf_op jit(solution)/shard_map/ppermute | solution.py:395
  40.9 8.5 %collective-permute-start.16 = (bf16[4,128,128]{2,1,0:T(8,128)(2,1)S(1)}, bf16[4,128,128]{2,1,0:T(8,128)(2,1)S(1)}, u32[]{:S(2)}, u32[]{:S(2)}) collective-permute-start(bf16[4,128,128]{2,1,0:T(8,128)(2,1)S(1)} %get-tuple-element.116), channel_id=1, source_target_pairs={{0,32},{32,0},{64,96},{96,64},{128,160},{160,128},{192,224},{224,1... | collective-permute-start | bytes 393224 | tf_op jit(solution)/shard_map/ppermute | solution.py:390
  41.0 12.7 %collective-permute-start.12 = (bf16[2,256,128]{2,1,0:T(8,128)(2,1)S(1)}, bf16[2,256,128]{2,1,0:T(8,128)(2,1)S(1)}, u32[]{:S(2)}, u32[]{:S(2)}) collective-permute-start(bf16[2,256,128]{2,1,0:T(8,128)(2,1)S(1)} %get-tuple-element.107), channel_id=1, source_target_pairs={{0,16},{8,24},{16,0},{24,8},{1,17},{9,25},{17,1},{25,9},{2,18},{10... | collective-permute-start | bytes 393224 | tf_op jit(solution)/shard_map/ppermute | solution.py:404
  42.3 7.0 %collective-permute-start.17 = (bf16[2,128,128]{2,1,0:T(8,128)(2,1)S(1)}, bf16[2,128,128]{2,1,0:T(8,128)(2,1)S(1)}, u32[]{:S(2)}, u32[]{:S(2)}) collective-permute-start(bf16[2,128,128]{2,1,0:T(8,128)(2,1)S(1)} %get-tuple-element.117), channel_id=1, source_target_pairs={{32,64},{96,128},{160,192},{64,32},{128,96},{192,160},{33,65},{97,... | collective-permute-start | bytes 196616 | tf_op jit(solution)/shard_map/ppermute | solution.py:395
  47.5 6.2 %collective-permute-start.13 = (bf16[2,256,128]{2,1,0:T(8,128)(2,1)S(1)}, bf16[2,256,128]{2,1,0:T(8,128)(2,1)S(1)}, u32[]{:S(2)}, u32[]{:S(2)}) collective-permute-start(bf16[2,256,128]{2,1,0:T(8,128)(2,1)S(1)} %get-tuple-element.108), channel_id=1, source_target_pairs={{0,24},{8,16},{16,8},{24,0},{1,25},{9,17},{17,9},{25,1},{2,26},{10... | collective-permute-start | bytes 393224 | tf_op jit(solution)/shard_map/ppermute | solution.py:404
  49.3 4.4 %collective-permute-start.14 = (bf16[2,256,128]{2,1,0:T(8,128)(2,1)S(1)}, bf16[2,256,128]{2,1,0:T(8,128)(2,1)S(1)}, u32[]{:S(2)}, u32[]{:S(2)}) collective-permute-start(bf16[2,256,128]{2,1,0:T(8,128)(2,1)S(1)} %get-tuple-element.109), channel_id=1, source_target_pairs={{0,8},{8,0},{16,24},{24,16},{1,9},{9,1},{17,25},{25,17},{2,10},{10... | collective-permute-start | bytes 393224 | tf_op jit(solution)/shard_map/ppermute | solution.py:404
  49.8 7.1 %collective-permute-start.18 = (bf16[2,256,128]{2,1,0:T(8,128)(2,1)S(1)}, bf16[2,256,128]{2,1,0:T(8,128)(2,1)S(1)}, u32[]{:S(2)}, u32[]{:S(2)}) collective-permute-start(bf16[2,256,128]{2,1,0:T(8,128)(2,1)S(1)} %get-tuple-element.119), channel_id=1, source_target_pairs={{0,16},{8,24},{16,0},{24,8},{1,17},{9,25},{17,1},{25,9},{2,18},{10... | collective-permute-start | bytes 393224 | tf_op jit(solution)/shard_map/ppermute | solution.py:404
  51.9 6.3 %collective-permute-start.19 = (bf16[2,256,128]{2,1,0:T(8,128)(2,1)S(1)}, bf16[2,256,128]{2,1,0:T(8,128)(2,1)S(1)}, u32[]{:S(2)}, u32[]{:S(2)}) collective-permute-start(bf16[2,256,128]{2,1,0:T(8,128)(2,1)S(1)} %get-tuple-element.120), channel_id=1, source_target_pairs={{0,24},{8,16},{16,8},{24,0},{1,25},{9,17},{17,9},{25,1},{2,26},{10... | collective-permute-start | bytes 393224 | tf_op jit(solution)/shard_map/ppermute | solution.py:404
  53.7 5.4 %collective-permute-start.20 = (bf16[2,256,128]{2,1,0:T(8,128)(2,1)S(1)}, bf16[2,256,128]{2,1,0:T(8,128)(2,1)S(1)}, u32[]{:S(2)}, u32[]{:S(2)}) collective-permute-start(bf16[2,256,128]{2,1,0:T(8,128)(2,1)S(1)} %get-tuple-element.121), channel_id=1, source_target_pairs={{0,8},{8,0},{16,24},{24,16},{1,9},{9,1},{17,25},{25,17},{2,10},{10... | collective-permute-start | bytes 393224 | tf_op jit(solution)/shard_map/ppermute | solution.py:404
  53.8 7.4 %collective-permute-start.15 = (bf16[2,128,512]{2,1,0:T(8,128)(2,1)S(1)}, bf16[2,128,512]{2,1,0:T(8,128)(2,1)S(1)}, u32[]{:S(2)}, u32[]{:S(2)}) collective-permute-start(bf16[2,128,512]{2,1,0:T(8,128)(2,1)S(1)} %get-tuple-element.111), channel_id=1, source_target_pairs={{0,4},{4,0},{1,5},{5,1},{2,6},{6,2},{3,7},{7,3},{8,12},{12,8},{9,1... | collective-permute-start | bytes 786440 | tf_op jit(solution)/shard_map/ppermute | solution.py:399
  59.2 3.2 %collective-permute-start.21 = (bf16[2,128,512]{2,1,0:T(8,128)(2,1)S(1)}, bf16[2,128,512]{2,1,0:T(8,128)(2,1)S(1)}, u32[]{:S(2)}, u32[]{:S(2)}) collective-permute-start(bf16[2,128,512]{2,1,0:T(8,128)(2,1)S(1)} %get-tuple-element.123), channel_id=1, source_target_pairs={{0,4},{4,0},{1,5},{5,1},{2,6},{6,2},{3,7},{7,3},{8,12},{12,8},{9,1... | collective-permute-start | bytes 786440 | tf_op jit(solution)/shard_map/ppermute | solution.py:399

commit v6 on v5

--- a/solution.py
+++ b/solution.py
@@ -334,18 +334,18 @@
         e = grads[rows(0, 4), :] * (0.5 * factor) + spread(buf, e, 256)
         spread(buf, e, 512)
         for j in range(GROUP):
-            total = None
+            lefts, rights = [], []
             for side in range(3):
                 b = j + 1 - side
                 cols = pl.ds(side * BLOCK, BLOCK)
                 if b in (0, GROUP - 1):
-                    left = edge[rows(b // (GROUP - 1)), cols]
+                    lefts.append(edge[rows(b // (GROUP - 1)), cols])
                 elif 0 < b < GROUP - 1:
-                    left = mid[rows(b - 1), cols]
+                    lefts.append(mid[rows(b - 1), cols])
                 else:
                     continue
-                part = tn(left, right[rows(b), :])
-                total = part if total is None else total + part
+                rights.append(right[rows(b), :])
+            total = tn(jnp.concatenate(lefts, axis=0), jnp.concatenate(rights, axis=0))
             res[rows(j), :] = total * factor + buf[rows(j), :]
 
     key_value(SCALE, sl_edge, sl_mid, sl_coarse, q, qp, k_grad)

time: 63.5 us -> 63.5 us (level)
  no operation moved by 1% of the time
where the time goes in v6:
time: 63.5 us; the launch traced here: 63.4 us
  starting transfers between devices  31.7 us (50%)
  blocking collectives  16.3 us (26%)
  Pallas kernels  7.78 us (12%)
  waiting for transfers between devices  5.54 us (9%)
  local copies, waits for them, and re-layouts  1.11 us (2%)
  between operations  0.97 us (2%)
    all_to_all x1, blocking collectives, exchange(): return lax.all_to_all(x, axes, 0, 0, tiled=True)  16.3 us
    ppermute x12, starting transfers between devices, swap_chips(): lax.ppermute(message, 'x', [(i, i ^ step) for i in range(CHIPS)])  14.7 us
    ppermute x2, starting transfers between devices, swap_other(): lax.ppermute(x, 'z', up + [(target, source) for source, target in up])  7.51 us
    ppermute x6, starting transfers between devices, swap_core(): return lax.ppermute(x, 'c', [(0, 1), (1, 0)])  6.43 us
    ppermute x12, waiting for transfers between devices, swap_chips(): lax.ppermute(message, 'x', [(i, i ^ step) for i in range(CHIPS)])  3.69 us
    ppermute x2, starting transfers between devices, swap_pair(): return lax.ppermute(x, 'z', [(i, i ^ 1) for i in range(lax.axis_size('z'))])  3.04 us
    pallas_call x2, Pallas kernels, deliver(): return finish(own, swap_core(away))  1.63 us
    pallas_call x1, Pallas kernels, local(): call(backward_inner_kernel, [whole_f, whole_f] + [part] * CHIPS + [messag...  1.54 us
  transfers between devices with their start and end apart: 22, of which 7 were waited for; matrix products, arithmetic and copies ran while one was open for 2% of the time, Pallas kernels for 5%

profile of v6, /device:TPU:33, one launch (start us, length us, event | category | flops | bytes accessed | tf_op | source)
XLA Modules:
  0.0 63.4 jit_solution(13540505279474615168)
XLA Ops:
  0.6 0.0 copy-start
  0.6 0.8 %collective-permute-start.5 = (bf16[128,1024]{1,0:T(8,128)(2,1)}, bf16[128,1024]{1,0:T(8,128)(2,1)S(1)}, u32[]{:S(2)}, u32[]{:S(2)}) collective-permute-start(bf16[128,1024]{1,0:T(8,128)(2,1)} %param.6), channel_id=1, source_target_pairs={{0,4},{4,0},{1,5},{5,1},{2,6},{6,2},{3,7},{7,3},{8,12},{12,8},{9,1... | collective-permute-start | bytes 786440 | tf_op jit(solution)/shard_map/ppermute | solution.py:399
  1.4 0.1 collective-permute-start.6
  1.5 0.4 collective-permute-start
  1.9 0.1 collective-permute-start.1
  2.0 1.0 %constant_dynamic-slice_fusion = (bf16[128,512]{1,0:T(8,128)(2,1)S(1)}, bf16[128,512]{1,0:T(8,128)(2,1)S(1)}) fusion(bf16[128,1024]{1,0:T(8,128)(2,1)} %param.7, s32[]{:T(128)S(6)} %select_n.4, bf16[128,1024]{1,0:T(8,128)(2,1)} %param.6), kind=kLoop, calls=%fused_computation | loop fusion | bytes 524292 | tf_op jit(solution)/shard_map/dynamic_slice | solution.py:440
  3.0 0.0 collective-permute-done.5.got_x
  3.0 0.1 collective-permute-done.6.got_y
  3.2 0.1 shard_map.86
  3.3 2.8 %collective-permute-start.7 = (bf16[2,256,128]{2,1,0:T(8,128)(2,1)S(1)}, bf16[2,256,128]{2,1,0:T(8,128)(2,1)S(1)}, u32[]{:S(2)}, u32[]{:S(2)}) collective-permute-start(bf16[2,256,128]{2,1,0:T(8,128)(2,1)S(1)} %get-tuple-element.71), channel_id=1, source_target_pairs={{0,16},{8,24},{16,0},{24,8},{1,17},{9,25},{17,1},{25,9},{2,18},{10... | collective-permute-start | bytes 393224 | tf_op jit(solution)/shard_map/ppermute | solution.py:404
  6.1 0.9 %collective-permute-start.8 = (bf16[2,256,128]{2,1,0:T(8,128)(2,1)S(1)}, bf16[2,256,128]{2,1,0:T(8,128)(2,1)S(1)}, u32[]{:S(2)}, u32[]{:S(2)}) collective-permute-start(bf16[2,256,128]{2,1,0:T(8,128)(2,1)S(1)} %get-tuple-element.72), channel_id=1, source_target_pairs={{0,24},{8,16},{16,8},{24,0},{1,25},{9,17},{17,9},{25,1},{2,26},{10... | collective-permute-start | bytes 393224 | tf_op jit(solution)/shard_map/ppermute | solution.py:404
  7.0 0.0 collective-permute-start.9
  7.0 0.0 collective-permute-done.1.got_y
  7.0 0.1 shard_map.84
  7.2 3.1 %collective-permute-start.2 = (bf16[2,256,128]{2,1,0:T(8,128)(2,1)S(1)}, bf16[2,256,128]{2,1,0:T(8,128)(2,1)S(1)}, u32[]{:S(2)}, u32[]{:S(2)}) collective-permute-start(bf16[2,256,128]{2,1,0:T(8,128)(2,1)S(1)} %get-tuple-element.66), channel_id=1, source_target_pairs={{0,16},{8,24},{16,0},{24,8},{1,17},{9,25},{17,1},{25,9},{2,18},{10... | collective-permute-start | bytes 393224 | tf_op jit(solution)/shard_map/ppermute | solution.py:404
  10.2 0.9 %collective-permute-start.3 = (bf16[2,256,128]{2,1,0:T(8,128)(2,1)S(1)}, bf16[2,256,128]{2,1,0:T(8,128)(2,1)S(1)}, u32[]{:S(2)}, u32[]{:S(2)}) collective-permute-start(bf16[2,256,128]{2,1,0:T(8,128)(2,1)S(1)} %get-tuple-element.67), channel_id=1, source_target_pairs={{0,24},{8,16},{16,8},{24,0},{1,25},{9,17},{17,9},{25,1},{2,26},{10... | collective-permute-start | bytes 393224 | tf_op jit(solution)/shard_map/ppermute | solution.py:404
  11.1 0.0 collective-permute-done.7.refs_1_
  11.1 0.0 collective-permute-start.4
  11.1 1.3 %collective-permute-done.8.refs_2_ = bf16[2,256,128]{2,1,0:T(8,128)(2,1)S(1)} collective-permute-done((bf16[2,256,128]{2,1,0:T(8,128)(2,1)S(1)}, bf16[2,256,128]{2,1,0:T(8,128)(2,1)S(1)}, u32[]{:S(2)}, u32[]{:S(2)}) %collective-permute-start.8) | collective-permute-done | bytes 131104 | tf_op jit(solution)/shard_map/ppermute | solution.py:404
  12.4 0.1 collective-permute-done.9.refs_3_
  12.5 0.3 shard_map.87
  12.8 3.0 %collective-permute-start.10 = (bf16[4,128,128]{2,1,0:T(8,128)(2,1)S(1)}, bf16[4,128,128]{2,1,0:T(8,128)(2,1)S(1)}, u32[]{:S(2)}, u32[]{:S(2)}) collective-permute-start(bf16[4,128,128]{2,1,0:T(8,128)(2,1)S(1)} %get-tuple-element.82), channel_id=1, source_target_pairs={{0,32},{32,0},{64,96},{96,64},{128,160},{160,128},{192,224},{224,1... | collective-permute-start | bytes 393224 | tf_op jit(solution)/shard_map/ppermute | solution.py:390
  15.7 2.3 %collective-permute-start.11 = (bf16[2,128,128]{2,1,0:T(8,128)(2,1)S(1)}, bf16[2,128,128]{2,1,0:T(8,128)(2,1)S(1)}, u32[]{:S(2)}, u32[]{:S(2)}) collective-permute-start(bf16[2,128,128]{2,1,0:T(8,128)(2,1)S(1)} %get-tuple-element.83), channel_id=1, source_target_pairs={{32,64},{96,128},{160,192},{64,32},{128,96},{192,160},{33,65},{97,... | collective-permute-start | bytes 196616 | tf_op jit(solution)/shard_map/ppermute | solution.py:395
  18.0 0.1 dynamic-slice_bitcast_fusion.gain.refs_2_
  18.1 0.0 collective-permute-done.4.refs_3_
  18.2 0.1 shard_map.85
  18.3 1.0 %shard_map.88 = (bf16[768,384]{1,0:T(8,128)(2,1)S(1)}, bf16[768,128]{1,0:T(8,128)(2,1)S(1)}, f32[1536,128]{1,0:T(8,128)S(1)}, f32[1536,128]{1,0:T(8,128)S(1)}, f32[1536,128]{1,0:T(8,128)S(1)}) custom-call(bf16[1024,128]{1,0:T(8,128)(2,1)S(1)} %get-tuple-element.69.q.refs_7_, bf16[1024,128]{1,0:T(8,128)(2,1)S(1)} %get-tuple-element.74.k, ...), custom_call_target="tpu_custom_call" | custom-call | flops 100000000 | tf_op jit(solution)/shard_map/pallas_call | solution.py:450
  19.3 1.4 %collective-permute-done.11.other = bf16[2,128,128]{2,1,0:T(8,128)(2,1)S(1)} collective-permute-done((bf16[2,128,128]{2,1,0:T(8,128)(2,1)S(1)}, bf16[2,128,128]{2,1,0:T(8,128)(2,1)S(1)}, u32[]{:S(2)}, u32[]{:S(2)}) %collective-permute-start.11) | collective-permute-done | bytes 65568 | tf_op jit(solution)/shard_map/ppermute | solution.py:395
  20.7 1.3 %shard_map.89 = (bf16[1024,128]{1,0:T(8,128)(2,1)S(1)}, bf16[32,16,128]{2,1,0:T(8,128)(2,1)S(1)}, bf16[256,384]{1,0:T(8,128)(2,1)S(1)}, bf16[128,128]{1,0:T(8,12...) custom-call(bf16[1024,128]{1,0:T(8,128)(2,1)S(1)} %get-tuple-element, ...), custom_call_target="tpu_custom_call" | custom-call | tf_op jit(solution)/shard_map/pallas_call | solution.py:453
  22.0 16.3 %all_to_all.5.refs_0_ = bf16[32,16,128]{2,1,0:T(8,128)(2,1)S(1)} all-to-all(bf16[32,16,128]{2,1,0:T(8,128)(2,1)S(1)} %get-tuple-element.88), channel_id=1, replica_groups=mesh['z'=8,'x'=4,'c'=2,'head'=4] {'x','c','head'}, dimensions={0} | all-to-all | bytes 262144 | tf_op jit(solution)/shard_map/all_to_all | solution.py:410
  38.3 1.1 %shard_map.90 = (bf16[1024,128]{1,0:T(8,128)(2,1)S(1)}, bf16[4,128,128]{2,1,0:T(8,128)(2,1)S(1)}, bf16[2,128,128]{2,1,0:T(8,128)(2,1)S(1)}, bf16[1024,128]{1,0:T...) custom-call(bf16[32,16,128]{2,1,0:T(8,128)(2,1)S(1)} %all_to_all.5.r, ...), custom_call_target="tpu_custom_call" | custom-call | tf_op jit(solution)/shard_map/pallas_call | solution.py:464
  39.4 1.5 %shard_map.91 = (f32[1024,128]{1,0:T(8,128)S(1)}, f32[1024,128]{1,0:T(8,128)S(1)}, bf16[2,256,128]{2,1,0:T(8,128)(2,1)S(1)}, bf16[2,256,128]{2,1,0:T(8,128)(2,1)...) custom-call(bf16[1024,128]{1,0:T(8,128)(2,1)S(1)} %get-tuple-element, ...), custom_call_target="tpu_custom_call" | custom-call | flops 200000000 | tf_op jit(solution)/shard_map/pallas_call | solution.py:470
  40.9 0.1 collective-permute-start.16
  41.0 1.3 %collective-permute-start.12 = (bf16[2,256,128]{2,1,0:T(8,128)(2,1)S(1)}, bf16[2,256,128]{2,1,0:T(8,128)(2,1)S(1)}, u32[]{:S(2)}, u32[]{:S(2)}) collective-permute-start(bf16[2,256,128]{2,1,0:T(8,128)(2,1)S(1)} %get-tuple-element.107), channel_id=1, source_target_pairs={{0,16},{8,24},{16,0},{24,8},{1,17},{9,25},{17,1},{25,9},{2,18},{10... | collective-permute-start | bytes 393224 | tf_op jit(solution)/shard_map/ppermute | solution.py:404
  42.3 5.2 %collective-permute-start.17 = (bf16[2,128,128]{2,1,0:T(8,128)(2,1)S(1)}, bf16[2,128,128]{2,1,0:T(8,128)(2,1)S(1)}, u32[]{:S(2)}, u32[]{:S(2)}) collective-permute-start(bf16[2,128,128]{2,1,0:T(8,128)(2,1)S(1)} %get-tuple-element.117), channel_id=1, source_target_pairs={{32,64},{96,128},{160,192},{64,32},{128,96},{192,160},{33,65},{97,... | collective-permute-start | bytes 196616 | tf_op jit(solution)/shard_map/ppermute | solution.py:395
  47.5 1.8 %collective-permute-start.13 = (bf16[2,256,128]{2,1,0:T(8,128)(2,1)S(1)}, bf16[2,256,128]{2,1,0:T(8,128)(2,1)S(1)}, u32[]{:S(2)}, u32[]{:S(2)}) collective-permute-start(bf16[2,256,128]{2,1,0:T(8,128)(2,1)S(1)} %get-tuple-element.108), channel_id=1, source_target_pairs={{0,24},{8,16},{16,8},{24,0},{1,25},{9,17},{17,9},{25,1},{2,26},{10... | collective-permute-start | bytes 393224 | tf_op jit(solution)/shard_map/ppermute | solution.py:404
  49.4 0.4 shard_map.94
  49.8 2.2 %collective-permute-start.18 = (bf16[2,256,128]{2,1,0:T(8,128)(2,1)S(1)}, bf16[2,256,128]{2,1,0:T(8,128)(2,1)S(1)}, u32[]{:S(2)}, u32[]{:S(2)}) collective-permute-start(bf16[2,256,128]{2,1,0:T(8,128)(2,1)S(1)} %get-tuple-element.119), channel_id=1, source_target_pairs={{0,16},{8,24},{16,0},{24,8},{1,17},{9,25},{17,1},{25,9},{2,18},{10... | collective-permute-start | bytes 393224 | tf_op jit(solution)/shard_map/ppermute | solution.py:404
  52.0 1.7 %collective-permute-start.19 = (bf16[2,256,128]{2,1,0:T(8,128)(2,1)S(1)}, bf16[2,256,128]{2,1,0:T(8,128)(2,1)S(1)}, u32[]{:S(2)}, u32[]{:S(2)}) collective-permute-start(bf16[2,256,128]{2,1,0:T(8,128)(2,1)S(1)} %get-tuple-element.120), channel_id=1, source_target_pairs={{0,24},{8,16},{16,8},{24,0},{1,25},{9,17},{17,9},{25,1},{2,26},{10... | collective-permute-start | bytes 393224 | tf_op jit(solution)/shard_map/ppermute | solution.py:404
  53.7 0.1 shard_map.92
  53.8 3.0 %collective-permute-start.15 = (bf16[2,128,512]{2,1,0:T(8,128)(2,1)S(1)}, bf16[2,128,512]{2,1,0:T(8,128)(2,1)S(1)}, u32[]{:S(2)}, u32[]{:S(2)}) collective-permute-start(bf16[2,128,512]{2,1,0:T(8,128)(2,1)S(1)} %get-tuple-element.111), channel_id=1, source_target_pairs={{0,4},{4,0},{1,5},{5,1},{2,6},{6,2},{3,7},{7,3},{8,12},{12,8},{9,1... | collective-permute-start | bytes 786440 | tf_op jit(solution)/shard_map/ppermute | solution.py:399
  56.9 1.4 %collective-permute-done.19.refs_2_ = bf16[2,256,128]{2,1,0:T(8,128)(2,1)S(1)} collective-permute-done((bf16[2,256,128]{2,1,0:T(8,128)(2,1)S(1)}, bf16[2,256,128]{2,1,0:T(8,128)(2,1)S(1)}, u32[]{:S(2)}, u32[]{:S(2)}) %collective-permute-start.19) | collective-permute-done | bytes 131104 | tf_op jit(solution)/shard_map/ppermute | solution.py:404
  58.3 0.8 %collective-permute-done.20.refs_3_ = bf16[2,256,128]{2,1,0:T(8,128)(2,1)S(1)} collective-permute-done((bf16[2,256,128]{2,1,0:T(8,128)(2,1)S(1)}, bf16[2,256,128]{2,1,0:T(8,128)(2,1)S(1)}, u32[]{:S(2)}, u32[]{:S(2)}) %collective-permute-start.20) | collective-permute-done | bytes 131104 | tf_op jit(solution)/shard_map/ppermute | solution.py:404
  59.1 0.1 shard_map.95
  59.2 2.0 %collective-permute-start.21 = (bf16[2,128,512]{2,1,0:T(8,128)(2,1)S(1)}, bf16[2,128,512]{2,1,0:T(8,128)(2,1)S(1)}, u32[]{:S(2)}, u32[]{:S(2)}) collective-permute-start(bf16[2,128,512]{2,1,0:T(8,128)(2,1)S(1)} %get-tuple-element.123), channel_id=1, source_target_pairs={{0,4},{4,0},{1,5},{5,1},{2,6},{6,2},{3,7},{7,3},{8,12},{12,8},{9,1... | collective-permute-start | bytes 786440 | tf_op jit(solution)/shard_map/ppermute | solution.py:399
  61.2 0.8 %shard_map.93 = (bf16[128,1024]{1,0:T(8,128)(2,1)}, bf16[128,1024]{1,0:T(8,128)(2,1)}) custom-call(bf16[2,128,512]{2,1,0:T(8,128)(2,1)S(1)} %get-tuple-element.110.own, bf16[2,128,512]{2,1,0:T(8,128)(2,1)S(1)} %collective-permute-done.15.got), custom_call_target="tpu_custom_call" | custom-call | tf_op jit(solution)/shard_map/pallas_call | solution.py:483
  62.1 0.3 collective-permute-done.21.got
  62.4 0.8 %shard_map.96 = (bf16[128,1024]{1,0:T(8,128)(2,1)}, bf16[128,1024]{1,0:T(8,128)(2,1)}) custom-call(bf16[2,128,512]{2,1,0:T(8,128)(2,1)S(1)} %get-tuple-element.122.own, bf16[2,128,512]{2,1,0:T(8,128)(2,1)S(1)} %collective-permute-done.21.got), custom_call_target="tpu_custom_call" | custom-call | tf_op jit(solution)/shard_map/pallas_call | solution.py:483
  (19 shorter events, 0.1 us)
Async XLA Ops:
  0.6 17.4 %copy-start = (f32[1024]{0:T(1024)S(1)}, f32[1024]{0:T(1024)}, u32[]{:S(2)}) copy-start(f32[1024]{0:T(1024)} %param.8) | copy-start | bytes 12292
  0.6 2.4 %collective-permute-start.5 = (bf16[128,1024]{1,0:T(8,128)(2,1)}, bf16[128,1024]{1,0:T(8,128)(2,1)S(1)}, u32[]{:S(2)}, u32[]{:S(2)}) collective-permute-start(bf16[128,1024]{1,0:T(8,128)(2,1)} %param.6), channel_id=1, source_target_pairs={{0,4},{4,0},{1,5},{5,1},{2,6},{6,2},{3,7},{7,3},{8,12},{12,8},{9,1... | collective-permute-start | bytes 786440 | tf_op jit(solution)/shard_map/ppermute | solution.py:399
  1.4 1.7 %collective-permute-start.6 = (bf16[128,1024]{1,0:T(8,128)(2,1)}, bf16[128,1024]{1,0:T(8,128)(2,1)S(1)}, u32[]{:S(2)}, u32[]{:S(2)}) collective-permute-start(bf16[128,1024]{1,0:T(8,128)(2,1)} %param.7), channel_id=1, source_target_pairs={{0,4},{4,0},{1,5},{5,1},{2,6},{6,2},{3,7},{7,3},{8,12},{12,8},{9,1... | collective-permute-start | bytes 786440 | tf_op jit(solution)/shard_map/ppermute | solution.py:399
  1.5 5.5 %collective-permute-start = (bf16[128,1024]{1,0:T(8,128)(2,1)}, bf16[128,1024]{1,0:T(8,128)(2,1)S(1)}, u32[]{:S(2)}, u32[]{:S(2)}) collective-permute-start(bf16[128,1024]{1,0:T(8,128)(2,1)} %param.5), channel_id=1, source_target_pairs={{0,4},{4,0},{1,5},{5,1},{2,6},{6,2},{3,7},{7,3},{8,12},{12,8},{9,1... | collective-permute-start | bytes 786440 | tf_op jit(solution)/shard_map/ppermute | solution.py:399
  1.9 5.1 %collective-permute-start.1 = (bf16[128,1024]{1,0:T(8,128)(2,1)}, bf16[128,1024]{1,0:T(8,128)(2,1)S(1)}, u32[]{:S(2)}, u32[]{:S(2)}) collective-permute-start(bf16[128,1024]{1,0:T(8,128)(2,1)} %param.9), channel_id=1, source_target_pairs={{0,4},{4,0},{1,5},{5,1},{2,6},{6,2},{3,7},{7,3},{8,12},{12,8},{9,1... | collective-permute-start | bytes 786440 | tf_op jit(solution)/shard_map/ppermute | solution.py:399
  3.2 3.8 %copy-start.1 = (bf16[128,1024]{1,0:T(8,128)(2,1)S(1)}, bf16[128,1024]{1,0:T(8,128)(2,1)}, u32[]{:S(2)}) copy-start(bf16[128,1024]{1,0:T(8,128)(2,1)} %param.5) | copy-start | bytes 786436
  3.2 3.8 %copy-start.2 = (bf16[128,1024]{1,0:T(8,128)(2,1)S(1)}, bf16[128,1024]{1,0:T(8,128)(2,1)}, u32[]{:S(2)}) copy-start(bf16[128,1024]{1,0:T(8,128)(2,1)} %param.9) | copy-start | bytes 786436
  3.3 7.8 %collective-permute-start.7 = (bf16[2,256,128]{2,1,0:T(8,128)(2,1)S(1)}, bf16[2,256,128]{2,1,0:T(8,128)(2,1)S(1)}, u32[]{:S(2)}, u32[]{:S(2)}) collective-permute-start(bf16[2,256,128]{2,1,0:T(8,128)(2,1)S(1)} %get-tuple-element.71), channel_id=1, source_target_pairs={{0,16},{8,24},{16,0},{24,8},{1,17},{9,25},{17,1},{25,9},{2,18},{10... | collective-permute-start | bytes 393224 | tf_op jit(solution)/shard_map/ppermute | solution.py:404
  6.1 6.3 %collective-permute-start.8 = (bf16[2,256,128]{2,1,0:T(8,128)(2,1)S(1)}, bf16[2,256,128]{2,1,0:T(8,128)(2,1)S(1)}, u32[]{:S(2)}, u32[]{:S(2)}) collective-permute-start(bf16[2,256,128]{2,1,0:T(8,128)(2,1)S(1)} %get-tuple-element.72), channel_id=1, source_target_pairs={{0,24},{8,16},{16,8},{24,0},{1,25},{9,17},{17,9},{25,1},{2,26},{10... | collective-permute-start | bytes 393224 | tf_op jit(solution)/shard_map/ppermute | solution.py:404
  7.0 5.5 %collective-permute-start.9 = (bf16[2,256,128]{2,1,0:T(8,128)(2,1)S(1)}, bf16[2,256,128]{2,1,0:T(8,128)(2,1)S(1)}, u32[]{:S(2)}, u32[]{:S(2)}) collective-permute-start(bf16[2,256,128]{2,1,0:T(8,128)(2,1)S(1)} %get-tuple-element.73), channel_id=1, source_target_pairs={{0,8},{8,0},{16,24},{24,16},{1,9},{9,1},{17,25},{25,17},{2,10},{10... | collective-permute-start | bytes 393224 | tf_op jit(solution)/shard_map/ppermute | solution.py:404
  7.2 11.0 %collective-permute-start.2 = (bf16[2,256,128]{2,1,0:T(8,128)(2,1)S(1)}, bf16[2,256,128]{2,1,0:T(8,128)(2,1)S(1)}, u32[]{:S(2)}, u32[]{:S(2)}) collective-permute-start(bf16[2,256,128]{2,1,0:T(8,128)(2,1)S(1)} %get-tuple-element.66), channel_id=1, source_target_pairs={{0,16},{8,24},{16,0},{24,8},{1,17},{9,25},{17,1},{25,9},{2,18},{10... | collective-permute-start | bytes 393224 | tf_op jit(solution)/shard_map/ppermute | solution.py:404
  10.2 7.9 %collective-permute-start.3 = (bf16[2,256,128]{2,1,0:T(8,128)(2,1)S(1)}, bf16[2,256,128]{2,1,0:T(8,128)(2,1)S(1)}, u32[]{:S(2)}, u32[]{:S(2)}) collective-permute-start(bf16[2,256,128]{2,1,0:T(8,128)(2,1)S(1)} %get-tuple-element.67), channel_id=1, source_target_pairs={{0,24},{8,16},{16,8},{24,0},{1,25},{9,17},{17,9},{25,1},{2,26},{10... | collective-permute-start | bytes 393224 | tf_op jit(solution)/shard_map/ppermute | solution.py:404
  11.1 7.1 %collective-permute-start.4 = (bf16[2,256,128]{2,1,0:T(8,128)(2,1)S(1)}, bf16[2,256,128]{2,1,0:T(8,128)(2,1)S(1)}, u32[]{:S(2)}, u32[]{:S(2)}) collective-permute-start(bf16[2,256,128]{2,1,0:T(8,128)(2,1)S(1)} %get-tuple-element.68), channel_id=1, source_target_pairs={{0,8},{8,0},{16,24},{24,16},{1,9},{9,1},{17,25},{25,17},{2,10},{10... | collective-permute-start | bytes 393224 | tf_op jit(solution)/shard_map/ppermute | solution.py:404
  12.8 8.0 %collective-permute-start.10 = (bf16[4,128,128]{2,1,0:T(8,128)(2,1)S(1)}, bf16[4,128,128]{2,1,0:T(8,128)(2,1)S(1)}, u32[]{:S(2)}, u32[]{:S(2)}) collective-permute-start(bf16[4,128,128]{2,1,0:T(8,128)(2,1)S(1)} %get-tuple-element.82), channel_id=1, source_target_pairs={{0,32},{32,0},{64,96},{96,64},{128,160},{160,128},{192,224},{224,1... | collective-permute-start | bytes 393224 | tf_op jit(solution)/shard_map/ppermute | solution.py:390
  15.7 5.0 %collective-permute-start.11 = (bf16[2,128,128]{2,1,0:T(8,128)(2,1)S(1)}, bf16[2,128,128]{2,1,0:T(8,128)(2,1)S(1)}, u32[]{:S(2)}, u32[]{:S(2)}) collective-permute-start(bf16[2,128,128]{2,1,0:T(8,128)(2,1)S(1)} %get-tuple-element.83), channel_id=1, source_target_pairs={{32,64},{96,128},{160,192},{64,32},{128,96},{192,160},{33,65},{97,... | collective-permute-start | bytes 196616 | tf_op jit(solution)/shard_map/ppermute | solution.py:395
  40.9 8.5 %collective-permute-start.16 = (bf16[4,128,128]{2,1,0:T(8,128)(2,1)S(1)}, bf16[4,128,128]{2,1,0:T(8,128)(2,1)S(1)}, u32[]{:S(2)}, u32[]{:S(2)}) collective-permute-start(bf16[4,128,128]{2,1,0:T(8,128)(2,1)S(1)} %get-tuple-element.116), channel_id=1, source_target_pairs={{0,32},{32,0},{64,96},{96,64},{128,160},{160,128},{192,224},{224,1... | collective-permute-start | bytes 393224 | tf_op jit(solution)/shard_map/ppermute | solution.py:390
  41.0 12.7 %collective-permute-start.12 = (bf16[2,256,128]{2,1,0:T(8,128)(2,1)S(1)}, bf16[2,256,128]{2,1,0:T(8,128)(2,1)S(1)}, u32[]{:S(2)}, u32[]{:S(2)}) collective-permute-start(bf16[2,256,128]{2,1,0:T(8,128)(2,1)S(1)} %get-tuple-element.107), channel_id=1, source_target_pairs={{0,16},{8,24},{16,0},{24,8},{1,17},{9,25},{17,1},{25,9},{2,18},{10... | collective-permute-start | bytes 393224 | tf_op jit(solution)/shard_map/ppermute | solution.py:404
  42.3 7.0 %collective-permute-start.17 = (bf16[2,128,128]{2,1,0:T(8,128)(2,1)S(1)}, bf16[2,128,128]{2,1,0:T(8,128)(2,1)S(1)}, u32[]{:S(2)}, u32[]{:S(2)}) collective-permute-start(bf16[2,128,128]{2,1,0:T(8,128)(2,1)S(1)} %get-tuple-element.117), channel_id=1, source_target_pairs={{32,64},{96,128},{160,192},{64,32},{128,96},{192,160},{33,65},{97,... | collective-permute-start | bytes 196616 | tf_op jit(solution)/shard_map/ppermute | solution.py:395
  47.5 6.2 %collective-permute-start.13 = (bf16[2,256,128]{2,1,0:T(8,128)(2,1)S(1)}, bf16[2,256,128]{2,1,0:T(8,128)(2,1)S(1)}, u32[]{:S(2)}, u32[]{:S(2)}) collective-permute-start(bf16[2,256,128]{2,1,0:T(8,128)(2,1)S(1)} %get-tuple-element.108), channel_id=1, source_target_pairs={{0,24},{8,16},{16,8},{24,0},{1,25},{9,17},{17,9},{25,1},{2,26},{10... | collective-permute-start | bytes 393224 | tf_op jit(solution)/shard_map/ppermute | solution.py:404
  49.3 4.4 %collective-permute-start.14 = (bf16[2,256,128]{2,1,0:T(8,128)(2,1)S(1)}, bf16[2,256,128]{2,1,0:T(8,128)(2,1)S(1)}, u32[]{:S(2)}, u32[]{:S(2)}) collective-permute-start(bf16[2,256,128]{2,1,0:T(8,128)(2,1)S(1)} %get-tuple-element.109), channel_id=1, source_target_pairs={{0,8},{8,0},{16,24},{24,16},{1,9},{9,1},{17,25},{25,17},{2,10},{10... | collective-permute-start | bytes 393224 | tf_op jit(solution)/shard_map/ppermute | solution.py:404
  49.8 7.1 %collective-permute-start.18 = (bf16[2,256,128]{2,1,0:T(8,128)(2,1)S(1)}, bf16[2,256,128]{2,1,0:T(8,128)(2,1)S(1)}, u32[]{:S(2)}, u32[]{:S(2)}) collective-permute-start(bf16[2,256,128]{2,1,0:T(8,128)(2,1)S(1)} %get-tuple-element.119), channel_id=1, source_target_pairs={{0,16},{8,24},{16,0},{24,8},{1,17},{9,25},{17,1},{25,9},{2,18},{10... | collective-permute-start | bytes 393224 | tf_op jit(solution)/shard_map/ppermute | solution.py:404
  52.0 6.3 %collective-permute-start.19 = (bf16[2,256,128]{2,1,0:T(8,128)(2,1)S(1)}, bf16[2,256,128]{2,1,0:T(8,128)(2,1)S(1)}, u32[]{:S(2)}, u32[]{:S(2)}) collective-permute-start(bf16[2,256,128]{2,1,0:T(8,128)(2,1)S(1)} %get-tuple-element.120), channel_id=1, source_target_pairs={{0,24},{8,16},{16,8},{24,0},{1,25},{9,17},{17,9},{25,1},{2,26},{10... | collective-permute-start | bytes 393224 | tf_op jit(solution)/shard_map/ppermute | solution.py:404
  53.7 5.4 %collective-permute-start.20 = (bf16[2,256,128]{2,1,0:T(8,128)(2,1)S(1)}, bf16[2,256,128]{2,1,0:T(8,128)(2,1)S(1)}, u32[]{:S(2)}, u32[]{:S(2)}) collective-permute-start(bf16[2,256,128]{2,1,0:T(8,128)(2,1)S(1)} %get-tuple-element.121), channel_id=1, source_target_pairs={{0,8},{8,0},{16,24},{24,16},{1,9},{9,1},{17,25},{25,17},{2,10},{10... | collective-permute-start | bytes 393224 | tf_op jit(solution)/shard_map/ppermute | solution.py:404
  53.8 7.4 %collective-permute-start.15 = (bf16[2,128,512]{2,1,0:T(8,128)(2,1)S(1)}, bf16[2,128,512]{2,1,0:T(8,128)(2,1)S(1)}, u32[]{:S(2)}, u32[]{:S(2)}) collective-permute-start(bf16[2,128,512]{2,1,0:T(8,128)(2,1)S(1)} %get-tuple-element.111), channel_id=1, source_target_pairs={{0,4},{4,0},{1,5},{5,1},{2,6},{6,2},{3,7},{7,3},{8,12},{12,8},{9,1... | collective-permute-start | bytes 786440 | tf_op jit(solution)/shard_map/ppermute | solution.py:399
  59.2 3.2 %collective-permute-start.21 = (bf16[2,128,512]{2,1,0:T(8,128)(2,1)S(1)}, bf16[2,128,512]{2,1,0:T(8,128)(2,1)S(1)}, u32[]{:S(2)}, u32[]{:S(2)}) collective-permute-start(bf16[2,128,512]{2,1,0:T(8,128)(2,1)S(1)} %get-tuple-element.123), channel_id=1, source_target_pairs={{0,4},{4,0},{1,5},{5,1},{2,6},{6,2},{3,7},{7,3},{8,12},{12,8},{9,1... | collective-permute-start | bytes 786440 | tf_op jit(solution)/shard_map/ppermute | solution.py:399
